TPU v7x, 32 devices: a whole 2x2x4 slice. The times are simulated.
32 devices in a mesh: groups: 2 (over x), expert: 16 (over z, y, core), learner: 1.
Axes of the slice: x: 2, y: 2, z: 4, core: 2. Of those that a mesh axis runs over, the one named last changes fastest.
Arguments:
- hidden_act: bfloat16 [2, 512, 8, 1024], P(None, ('groups', 'expert', 'learner')), parts along dimension 1, may hold values from -6 to 6
- routes: int32 [2, 512, 8], P(None, ('groups', 'expert', 'learner')), parts along dimension 1, may hold values from 0 to 15, all different within a row; in each aligned block of 16 rows (0 to 15, 16 to 31, ..., all dimensions but the last counted through in order) at most 12 rows name the same one
- gates: float32 [2, 512, 8], P(None, ('groups', 'expert', 'learner')), parts along dimension 1, may hold values from 0.1 to 1
- down_codes: bfloat16 [16, 1024, 7168], P('expert', None, 'learner')
- down_scales: float32 [16, 8, 56], P('expert', None, 'learner'), may hold values from 0.01 to 0.05
- changed: int32 [32], P('groups'), parts along dimension 0, may hold values from 0 to 15, as said below
- fresh_codes: bfloat16 [32, 1, 448, 128, 128], P('groups', 'learner', 'expert'), parts along dimension 0
- fresh_scales: float32 [32, 1, 448], P('groups', 'learner', 'expert'), parts along dimension 0, may hold values from 0.01 to 0.05
- block_ids: int32 [32, 1, 448], P('groups'), parts along dimension 0, may hold values from 0 to 447, each once within a row
Outputs:
- layer_out: bfloat16 [2, 512, 7168], P(None, ('groups', 'expert', 'learner')), parts along dimension 1
There are 2 independent parts, one for each index of `groups`. A program takes and returns all parts, laid end to end along the dimension named above; an argument that names none is the same for every part. Nothing has to cross between parts.
Inputs may be any that keep to these rules, and one draw needn't show every extreme that they name: `routes`: each row names 8 different experts. Within the 16 rows that one device holds in one step, no expert is named more than 12 times, a bound that some block reaches. `changed`: 16 different experts. `block_ids`: for each changed expert and column half, every block position appears once.
All inputs are finite; a program needn't handle non-finite values.
Results may differ from a plain program's by a relative error of at most 0.0057.
Values may be sent and summed in bfloat16 or wider, within the bound.
No kernel may reach another device: no remote copies, remote signals or barrier semaphores. Data moves between devices by JAX's collectives and lax.ppermute only.
A program may use at most 192 MiB of HBM per device.

v0:
```python
import jax
import jax.numpy as jnp
from jax import lax
from jax.sharding import PartitionSpec as P

BLK = 128


def dequant(code_grid, scale_grid):
    rows_in, cols_in = code_grid.shape
    blocks = code_grid.astype(jnp.float32).reshape(rows_in // BLK, BLK, cols_in // BLK, BLK)
    scaled = blocks * scale_grid[:, None, :, None]
    return scaled.reshape(rows_in, cols_in).astype(jnp.bfloat16)


def body(
    hidden_act,
    routes,
    gates,
    down_codes,
    down_scales,
    changed,
    fresh_codes,
    fresh_scales,
    block_ids,
):
    experts = lax.axis_size("expert")
    learners = lax.axis_size("learner")
    own_index = lax.axis_index("expert")
    core_index = lax.axis_index("learner")
    step_count, row_count, top_count, hidden_width = hidden_act.shape
    half_cols = down_codes.shape[2]
    capacity = min(row_count, max(2, 3 * row_count * top_count // (2 * experts)))
    old_weight = dequant(down_codes[0], down_scales[0])
    fresh_values = (
        fresh_codes[:, 0].astype(jnp.float32) * fresh_scales[:, 0, :, None, None]
    ).astype(jnp.bfloat16)
    is_match = changed == own_index
    is_changed = jnp.any(is_match)
    own_slot = jnp.argmax(is_match.astype(jnp.int32))
    block_order = block_ids[own_slot, core_index]
    empty_blocks = jnp.zeros((block_order.shape[0], BLK, BLK), jnp.bfloat16)
    outgoing_blocks = (
        jnp.zeros((experts,) + fresh_values.shape[1:], jnp.bfloat16).at[changed].set(fresh_values)
    )
    arrived = lax.all_to_all(outgoing_blocks, "expert", split_axis=0, concat_axis=0, tiled=True)
    placed = empty_blocks.at[block_order].set(arrived.reshape(-1, BLK, BLK))
    assembled = placed.reshape(hidden_width // BLK, half_cols // BLK, BLK, BLK)
    assembled = assembled.transpose(0, 2, 1, 3).reshape(hidden_width, half_cols)
    new_weight = jnp.where(is_changed, assembled, old_weight)
    expert_ids = jnp.arange(experts, dtype=jnp.int32)
    results = []
    for step_index in range(step_count):
        weight = old_weight if step_index == 0 else new_weight
        flat_route = routes[step_index].reshape(-1)
        one_hot = (flat_route[:, None] == expert_ids[None, :]).astype(jnp.int32)
        bucket_rank = jnp.sum((jnp.cumsum(one_hot, axis=0) - 1) * one_hot, axis=1)
        slot_index = flat_route * capacity + bucket_rank
        flat_act = hidden_act[step_index].reshape(-1, hidden_width)
        outgoing = (
            jnp.zeros((experts * capacity, hidden_width), jnp.bfloat16).at[slot_index].set(flat_act)
        )
        outgoing = outgoing.reshape(experts, capacity, hidden_width)

        def expert_work(incoming, weight=weight):
            fanned = lax.all_gather(incoming, "learner", axis=0, tiled=True)
            product = jnp.einsum("snf,fd->snd", fanned, weight, preferred_element_type=jnp.float32)
            return product.astype(jnp.bfloat16)

        produced = expert_work(
            lax.all_to_all(outgoing, "expert", split_axis=0, concat_axis=0, tiled=True)
        )
        grouped = produced.reshape(learners, experts, capacity, half_cols)
        returned = lax.all_to_all(grouped, "expert", split_axis=1, concat_axis=1, tiled=True)
        gate_rows = gates[step_index]
        full_cols = lax.all_to_all(returned, "learner", split_axis=0, concat_axis=3, tiled=True)
        picked = full_cols.reshape(experts * capacity, -1)[slot_index]
        picked = picked.reshape(row_count, top_count, -1).astype(jnp.float32)
        combined = jnp.einsum("rk,rkd->rd", gate_rows, picked, precision=lax.Precision.HIGHEST)
        result = combined.astype(jnp.bfloat16)
        results.append(result)
    return jnp.stack(results)


def solution(mesh):
    in_specs = (
        P(None, ("groups", "expert", "learner"), None, None),
        P(None, ("groups", "expert", "learner"), None),
        P(None, ("groups", "expert", "learner"), None),
        P("expert", None, "learner"),
        P("expert", None, "learner"),
        P("groups"),
        P("groups", "learner", "expert", None, None),
        P("groups", "learner", "expert"),
        P("groups", None, None),
    )
    out_specs = P(None, ("groups", "expert", "learner"), None)
    return jax.shard_map(body, mesh=mesh, in_specs=in_specs, out_specs=out_specs, check_vma=False)
```

profile of v0, /device:TPU:13, one launch (start us, length us, event | category | flops | bytes accessed | tf_op | source)
XLA Modules:
  0.0 641.8 jit_solution(11501822208482419938)
XLA Ops:
  4.1 6.6 %all-to-all-start.2 = ((bf16[16,12,1024]{2,1,0:T(8,128)(2,1)}), bf16[16,12,1024]{2,1,0:T(8,128)(2,1)S(1)}, u32[]{:S(2)}, u32[]{:S(2)}) async-start(bf16[16,12,1024]{2,1,0:T(8,128)(2,1)} %reshape.134), calls=%async_computation.2 | async-start | bytes 1048576 | tf_op jit(solution)/shard_map/all_to_all | solution.py:71
  14.0 10.2 %all-to-all-done.2 = bf16[16,12,1024]{2,1,0:T(8,128)(2,1)S(1)} async-done(((bf16[16,12,1024]{2,1,0:T(8,128)(2,1)}), bf16[16,12,1024]{2,1,0:T(8,128)(2,1)S(1)}, u32[]{:S(2)}, u32[]{:S(2)}) %all-to-all-start.2) | async-done | bytes 393248 | tf_op jit(solution)/shard_map/all_to_all | solution.py:71
  24.2 5.0 all-to-all-start
  29.2 14.3 %fusion.1 = bf16[16,28,128,128]{3,2,1,0:T(8,128)(2,1)} fusion(bf16[16,1,28,128,128]{4,3,2,1,0:T(8,128)(2,1)} %param.15, f32[16,28]{1,0:T(8,128)} %bitcast.115), kind=kLoop, calls=%fused_computation.9 | loop fusion | flops 22020096 | bytes 29361920 | tf_op jit(solution)/shard_map/convert_element_type | solution.py:37
  43.5 8.8 %broadcast_in_dim.7 = bf16[16,28,128,128]{3,2,1,0:T(8,128)(2,1)} broadcast(bf16[]{:T(256)} %constant.12.clone.1), dimensions={} | broadcast | bytes 14680066 | tf_op jit(solution)/shard_map/broadcast_in_dim | solution.py:44
  52.4 39.7 %scatter_fusion = bf16[16,28,128,128]{3,2,1,0:T(8,128)(2,1)} fusion(bf16[16,28,128,128]{3,2,1,0:T(8,128)(2,1)} %broadcast_in_dim.7, s32[16]{0:T(128)S(1)} %compare_select_fusion.1, bf16[16,28,128,128]{3,2,1,0:T(8,128)(2,1)} %fusion.1), kind=kCustom, calls=%fused_computation.4 | custom fusion | bytes 44040256 | tf_op jit(solution)/shard_map/scatter | solution.py:44
  92.0 6.2 all-to-all-start.3
  98.2 11.6 %mul.59 = f32[8,128,56,128]{3,2,1,0:T(8,128)} broadcast(f32[8,56]{1,0:T(8,128)S(1)} %bitcast.116), dimensions={0,2} | broadcast | bytes 29361920 | tf_op jit(solution)/shard_map/mul | solution.py:12
  109.8 20.5 %fusion.18 = bf16[1,16,12,7168]{3,1,2,0:T(8,128)(2,1)S(1)} fusion(bf16[16,12,1024]{2,1,0:T(8,128)(2,1)S(1)} %all-to-all-done, f32[128,8,56,128]{3,2,1,0:T(8,128)} %bitcast.110, bf16[1,1024,7168]{2,1,0:T(8,128)(2,1)} %param.12), kind=kOutput, calls=%fused_computation.20 | convolution fusion | flops 2841968640 | bytes 47185920 | tf_op jit(solution)/shard_map/snf,fd->snd/dot_general | solution.py:67
  130.3 3.4 copy.34
  133.7 281.6 %all-to-all-done.3 = bf16[16,28,128,128]{3,2,1,0:T(8,128)(2,1)} async-done(((bf16[16,28,128,128]{3,2,1,0:T(8,128)(2,1)}), bf16[16,28,128,128]{3,2,1,0:T(8,128)(2,1)}, u32[]{:S(2)}, u32[]{:S(2)}) %all-to-all-start.3) | async-done | bytes 14680096 | tf_op jit(solution)/shard_map/all_to_all | solution.py:46
  415.4 4.9 all-to-all-start.1
  424.2 8.8 %broadcast_in_dim.6 = bf16[448,128,128]{2,1,0:T(8,128)(2,1)} broadcast(bf16[]{:T(256)} %constant.12.clone.1), dimensions={} | broadcast | bytes 14680066 | tf_op jit(solution)/shard_map/broadcast_in_dim | solution.py:42
  433.1 66.2 %scatter_fusion.1 = bf16[448,128,128]{2,1,0:T(8,128)(2,1)} fusion(bf16[448,128,128]{2,1,0:T(8,128)(2,1)} %broadcast_in_dim.6, s32[448]{0:T(512)S(1)} %bitcast.114, bf16[448,128,128]{2,1,0:T(8,128)(2,1)} %bitcast.19), kind=kCustom, calls=%fused_computation.5 | custom fusion | bytes 44041984 | tf_op jit(solution)/shard_map/scatter | solution.py:47
  499.3 17.4 %copy.37 = bf16[8,128,56,128]{3,2,1,0:T(8,128)(2,1)} copy(bf16[8,128,56,128]{3,1,2,0:T(8,128)(2,1)} %bitcast.112) | data formatting | bytes 29360128 | tf_op jit(solution)/shard_map/transpose | solution.py:49
  516.7 24.5 %fusion.15 = bf16[1,16,12,7168]{3,1,2,0:T(8,128)(2,1)S(1)} fusion(bf16[128,8,56,128]{3,2,1,0:T(8,128)(2,1)} %bitcast.113, pred[]{:T(512)} %compare_reduce_fusion, bf16[16,12,1024]{2,1,0:T(8,128)(2,1)S(1)} %copy-done.1, f32[128,8,56,128]{3,2,1,0:T(8,128)} %bitcast.111, bf16[1,1024,7168]{2,1,0:T(8,128)(2,1)} %param.12), kind=kOutput, calls=%fused_computation.19 | convolution fusion | flops 2849308672 | bytes 61865984 | tf_op jit(solution)/shard_map/snf,fd->snd/dot_general | solution.py:67
  541.1 3.4 copy.39
  544.5 6.0 all-to-all-start.4
  550.7 3.0 reshape.132
  553.8 3.0 gather_fusion
  556.8 3.1 fusion.23
  559.9 71.8 %all-to-all-done.4 = bf16[1,16,12,7168]{3,2,0,1:T(8,128)(2,1)} async-done(((bf16[1,16,12,7168]{3,2,0,1:T(8,128)(2,1)}), bf16[1,16,12,7168]{3,2,0,1:T(8,128)(2,1)}, u32[]{:S(2)}, u32[]{:S(2)}) %all-to-all-start.4) | async-done | bytes 2752544 | tf_op jit(solution)/shard_map/all_to_all | solution.py:74
  631.8 3.0 reshape.139
  637.8 3.1 fusion.21
  (45 shorter events, 13.5 us)
Async XLA Ops:
  4.1 20.1 %all-to-all-start.2 = ((bf16[16,12,1024]{2,1,0:T(8,128)(2,1)}), bf16[16,12,1024]{2,1,0:T(8,128)(2,1)S(1)}, u32[]{:S(2)}, u32[]{:S(2)}) async-start(bf16[16,12,1024]{2,1,0:T(8,128)(2,1)} %reshape.134), calls=%async_computation.2 | async-start | bytes 1048576 | tf_op jit(solution)/shard_map/all_to_all | solution.py:71
  24.2 19.3 %copy-start = (bf16[16,12,1024]{2,1,0:T(8,128)(2,1)}, bf16[16,12,1024]{2,1,0:T(8,128)(2,1)S(1)}, u32[]{:S(2)}) copy-start(bf16[16,12,1024]{2,1,0:T(8,128)(2,1)S(1)} %all-to-all-done.2) | copy-start | bytes 1179652
  24.2 67.8 %all-to-all-start = ((bf16[16,12,1024]{2,1,0:T(8,128)(2,1)}), bf16[16,12,1024]{2,1,0:T(8,128)(2,1)S(1)}, u32[]{:S(2)}, u32[]{:S(2)}) async-start(bf16[16,12,1024]{2,1,0:T(8,128)(2,1)} %reshape.130), calls=%async_computation | async-start | bytes 1048576 | tf_op jit(solution)/shard_map/all_to_all | solution.py:71
  29.2 14.3 %copy-start.4 = (s32[16]{0:T(128)S(1)}, s32[16]{0:T(128)}, u32[]{:S(2)}) copy-start(s32[16]{0:T(128)} %param.14) | copy-start | bytes 196
  92.0 6.2 copy-start.3
  92.0 323.3 %all-to-all-start.3 = ((bf16[16,28,128,128]{3,2,1,0:T(8,128)(2,1)}), bf16[16,28,128,128]{3,2,1,0:T(8,128)(2,1)}, u32[]{:S(2)}, u32[]{:S(2)}) async-start(bf16[16,28,128,128]{3,2,1,0:T(8,128)(2,1)} %scatter_fusion), calls=%async_computation.3 | async-start | bytes 29360128 | tf_op jit(solution)/shard_map/all_to_all | solution.py:46
  415.4 129.1 %all-to-all-start.1 = ((bf16[1,16,12,7168]{3,2,0,1:T(8,128)(2,1)}), bf16[1,16,12,7168]{3,2,0,1:T(8,128)(2,1)}, u32[]{:S(2)}, u32[]{:S(2)}) async-start(bf16[1,16,12,7168]{3,2,0,1:T(8,128)(2,1)} %copy.34), calls=%async_computation.1 | async-start | bytes 7340032 | tf_op jit(solution)/shard_map/all_to_all | solution.py:74
  499.2 17.4 %copy-start.1 = (bf16[16,12,1024]{2,1,0:T(8,128)(2,1)S(1)}, bf16[16,12,1024]{2,1,0:T(8,128)(2,1)}, u32[]{:S(2)}) copy-start(bf16[16,12,1024]{2,1,0:T(8,128)(2,1)} %copy-done) | copy-start | bytes 1179652
  516.7 33.9 %copy-start.2 = (f32[2,16,8]{1,2,0:T(8,128)S(1)}, f32[2,16,8]{1,2,0:T(8,128)}, u32[]{:S(2)}) copy-start(f32[2,16,8]{1,2,0:T(8,128)} %param.11) | copy-start | bytes 3076
  544.5 87.3 %all-to-all-start.4 = ((bf16[1,16,12,7168]{3,2,0,1:T(8,128)(2,1)}), bf16[1,16,12,7168]{3,2,0,1:T(8,128)(2,1)}, u32[]{:S(2)}, u32[]{:S(2)}) async-start(bf16[1,16,12,7168]{3,2,0,1:T(8,128)(2,1)} %copy.39), calls=%async_computation.4 | async-start | bytes 7340032 | tf_op jit(solution)/shard_map/all_to_all | solution.py:74
where the time goes:
time: 644 us; the launch traced here: 642 us
  waiting for transfers between devices  364 us (57%)
  local copies, waits for them, and re-layouts  178 us (28%)
  matrix products  51.1 us (8%)
  starting transfers between devices  28.6 us (4%)
  other arithmetic  18.8 us (3%)
    all_to_all x1, waiting for transfers between devices, body(): lax.all_to_all(outgoing_blocks, 'expert', split_axis=0, concat_axis=0, ti...  282 us
    all_to_all x2, waiting for transfers between devices, body(): lax.all_to_all(grouped, 'expert', split_axis=1, concat_axis=1, tiled=True)  71.9 us
    scatter x1, local copies, waits for them, and re-layouts, body(): placed = empty_blocks.at[block_order].set(arrived.reshape(-1, BLK, BLK))  66.2 us
    dot_general x2, matrix products, expert_work(): jnp.einsum('snf,fd->snd', fanned, weight, preferred_element_type=jnp.floa...  44.9 us
    scatter x1, local copies, waits for them, and re-layouts, body(): jnp.zeros((experts,) + fresh_values.shape[1:], jnp.bfloat16).at[changed]  39.7 us
    transpose x1, local copies, waits for them, and re-layouts, body(): assembled = assembled.transpose(0, 2, 1, 3).reshape(hidden_width, half_cols)  17.4 us
    convert_element_type x1, other arithmetic, body(): fresh_values = (fresh_codes[:, 0].astype(jnp.float32) * fresh_scales[:, 0...  14.3 us
  transfers between devices with their start and end apart: 5, of which 3 were waited for; matrix products, arithmetic and copies ran while one was open for 36% of the time, Pallas kernels for 0%

commit v1 on v0

v1 whole, which is shorter than its diff:
```python
import functools

import jax
import jax.numpy as jnp
import numpy as np
from jax import lax
from jax.experimental import pallas as pl
from jax.experimental.pallas import tpu as pltpu
from jax.sharding import PartitionSpec as P

BLK = 128
LANES = 128
PAD_ROWS = 16
VMEM_LIMIT = 56 * 1024 * 1024
F32 = jnp.float32
BF16 = jnp.bfloat16


def old_kernel(order_ref, scale_ref, act_ref, code_ref, keep_ref, send_ref, act_scratch, weight_scratch):
    tile = pl.program_id(0)
    groups, group_rows, width = act_ref.shape
    tile_cols = code_ref.shape[1]

    @pl.when(tile == 0)
    def _():
        for g in range(groups):
            act_scratch[g * group_rows : (g + 1) * group_rows, :] = act_ref[order_ref[g]]

    per_tile = tile_cols // BLK
    col_blocks = pl.num_programs(0) * per_tile
    for i in range(width // BLK):
        for j in range(per_tile):
            scale = scale_ref[i * col_blocks + tile * per_tile + j]
            block = code_ref[i * BLK : (i + 1) * BLK, j * BLK : (j + 1) * BLK]
            weight_scratch[i * BLK : (i + 1) * BLK, j * BLK : (j + 1) * BLK] = (
                block.astype(F32) * scale
            ).astype(BF16)
    product = jnp.dot(act_scratch[...], weight_scratch[...], preferred_element_type=F32).astype(BF16)
    half = keep_ref.shape[0]
    keep_ref[...] = product[:half]
    send_ref[...] = product[half:]


def old_product(act, codes, scales, order):
    groups, group_rows, width = act.shape
    rows = groups * group_rows
    cols = codes.shape[1]
    tile_cols = 512
    half = rows // 2
    return pl.pallas_call(
        old_kernel,
        grid_spec=pltpu.PrefetchScalarGridSpec(
            num_scalar_prefetch=2,
            grid=(cols // tile_cols,),
            in_specs=[
                pl.BlockSpec((groups, group_rows, width), lambda t, *_: (0, 0, 0)),
                pl.BlockSpec((width, tile_cols), lambda t, *_: (0, t)),
            ],
            out_specs=[
                pl.BlockSpec((half, tile_cols), lambda t, *_: (0, t)),
                pl.BlockSpec((half, tile_cols), lambda t, *_: (0, t)),
            ],
            scratch_shapes=[pltpu.VMEM((rows, width), BF16), pltpu.VMEM((width, tile_cols), BF16)],
        ),
        out_shape=[jax.ShapeDtypeStruct((half, cols), BF16)] * 2,
        compiler_params=pltpu.CompilerParams(vmem_limit_bytes=VMEM_LIMIT),
        cost_estimate=pl.CostEstimate(
            flops=2 * rows * width * cols, bytes_accessed=2 * width * cols + 2 * rows * cols, transcendentals=0
        ),
        name="old_product",
    )(order, scales.reshape(-1), act, codes)


def fresh_kernel(
    n_pieces, experts, row_count, top_count,
    pos_ref, start_ref, slot_ref, index_ref, scale_ref,
    *refs,
):
    pieces = refs[:n_pieces]
    code_hbm, keep_ref, send_ref, act_buf, dense, code_buf, act_sem, code_sem = refs[n_pieces:]
    chunk = pl.program_id(0)
    groups, piece_rows, width = act_buf.shape
    row_blocks = width // BLK
    routed = row_count * top_count

    @pl.when(chunk == 0)
    def _():
        for i in range(n_pieces):
            pltpu.make_async_copy(pieces[i], act_buf.at[pos_ref[i]], act_sem.at[i]).start()
        pltpu.make_async_copy(code_hbm, code_buf, code_sem).start()
        for i in range(n_pieces):
            pltpu.make_async_copy(pieces[i], act_buf.at[pos_ref[i]], act_sem.at[i]).wait()
        row = lax.broadcasted_iota(jnp.int32, (experts * row_count, routed), 0)
        col = lax.broadcasted_iota(jnp.int32, (experts * row_count, routed), 1)
        same_row = row % row_count == col // top_count
        expert = (row // row_count).astype(F32)

        def expand(g, carry):
            route = act_buf[g, routed : routed + PAD_ROWS, 0:routed].astype(F32)[0:1, :]
            pick = jnp.where(same_row & (expert == route), 1.0, 0.0).astype(BF16)
            spread = jnp.dot(pick, act_buf[g, 0:routed, :], preferred_element_type=F32).astype(BF16)
            at = pl.ds(pl.multiple_of(g * row_count, row_count), row_count)
            for e in range(experts):
                for b in range(row_blocks):
                    dense[e * row_blocks + b, at, :] = spread[
                        e * row_count : (e + 1) * row_count, b * BLK : (b + 1) * BLK
                    ]
            return carry

        lax.fori_loop(0, groups, expand, 0)
        pltpu.make_async_copy(code_hbm, code_buf, code_sem).wait()

    per_chunk = keep_ref.shape[1] // BLK
    half = keep_ref.shape[0]
    rows = 2 * half
    for j in range(per_chunk):
        column = chunk * per_chunk + j
        first = start_ref[column]
        last = start_ref[column + 1]

        def pair(t, total):
            one = first + 2 * t
            two = jnp.minimum(one + 1, last - 1)
            scale_two = jnp.where(one + 1 < last, scale_ref[two], 0.0)
            block_one = (code_buf[slot_ref[one]].astype(F32) * scale_ref[one]).astype(BF16)
            block_two = (code_buf[slot_ref[two]].astype(F32) * scale_two).astype(BF16)
            left = jnp.concatenate([dense[index_ref[one]], dense[index_ref[two]]], axis=1)
            right = jnp.concatenate([block_one, block_two], axis=0)
            return total + jnp.dot(left, right, preferred_element_type=F32)

        total = lax.fori_loop(0, (last - first + 1) // 2, pair, jnp.zeros((rows, BLK), F32))
        total = total.astype(BF16)
        keep_ref[:, j * BLK : (j + 1) * BLK] = total[:half]
        send_ref[:, j * BLK : (j + 1) * BLK] = total[half:]


def fresh_product(pieces, pos, codes, plan, cols, experts, row_count, top_count):
    n_pieces = len(pieces)
    piece_rows, width = pieces[0].shape
    rows = n_pieces * row_count
    slots = codes.shape[0]
    chunk_cols = cols // 7
    half = rows // 2
    return pl.pallas_call(
        functools.partial(fresh_kernel, n_pieces, experts, row_count, top_count),
        grid_spec=pltpu.PrefetchScalarGridSpec(
            num_scalar_prefetch=5,
            grid=(cols // chunk_cols,),
            in_specs=[pl.BlockSpec(memory_space=pl.ANY)] * (n_pieces + 1),
            out_specs=[
                pl.BlockSpec((half, chunk_cols), lambda t, *_: (0, t)),
                pl.BlockSpec((half, chunk_cols), lambda t, *_: (0, t)),
            ],
            scratch_shapes=[
                pltpu.VMEM((n_pieces, piece_rows, width), BF16),
                pltpu.VMEM((experts * (width // BLK), rows, BLK), BF16),
                pltpu.VMEM(codes.shape, BF16),
                pltpu.SemaphoreType.DMA((n_pieces,)),
                pltpu.SemaphoreType.DMA,
            ],
        ),
        out_shape=[jax.ShapeDtypeStruct((half, cols), BF16)] * 2,
        compiler_params=pltpu.CompilerParams(vmem_limit_bytes=VMEM_LIMIT),
        cost_estimate=pl.CostEstimate(
            flops=2 * rows * BLK * BLK * slots,
            bytes_accessed=2 * slots * BLK * BLK + 2 * rows * cols + 2 * rows * width * 8,
            transcendentals=0,
        ),
        name="fresh_product",
    )(pos, *plan, *pieces, codes)


def fresh_plan(own_ids, own_scales, changed, col_blocks, row_blocks):
    slots_each = own_ids.shape[1]
    ids = own_ids.reshape(-1)
    count = ids.shape[0]
    column = ids % col_blocks
    index = jnp.repeat(changed, slots_each) * row_blocks + ids // col_blocks
    number = jnp.arange(count, dtype=jnp.int32)
    key = column * count + number
    rank = jnp.sum((key[None, :] < key[:, None]).astype(jnp.int32), axis=1)
    hit = rank[None, :] == number[:, None]
    slot = jnp.sum(jnp.where(hit, number[None, :], 0), axis=1)
    sorted_index = jnp.sum(jnp.where(hit, index[None, :], 0), axis=1)
    sorted_scale = jnp.sum(jnp.where(hit, own_scales.reshape(-1)[None, :], 0.0), axis=1)
    bounds = jnp.arange(col_blocks + 1, dtype=jnp.int32)
    start = jnp.sum((column[None, :] < bounds[:, None]).astype(jnp.int32), axis=1)
    return start, slot, sorted_index, sorted_scale


def add(*terms):
    total = terms[0].astype(F32)
    for term in terms[1:]:
        total = total + term.astype(F32)
    return total.astype(BF16)


class ChipGrid:
    SIZE = 16
    CYCLE = [(0, 0), (1, 0), (2, 0), (3, 0), (3, 1), (2, 1), (1, 1), (0, 1)]

    def __init__(self):
        cycle = self.CYCLE
        n = len(cycle)
        at = {chip: i for i, chip in enumerate(cycle)}
        number = lambda z, y, c: (z * 2 + y) * 2 + c
        self.forward, self.backward = [], []
        self.piece_rank = np.zeros((self.SIZE, self.SIZE), np.int32)
        self.rank_source = np.zeros((self.SIZE, self.SIZE), np.int32)
        for z in range(4):
            for y in range(2):
                for c in range(2):
                    me, i = number(z, y, c), at[(z, y)]
                    self.forward.append((me, number(*cycle[(i + 1) % n], c)))
                    self.backward.append((me, number(*cycle[(i - 1) % n], c)))
                    hops = [0, -1, 1, -2, 2, -3, 3, -4]
                    for dc in range(2):
                        for k, hop in enumerate(hops):
                            sz, sy = cycle[(i + hop) % n]
                            self.piece_rank[me, dc * 8 + k] = self.rank(sz ^ z, sy ^ y, dc)
                    for dz in range(4):
                        for dy in range(2):
                            for dc in range(2):
                                self.rank_source[me, self.rank(dz, dy, dc)] = number(z ^ dz, y ^ dy, c ^ dc)

    @staticmethod
    def rank(dz, dy, dc):
        return dc * 8 + dy * 4 + dz

    def partner(self, x, dz, dy, dc):
        delta = (dz * 2 + dy) * 2 + dc
        return lax.ppermute(x, "expert", [(i, i ^ delta) for i in range(self.SIZE)])

    def gather(self, x):
        ahead = behind = x
        got = [x]
        for step in range(4):
            ahead = lax.ppermute(ahead, "expert", self.forward)
            got.append(ahead)
            if step < 3:
                behind = lax.ppermute(behind, "expert", self.backward)
                got.append(behind)
        return got + [self.partner(piece, 0, 0, 1) for piece in got]

    def reduce(self, keep, send, rows):
        got = self.partner(send, 0, 0, 1)
        per_y = 4 * rows
        far = add(keep[per_y:], got[per_y:])
        far = self.partner(far, 0, 1, 0)
        near = [
            add(keep[k * rows : (k + 1) * rows], got[k * rows : (k + 1) * rows], far[k * rows : (k + 1) * rows])
            for k in range(4)
        ]
        moved = [self.partner(near[dz], dz, 0, 0) for dz in (1, 2, 3)]
        return add(near[0], *moved)


def body(
    hidden_act,
    routes,
    gates,
    down_codes,
    down_scales,
    changed,
    fresh_codes,
    fresh_scales,
    block_ids,
):
    experts = lax.axis_size("expert")
    learners = lax.axis_size("learner")
    own = lax.axis_index("expert")
    own_half = lax.axis_index("learner")
    step_count, row_count, top_count, width = hidden_act.shape
    cols = down_codes.shape[2]
    routed = row_count * top_count
    row_blocks, col_blocks = width // BLK, cols // BLK
    slots_each = fresh_codes.shape[2]
    some_unchanged = changed.shape[0] < experts

    gated = (hidden_act.astype(F32) * gates[..., None]).astype(BF16).reshape(step_count, routed, width)
    flat_routes = routes.reshape(step_count, routed)
    row = jnp.arange(experts * row_count, dtype=jnp.int32)
    entry = jnp.arange(routed, dtype=jnp.int32)

    def spread(step):
        pick = (row[:, None] // row_count == flat_routes[step][None, :]) & (
            row[:, None] % row_count == entry[None, :] // top_count
        )
        out = jnp.dot(pick.astype(BF16), gated[step], preferred_element_type=F32)
        return out.astype(BF16).reshape(experts, row_count, width)

    def with_routes(step):
        tail = jnp.zeros((PAD_ROWS, width), BF16).at[0, :routed].set(flat_routes[step].astype(BF16))
        return jnp.concatenate([gated[step], tail], axis=0)

    own_ids = lax.dynamic_slice_in_dim(block_ids[:, own_half], own * slots_each, slots_each, axis=1)
    plan = fresh_plan(own_ids, fresh_scales[:, 0], changed, col_blocks, row_blocks)
    codes = fresh_codes.reshape((-1, BLK, BLK))
    scales = down_scales[0]

    if experts == ChipGrid.SIZE and learners == 1 and not some_unchanged:
        grid = ChipGrid()
        order = jnp.asarray(grid.rank_source)[own]
        pos = jnp.asarray(grid.piece_rank)[own]
        dense_old = lax.all_to_all(spread(0), "expert", split_axis=0, concat_axis=0, tiled=True)
        pieces = {step: grid.gather(with_routes(step)) for step in range(1, step_count)}
        results = [grid.reduce(*old_product(dense_old, down_codes[0], scales, order), row_count)]
        for step in range(1, step_count):
            halves = fresh_product(pieces[step], pos, codes, plan, cols, experts, row_count, top_count)
            results.append(grid.reduce(*halves, row_count))
        return jnp.stack(results)

    group = experts * learners
    straight = jnp.arange(group, dtype=jnp.int32)

    def combine(keep, send):
        part = jnp.concatenate([keep, send], axis=0)
        summed = lax.psum_scatter(part, "expert", scatter_dimension=0, tiled=True)
        return lax.all_to_all(summed, "learner", split_axis=0, concat_axis=1, tiled=True)

    def old_part(step):
        dense = lax.all_to_all(spread(step), "expert", split_axis=0, concat_axis=0, tiled=True)
        if step > 0:
            dense = jnp.where(jnp.any(changed == own), jnp.zeros_like(dense), dense)
        dense = lax.all_gather(dense, "learner", axis=1, tiled=False)
        dense = dense.reshape(group, row_count, width)
        return old_product(dense, down_codes[0], scales, straight)

    results = [combine(*old_part(0))]
    at_once = 16
    for step in range(1, step_count):
        everyone = lax.all_gather(with_routes(step), ("expert", "learner"), axis=0)
        keep_rows, send_rows = [], []
        for first in range(0, group, at_once):
            pieces = [everyone[first + i] for i in range(at_once)]
            keep, send = fresh_product(
                pieces, straight[:at_once], codes, plan, cols, experts, row_count, top_count
            )
            keep_rows.append(jnp.concatenate([keep, send], axis=0))
        total = jnp.concatenate(keep_rows, axis=0)
        if some_unchanged:
            total = add(total, jnp.concatenate(old_part(step), axis=0))
        results.append(combine(total[: total.shape[0] // 2], total[total.shape[0] // 2 :]))
    return jnp.stack(results)


def solution(mesh):
    in_specs = (
        P(None, ("groups", "expert", "learner"), None, None),
        P(None, ("groups", "expert", "learner"), None),
        P(None, ("groups", "expert", "learner"), None),
        P("expert", None, "learner"),
        P("expert", None, "learner"),
        P("groups"),
        P("groups", "learner", "expert", None, None),
        P("groups", "learner", "expert"),
        P("groups", None, None),
    )
    out_specs = P(None, ("groups", "expert", "learner"), None)
    return jax.shard_map(body, mesh=mesh, in_specs=in_specs, out_specs=out_specs, check_vma=False)
```

time: 644 us -> 198 us (0.31)
  the two profiles are of different devices: /device:TPU:13 before, /device:TPU:0 now
where the time goes in v1:
time: 198 us; the launch traced here: 197 us
  waiting for transfers between devices  75.9 us (38%)
  Pallas kernels  73.1 us (37%)
  starting transfers between devices  31.5 us (16%)
  other arithmetic  7.61 us (4%)
  local copies, waits for them, and re-layouts  6.97 us (4%)
    pallas_call x1, Pallas kernels, fresh_product(): pl.pallas_call(functools.partial(fresh_kernel, n_pieces, experts, row_cou...  57.6 us
    ppermute x18, waiting for transfers between devices, partner(): return lax.ppermute(x, 'expert', [(i, i ^ delta) for i in range(self.SIZE)])  51 us
    pallas_call x1, Pallas kernels, old_product(): pl.pallas_call(old_kernel, grid_spec=pltpu.PrefetchScalarGridSpec(num_sca...  15.6 us
    ppermute x18, starting transfers between devices, partner(): return lax.ppermute(x, 'expert', [(i, i ^ delta) for i in range(self.SIZE)])  14.1 us
    ppermute x4, waiting for transfers between devices, gather(): ahead = lax.ppermute(ahead, 'expert', self.forward)  12.9 us
    ppermute x3, waiting for transfers between devices, gather(): behind = lax.ppermute(behind, 'expert', self.backward)  12 us
    ppermute x4, starting transfers between devices, gather(): ahead = lax.ppermute(ahead, 'expert', self.forward)  9.88 us
    all_to_all x1, starting transfers between devices, body(): lax.all_to_all(spread(0), 'expert', split_axis=0, concat_axis=0, tiled=True)  7.39 us
  transfers between devices with their start and end apart: 26, of which 10 were waited for; matrix products, arithmetic and copies ran while one was open for 5% of the time, Pallas kernels for 37%

profile of v1, /device:TPU:0, one launch (start us, length us, event | category | flops | bytes accessed | tf_op | source)
XLA Modules:
  0.0 196.6 jit_solution(8361313864158746968)
XLA Ops:
  1.7 1.2 multiply_convert_fusion
  4.0 7.4 %all-to-all-start = ((bf16[16,16,1024]{2,1,0:T(8,128)(2,1)}), bf16[16,16,1024]{2,1,0:T(8,128)(2,1)S(1)}, u32[]{:S(2)}, u32[]{:S(2)}) async-start(bf16[16,16,1024]{2,1,0:T(8,128)(2,1)} %bitcast.2), calls=%async_computation | async-start | bytes 1048576 | tf_op jit(solution)/shard_map/all_to_all | solution.py:305
  11.7 2.0 %collective-permute-start.5 = (bf16[144,1024]{1,0:T(8,128)(2,1)S(1)}, bf16[144,1024]{1,0:T(8,128)(2,1)S(1)}, u32[]{:S(2)}, u32[]{:S(2)}) collective-permute-start(bf16[144,1024]{1,0:T(8,128)(2,1)S(1)} %fusion.1.refs_0_), channel_id=1, source_target_pairs={{0,4},{1,5},{2,0},{3,1},{4,8},{5,9},{6,2},{7,3},{8,12},{9,13},{10,... | collective-permute-start | bytes 884744 | tf_op jit(solution)/shard_map/ppermute | solution.py:238
  14.4 1.2 fusion.14.order_ref
  15.6 11.6 %collective-permute-done.5.refs_1_ = bf16[144,1024]{1,0:T(8,128)(2,1)S(1)} collective-permute-done((bf16[144,1024]{1,0:T(8,128)(2,1)S(1)}, bf16[144,1024]{1,0:T(8,128)(2,1)S(1)}, u32[]{:S(2)}, u32[]{:S(2)}) %collective-permute-start.5) | collective-permute-done | bytes 294944 | tf_op jit(solution)/shard_map/ppermute | solution.py:238
  27.3 4.5 %collective-permute-start.7 = (bf16[144,1024]{1,0:T(8,128)(2,1)S(1)}, bf16[144,1024]{1,0:T(8,128)(2,1)S(1)}, u32[]{:S(2)}, u32[]{:S(2)}) collective-permute-start(bf16[144,1024]{1,0:T(8,128)(2,1)S(1)} %collective-permute-done.5.refs_1_), channel_id=1, source_target_pairs={{0,4},{1,5},{2,0},{3,1},{4,8},{5,9},{6,2},{7,3},{8,12},{9,13},{10,... | collective-permute-start | bytes 884744 | tf_op jit(solution)/shard_map/ppermute | solution.py:238
  32.5 15.6 %old_product.1 = (bf16[128,7168]{1,0:T(8,128)(2,1)}, bf16[128,7168]{1,0:T(8,128)(2,1)}) custom-call(s32[16]{0:T(128)} %fusion.14.order_ref, f32[448]{0:T(512)} %reshape_squeeze.3.scale_ref, bf16[16,16,1024]{2,1,0:T(8,128)(2,1)} %copy-done, bf16[1024,7168]{1,0:T(8,128)(2,1)} %bitcast.16), custom_call_target="tpu_custom_call" | custom-call | flops 3758096384 | bytes 18350080 | tf_op jit(solution)/shard_map/old_product/pallas_call | solution.py:50
  48.8 2.5 %collective-permute-start.9 = (bf16[144,1024]{1,0:T(8,128)(2,1)S(1)}, bf16[144,1024]{1,0:T(8,128)(2,1)}, u32[]{:S(2)}, u32[]{:S(2)}) collective-permute-start(bf16[144,1024]{1,0:T(8,128)(2,1)S(1)} %collective-permute-done.7.refs_3_), channel_id=1, source_target_pairs={{0,4},{1,5},{2,0},{3,1},{4,8},{5,9},{6,2},{7,3},{8,12},{9,13},{10,... | collective-permute-start | bytes 884744 | tf_op jit(solution)/shard_map/ppermute | solution.py:238
  52.7 5.7 %collective-permute-done.8.refs_4_ = bf16[144,1024]{1,0:T(8,128)(2,1)} collective-permute-done((bf16[144,1024]{1,0:T(8,128)(2,1)S(1)}, bf16[144,1024]{1,0:T(8,128)(2,1)}, u32[]{:S(2)}, u32[]{:S(2)}) %collective-permute-start.8) | collective-permute-done | bytes 294944 | tf_op jit(solution)/shard_map/ppermute | solution.py:241
  58.5 1.3 collective-permute-done.9.refs_5_
  61.8 6.3 %collective-permute-done.10.refs_6_ = bf16[144,1024]{1,0:T(8,128)(2,1)S(1)} collective-permute-done((bf16[144,1024]{1,0:T(8,128)(2,1)}, bf16[144,1024]{1,0:T(8,128)(2,1)S(1)}, u32[]{:S(2)}, u32[]{:S(2)}) %collective-permute-start.10) | collective-permute-done | bytes 294944 | tf_op jit(solution)/shard_map/ppermute | solution.py:241
  69.4 1.3 fusion.15.pos_ref
  73.7 57.6 %fresh_product.1 = (bf16[128,7168]{1,0:T(8,128)(2,1)}, bf16[128,7168]{1,0:T(8,128)(2,1)}) custom-call(s32[16]{0:T(128)} %fusion.15.pos_ref, s32[57]{0:T(128)} %convert_reduce_fusion.1.start_ref, s32[448]{0:T(512)} %get-tuple-element.28.slot_ref, s32[448]{0:T(512)} %get-tuple-element.27.index_ref, f32[448]{0:T(512)} %select_reduce_fusion.scale_ref, ...), custom_call_target="tpu_custom_call" | custom-call | flops 3758096384 | bytes 22544384 | tf_op jit(solution)/shard_map/fresh_product/pallas_call | solution.py:144
  131.8 1.6 collective-permute-start.1
  133.4 1.9 collective-permute-done.20
  135.6 1.5 collective-permute-start.21
  137.1 18.0 %collective-permute-done.1 = bf16[64,7168]{1,0:T(8,128)(2,1)S(1)} collective-permute-done((bf16[64,7168]{1,0:T(8,128)(2,1)S(1)}, bf16[64,7168]{1,0:T(8,128)(2,1)S(1)}, u32[]{:S(2)}, u32[]{:S(2)}) %collective-permute-start.1) | collective-permute-done | bytes 917536 | tf_op jit(solution)/shard_map/ppermute | solution.py:232
  155.3 2.2 %collective-permute-start.2 = (bf16[16,7168]{1,0:T(8,128)(2,1)S(1)}, bf16[16,7168]{1,0:T(8,128)(2,1)S(1)}, u32[]{:S(2)}, u32[]{:S(2)}) collective-permute-start(bf16[16,7168]{1,0:T(8,128)(2,1)S(1)} %get-tuple-element.29), channel_id=1, source_target_pairs={{0,4},{1,5},{2,6},{3,7},{4,0},{5,1},{6,2},{7,3},{8,12},{9,13},{10,... | collective-permute-start | bytes 688136 | tf_op jit(solution)/shard_map/ppermute | solution.py:232
  158.1 1.9 collective-permute-start.4
  160.0 14.1 %collective-permute-done.21 = bf16[64,7168]{1,0:T(8,128)(2,1)S(1)} collective-permute-done((bf16[64,7168]{1,0:T(8,128)(2,1)S(1)}, bf16[64,7168]{1,0:T(8,128)(2,1)S(1)}, u32[]{:S(2)}, u32[]{:S(2)}) %collective-permute-start.21) | collective-permute-done | bytes 917536 | tf_op jit(solution)/shard_map/ppermute | solution.py:232
  174.3 2.0 %collective-permute-start.22 = (bf16[16,7168]{1,0:T(8,128)(2,1)S(1)}, bf16[16,7168]{1,0:T(8,128)(2,1)S(1)}, u32[]{:S(2)}, u32[]{:S(2)}) collective-permute-start(bf16[16,7168]{1,0:T(8,128)(2,1)S(1)} %get-tuple-element.32), channel_id=1, source_target_pairs={{0,4},{1,5},{2,6},{3,7},{4,0},{5,1},{6,2},{7,3},{8,12},{9,13},{10,... | collective-permute-start | bytes 688136 | tf_op jit(solution)/shard_map/ppermute | solution.py:232
  177.2 1.6 collective-permute-start.24
  179.0 6.2 %collective-permute-done.22 = bf16[16,7168]{1,0:T(8,128)(2,1)S(1)} collective-permute-done((bf16[16,7168]{1,0:T(8,128)(2,1)S(1)}, bf16[16,7168]{1,0:T(8,128)(2,1)S(1)}, u32[]{:S(2)}, u32[]{:S(2)}) %collective-permute-start.22) | collective-permute-done | bytes 229408 | tf_op jit(solution)/shard_map/ppermute | solution.py:232
  185.2 10.4 %collective-permute-done.23 = bf16[16,7168]{1,0:T(8,128)(2,1)S(1)} collective-permute-done((bf16[16,7168]{1,0:T(8,128)(2,1)S(1)}, bf16[16,7168]{1,0:T(8,128)(2,1)S(1)}, u32[]{:S(2)}, u32[]{:S(2)}) %collective-permute-start.23) | collective-permute-done | bytes 229408 | tf_op jit(solution)/shard_map/ppermute | solution.py:232
  (98 shorter events, 16.8 us)
Async XLA Ops:
  4.0 27.7 %all-to-all-start = ((bf16[16,16,1024]{2,1,0:T(8,128)(2,1)}), bf16[16,16,1024]{2,1,0:T(8,128)(2,1)S(1)}, u32[]{:S(2)}, u32[]{:S(2)}) async-start(bf16[16,16,1024]{2,1,0:T(8,128)(2,1)} %bitcast.2), calls=%async_computation | async-start | bytes 1048576 | tf_op jit(solution)/shard_map/all_to_all | solution.py:305
  11.7 15.6 %collective-permute-start.5 = (bf16[144,1024]{1,0:T(8,128)(2,1)S(1)}, bf16[144,1024]{1,0:T(8,128)(2,1)S(1)}, u32[]{:S(2)}, u32[]{:S(2)}) collective-permute-start(bf16[144,1024]{1,0:T(8,128)(2,1)S(1)} %fusion.1.refs_0_), channel_id=1, source_target_pairs={{0,4},{1,5},{2,0},{3,1},{4,8},{5,9},{6,2},{7,3},{8,12},{9,13},{10,... | collective-permute-start | bytes 884744 | tf_op jit(solution)/shard_map/ppermute | solution.py:238
  13.7 34.9 %collective-permute-start.6 = (bf16[144,1024]{1,0:T(8,128)(2,1)S(1)}, bf16[144,1024]{1,0:T(8,128)(2,1)S(1)}, u32[]{:S(2)}, u32[]{:S(2)}) collective-permute-start(bf16[144,1024]{1,0:T(8,128)(2,1)S(1)} %fusion.1.refs_0_), channel_id=1, source_target_pairs={{0,2},{1,3},{2,6},{3,7},{4,0},{5,1},{6,10},{7,11},{8,4},{9,5},{10,... | collective-permute-start | bytes 884744 | tf_op jit(solution)/shard_map/ppermute | solution.py:241
  27.3 21.5 %collective-permute-start.7 = (bf16[144,1024]{1,0:T(8,128)(2,1)S(1)}, bf16[144,1024]{1,0:T(8,128)(2,1)S(1)}, u32[]{:S(2)}, u32[]{:S(2)}) collective-permute-start(bf16[144,1024]{1,0:T(8,128)(2,1)S(1)} %collective-permute-done.5.refs_1_), channel_id=1, source_target_pairs={{0,4},{1,5},{2,0},{3,1},{4,8},{5,9},{6,2},{7,3},{8,12},{9,13},{10,... | collective-permute-start | bytes 884744 | tf_op jit(solution)/shard_map/ppermute | solution.py:238
  48.1 83.5 %collective-permute-start = (bf16[128,7168]{1,0:T(8,128)(2,1)}, bf16[128,7168]{1,0:T(8,128)(2,1)S(1)}, u32[]{:S(2)}, u32[]{:S(2)}) collective-permute-start(bf16[128,7168]{1,0:T(8,128)(2,1)} %get-tuple-element.22), channel_id=1, source_target_pairs={{0,1},{1,0},{2,3},{3,2},{4,5},{5,4},{6,7},{7,6},{8,9},{9,8},{10,11... | collective-permute-start | bytes 5505032 | tf_op jit(solution)/shard_map/ppermute | solution.py:232
  48.6 9.8 %collective-permute-start.8 = (bf16[144,1024]{1,0:T(8,128)(2,1)S(1)}, bf16[144,1024]{1,0:T(8,128)(2,1)}, u32[]{:S(2)}, u32[]{:S(2)}) collective-permute-start(bf16[144,1024]{1,0:T(8,128)(2,1)S(1)} %collective-permute-done.6.refs_2_), channel_id=1, source_target_pairs={{0,2},{1,3},{2,6},{3,7},{4,0},{5,1},{6,10},{7,11},{8,4},{9,5},{10,... | collective-permute-start | bytes 884744 | tf_op jit(solution)/shard_map/ppermute | solution.py:241
  48.6 9.8 %collective-permute-start.13 = (bf16[144,1024]{1,0:T(8,128)(2,1)S(1)}, bf16[144,1024]{1,0:T(8,128)(2,1)}, u32[]{:S(2)}, u32[]{:S(2)}) collective-permute-start(bf16[144,1024]{1,0:T(8,128)(2,1)S(1)} %collective-permute-done.5.refs_1_), channel_id=1, source_target_pairs={{0,1},{1,0},{2,3},{3,2},{4,5},{5,4},{6,7},{7,6},{8,9},{9,8},{10,11... | collective-permute-start | bytes 884744 | tf_op jit(solution)/shard_map/ppermute | solution.py:232
  48.8 11.0 %collective-permute-start.9 = (bf16[144,1024]{1,0:T(8,128)(2,1)S(1)}, bf16[144,1024]{1,0:T(8,128)(2,1)}, u32[]{:S(2)}, u32[]{:S(2)}) collective-permute-start(bf16[144,1024]{1,0:T(8,128)(2,1)S(1)} %collective-permute-done.7.refs_3_), channel_id=1, source_target_pairs={{0,4},{1,5},{2,0},{3,1},{4,8},{5,9},{6,2},{7,3},{8,12},{9,13},{10,... | collective-permute-start | bytes 884744 | tf_op jit(solution)/shard_map/ppermute | solution.py:238
  52.3 9.3 %collective-permute-start.14 = (bf16[144,1024]{1,0:T(8,128)(2,1)S(1)}, bf16[144,1024]{1,0:T(8,128)(2,1)S(1)}, u32[]{:S(2)}, u32[]{:S(2)}) collective-permute-start(bf16[144,1024]{1,0:T(8,128)(2,1)S(1)} %collective-permute-done.6.refs_2_), channel_id=1, source_target_pairs={{0,1},{1,0},{2,3},{3,2},{4,5},{5,4},{6,7},{7,6},{8,9},{9,8},{10,11... | collective-permute-start | bytes 884744 | tf_op jit(solution)/shard_map/ppermute | solution.py:232
  58.4 9.6 %collective-permute-start.15 = (bf16[144,1024]{1,0:T(8,128)(2,1)S(1)}, bf16[144,1024]{1,0:T(8,128)(2,1)S(1)}, u32[]{:S(2)}, u32[]{:S(2)}) collective-permute-start(bf16[144,1024]{1,0:T(8,128)(2,1)S(1)} %collective-permute-done.7.refs_3_), channel_id=1, source_target_pairs={{0,1},{1,0},{2,3},{3,2},{4,5},{5,4},{6,7},{7,6},{8,9},{9,8},{10,11... | collective-permute-start | bytes 884744 | tf_op jit(solution)/shard_map/ppermute | solution.py:232
  58.4 9.6 %collective-permute-start.10 = (bf16[144,1024]{1,0:T(8,128)(2,1)}, bf16[144,1024]{1,0:T(8,128)(2,1)S(1)}, u32[]{:S(2)}, u32[]{:S(2)}) collective-permute-start(bf16[144,1024]{1,0:T(8,128)(2,1)} %collective-permute-done.8.refs_4_), channel_id=1, source_target_pairs={{0,2},{1,3},{2,6},{3,7},{4,0},{5,1},{6,10},{7,11},{8,4},{9,5},{10,... | collective-permute-start | bytes 884744 | tf_op jit(solution)/shard_map/ppermute | solution.py:241
  59.8 9.6 %collective-permute-start.11 = (bf16[144,1024]{1,0:T(8,128)(2,1)}, bf16[144,1024]{1,0:T(8,128)(2,1)}, u32[]{:S(2)}, u32[]{:S(2)}) collective-permute-start(bf16[144,1024]{1,0:T(8,128)(2,1)} %collective-permute-done.9.refs_5_), channel_id=1, source_target_pairs={{0,4},{1,5},{2,0},{3,1},{4,8},{5,9},{6,2},{7,3},{8,12},{9,13},{10,... | collective-permute-start | bytes 884744 | tf_op jit(solution)/shard_map/ppermute | solution.py:238
  61.7 11.9 %collective-permute-start.16 = (bf16[144,1024]{1,0:T(8,128)(2,1)}, bf16[144,1024]{1,0:T(8,128)(2,1)}, u32[]{:S(2)}, u32[]{:S(2)}) collective-permute-start(bf16[144,1024]{1,0:T(8,128)(2,1)} %collective-permute-done.8.refs_4_), channel_id=1, source_target_pairs={{0,1},{1,0},{2,3},{3,2},{4,5},{5,4},{6,7},{7,6},{8,9},{9,8},{10,11... | collective-permute-start | bytes 884744 | tf_op jit(solution)/shard_map/ppermute | solution.py:232
  68.1 5.6 %collective-permute-start.17 = (bf16[144,1024]{1,0:T(8,128)(2,1)}, bf16[144,1024]{1,0:T(8,128)(2,1)}, u32[]{:S(2)}, u32[]{:S(2)}) collective-permute-start(bf16[144,1024]{1,0:T(8,128)(2,1)} %collective-permute-done.9.refs_5_), channel_id=1, source_target_pairs={{0,1},{1,0},{2,3},{3,2},{4,5},{5,4},{6,7},{7,6},{8,9},{9,8},{10,11... | collective-permute-start | bytes 884744 | tf_op jit(solution)/shard_map/ppermute | solution.py:232
  68.8 4.8 %collective-permute-start.18 = (bf16[144,1024]{1,0:T(8,128)(2,1)S(1)}, bf16[144,1024]{1,0:T(8,128)(2,1)}, u32[]{:S(2)}, u32[]{:S(2)}) collective-permute-start(bf16[144,1024]{1,0:T(8,128)(2,1)S(1)} %collective-permute-done.10.refs_6_), channel_id=1, source_target_pairs={{0,1},{1,0},{2,3},{3,2},{4,5},{5,4},{6,7},{7,6},{8,9},{9,8},{10,11... | collective-permute-start | bytes 884744 | tf_op jit(solution)/shard_map/ppermute | solution.py:232
  69.3 4.3 %collective-permute-start.19 = (bf16[144,1024]{1,0:T(8,128)(2,1)}, bf16[144,1024]{1,0:T(8,128)(2,1)}, u32[]{:S(2)}, u32[]{:S(2)}) collective-permute-start(bf16[144,1024]{1,0:T(8,128)(2,1)} %collective-permute-done.11.refs_7_), channel_id=1, source_target_pairs={{0,1},{1,0},{2,3},{3,2},{4,5},{5,4},{6,7},{7,6},{8,9},{9,8},{10,11... | collective-permute-start | bytes 884744 | tf_op jit(solution)/shard_map/ppermute | solution.py:232
  131.8 23.2 %collective-permute-start.1 = (bf16[64,7168]{1,0:T(8,128)(2,1)S(1)}, bf16[64,7168]{1,0:T(8,128)(2,1)S(1)}, u32[]{:S(2)}, u32[]{:S(2)}) collective-permute-start(bf16[64,7168]{1,0:T(8,128)(2,1)S(1)} %add_convert_fusion.1), channel_id=1, source_target_pairs={{0,2},{1,3},{2,0},{3,1},{4,6},{5,7},{6,4},{7,5},{8,10},{9,11},{10,... | collective-permute-start | bytes 2752520 | tf_op jit(solution)/shard_map/ppermute | solution.py:232
  135.6 38.5 %collective-permute-start.21 = (bf16[64,7168]{1,0:T(8,128)(2,1)S(1)}, bf16[64,7168]{1,0:T(8,128)(2,1)S(1)}, u32[]{:S(2)}, u32[]{:S(2)}) collective-permute-start(bf16[64,7168]{1,0:T(8,128)(2,1)S(1)} %add_convert_fusion), channel_id=1, source_target_pairs={{0,2},{1,3},{2,0},{3,1},{4,6},{5,7},{6,4},{7,5},{8,10},{9,11},{10,... | collective-permute-start | bytes 2752520 | tf_op jit(solution)/shard_map/ppermute | solution.py:232
  155.3 21.8 %collective-permute-start.2 = (bf16[16,7168]{1,0:T(8,128)(2,1)S(1)}, bf16[16,7168]{1,0:T(8,128)(2,1)S(1)}, u32[]{:S(2)}, u32[]{:S(2)}) collective-permute-start(bf16[16,7168]{1,0:T(8,128)(2,1)S(1)} %get-tuple-element.29), channel_id=1, source_target_pairs={{0,4},{1,5},{2,6},{3,7},{4,0},{5,1},{6,2},{7,3},{8,12},{9,13},{10,... | collective-permute-start | bytes 688136 | tf_op jit(solution)/shard_map/ppermute | solution.py:232
  157.6 21.2 %collective-permute-start.3 = (bf16[16,7168]{1,0:T(8,128)(2,1)S(1)}, bf16[16,7168]{1,0:T(8,128)(2,1)S(1)}, u32[]{:S(2)}, u32[]{:S(2)}) collective-permute-start(bf16[16,7168]{1,0:T(8,128)(2,1)S(1)} %get-tuple-element.31), channel_id=1, source_target_pairs={{0,8},{1,9},{2,10},{3,11},{4,12},{5,13},{6,14},{7,15},{8,0},{9,1},... | collective-permute-start | bytes 688136 | tf_op jit(solution)/shard_map/ppermute | solution.py:232
  158.1 20.7 %collective-permute-start.4 = (bf16[16,7168]{1,0:T(8,128)(2,1)S(1)}, bf16[16,7168]{1,0:T(8,128)(2,1)S(1)}, u32[]{:S(2)}, u32[]{:S(2)}) collective-permute-start(bf16[16,7168]{1,0:T(8,128)(2,1)S(1)} %get-tuple-element.30), channel_id=1, source_target_pairs={{0,12},{1,13},{2,14},{3,15},{4,8},{5,9},{6,10},{7,11},{8,4},{9,5},... | collective-permute-start | bytes 688136 | tf_op jit(solution)/shard_map/ppermute | solution.py:232
  174.3 10.9 %collective-permute-start.22 = (bf16[16,7168]{1,0:T(8,128)(2,1)S(1)}, bf16[16,7168]{1,0:T(8,128)(2,1)S(1)}, u32[]{:S(2)}, u32[]{:S(2)}) collective-permute-start(bf16[16,7168]{1,0:T(8,128)(2,1)S(1)} %get-tuple-element.32), channel_id=1, source_target_pairs={{0,4},{1,5},{2,6},{3,7},{4,0},{5,1},{6,2},{7,3},{8,12},{9,13},{10,... | collective-permute-start | bytes 688136 | tf_op jit(solution)/shard_map/ppermute | solution.py:232
  176.3 19.3 %collective-permute-start.23 = (bf16[16,7168]{1,0:T(8,128)(2,1)S(1)}, bf16[16,7168]{1,0:T(8,128)(2,1)S(1)}, u32[]{:S(2)}, u32[]{:S(2)}) collective-permute-start(bf16[16,7168]{1,0:T(8,128)(2,1)S(1)} %get-tuple-element.34), channel_id=1, source_target_pairs={{0,8},{1,9},{2,10},{3,11},{4,12},{5,13},{6,14},{7,15},{8,0},{9,1},... | collective-permute-start | bytes 688136 | tf_op jit(solution)/shard_map/ppermute | solution.py:232
  177.2 18.4 %collective-permute-start.24 = (bf16[16,7168]{1,0:T(8,128)(2,1)S(1)}, bf16[16,7168]{1,0:T(8,128)(2,1)S(1)}, u32[]{:S(2)}, u32[]{:S(2)}) collective-permute-start(bf16[16,7168]{1,0:T(8,128)(2,1)S(1)} %get-tuple-element.33), channel_id=1, source_target_pairs={{0,12},{1,13},{2,14},{3,15},{4,8},{5,9},{6,10},{7,11},{8,4},{9,5},... | collective-permute-start | bytes 688136 | tf_op jit(solution)/shard_map/ppermute | solution.py:232
  (17 other events, 307.3 us)

commit v2 on v1

v2 whole, which is shorter than its diff:
```python
import functools

import jax
import jax.numpy as jnp
import numpy as np
from jax import lax
from jax.experimental import pallas as pl
from jax.experimental.pallas import tpu as pltpu
from jax.sharding import PartitionSpec as P

BLK = 128
LANES = 128
PAD_ROWS = 16
PAIRS = 16
SPARE_VMEM = 3 * 1024 * 1024
F32 = jnp.float32
BF16 = jnp.bfloat16


def in_vmem(x):
    return pltpu.with_memory_space_constraint(x, pltpu.VMEM)


def old_kernel(order_ref, scale_ref, act_ref, code_hbm, keep_ref, send_ref, act_scratch, code_buf, code_sem):
    groups, group_rows, width = act_ref.shape
    chunks, _, chunk_cols = code_buf.shape

    def arrival(c):
        columns = pl.ds(c * chunk_cols, chunk_cols)
        return pltpu.make_async_copy(code_hbm.at[:, columns], code_buf.at[c], code_sem.at[c])

    for c in range(chunks):
        arrival(c).start()
    for g in range(groups):
        act_scratch[g * group_rows : (g + 1) * group_rows, :] = act_ref[order_ref[g]]
    act = act_scratch[...]
    half = act.shape[0] // 2
    per_chunk = chunk_cols // BLK
    for c in range(chunks):
        arrival(c).wait()
        for t in range(0, per_chunk, 2):
            rows = []
            for i in range(width // BLK):
                pair = []
                for j in range(t, t + 2):
                    block = code_buf[c, i * BLK : (i + 1) * BLK, j * BLK : (j + 1) * BLK]
                    scale = scale_ref[i * chunks * per_chunk + c * per_chunk + j]
                    pair.append((block.astype(F32) * scale).astype(BF16))
                rows.append(jnp.concatenate(pair, axis=1))
            weight = jnp.concatenate(rows, axis=0)
            product = jnp.dot(act, weight, preferred_element_type=F32).astype(BF16)
            at = slice(c * chunk_cols + t * BLK, c * chunk_cols + (t + 2) * BLK)
            keep_ref[:, at] = product[:half]
            send_ref[:, at] = product[half:]


def halves_of(rows, part_blocks):
    shapes = []
    for blocks in part_blocks:
        shapes += [pltpu.VMEM((rows // 2, blocks * BLK), BF16)] * 2
    return shapes


def old_product(act, codes, scales, order):
    groups, group_rows, width = act.shape
    rows, cols = groups * group_rows, codes.shape[1]
    chunks = cols // (14 * BLK)
    whole = pl.BlockSpec(memory_space=pltpu.VMEM)
    return pl.pallas_call(
        old_kernel,
        grid_spec=pltpu.PrefetchScalarGridSpec(
            num_scalar_prefetch=2,
            grid=(),
            in_specs=[whole, pl.BlockSpec(memory_space=pl.ANY)],
            out_specs=[whole] * 2,
            scratch_shapes=[
                pltpu.VMEM((rows, width), BF16),
                pltpu.VMEM((chunks, width, cols // chunks), BF16),
                pltpu.SemaphoreType.DMA((chunks,)),
            ],
        ),
        out_shape=halves_of(rows, (cols // BLK,)),
        compiler_params=pltpu.CompilerParams(vmem_limit_bytes=2 * (rows + cols) * width + SPARE_VMEM),
        cost_estimate=pl.CostEstimate(
            flops=2 * rows * width * cols, bytes_accessed=2 * width * cols + 2 * rows * cols, transcendentals=0
        ),
        name="old_product",
    )(order, scales.reshape(-1), in_vmem(act), pltpu.with_memory_space_constraint(codes, pltpu.HBM))


def fresh_kernel(
    n_pieces, experts, row_count, top_count, part_blocks,
    pos_ref, steps_ref, column_ref, slot_ref, index_ref, scale_ref,
    *refs,
):
    pieces, code_ref = refs[:n_pieces], refs[n_pieces]
    outs, dense, total = refs[n_pieces + 1 : -2], refs[-2], refs[-1]
    width = pieces[0].shape[1]
    row_blocks = width // BLK
    routed = row_count * top_count
    slots = code_ref.shape[0]
    half = dense.shape[1] // 2

    row = lax.broadcasted_iota(jnp.int32, (experts * row_count, routed), 0)
    col = lax.broadcasted_iota(jnp.int32, (experts * row_count, routed), 1)
    same_row = row % row_count == col // top_count
    expert = (row // row_count).astype(F32)
    for i in range(n_pieces):
        route = pieces[i][routed : routed + PAD_ROWS, 0:routed].astype(F32)[0:1, :]
        pick = jnp.where(same_row & (expert == route), 1.0, 0.0).astype(BF16)
        spread = jnp.dot(pick, pieces[i][0:routed, :], preferred_element_type=F32).astype(BF16)
        at = pl.ds(pl.multiple_of(pos_ref[i] * row_count, row_count), row_count)
        for e in range(experts):
            for b in range(row_blocks):
                dense[e * row_blocks + b, at, :] = spread[
                    e * row_count : (e + 1) * row_count, b * BLK : (b + 1) * BLK
                ]

    def clear(j, carry):
        total[j] = jnp.zeros(total.shape[1:], F32)
        return carry

    def some_pairs(t, carry):
        products = []
        for u in range(PAIRS):
            number = t * PAIRS + u
            left, right = [], []
            for q in range(2):
                slot = slot_ref[2 * number + q]
                block = code_ref[jnp.minimum(slot, slots - 1)]
                right.append((block.astype(F32) * scale_ref[slot]).astype(BF16))
                left.append(dense[index_ref[slot]])
            left, right = jnp.concatenate(left, axis=1), jnp.concatenate(right, axis=0)
            products.append(jnp.dot(left, right, preferred_element_type=F32))
        for u in range(PAIRS):
            total[column_ref[t * PAIRS + u]] += products[u]
        return carry

    lax.fori_loop(0, total.shape[0], clear, 0)
    lax.fori_loop(0, steps_ref[0], some_pairs, 0)
    first = 0
    for part, blocks in enumerate(part_blocks):
        for j in range(blocks):
            done = total[first + j].astype(BF16)
            outs[2 * part][:, j * BLK : (j + 1) * BLK] = done[:half]
            outs[2 * part + 1][:, j * BLK : (j + 1) * BLK] = done[half:]
        first += blocks


def fresh_product(pieces, pos, codes, plan, part_blocks, experts, row_count, top_count):
    n_pieces = len(pieces)
    rows, cols = n_pieces * row_count, sum(part_blocks) * BLK
    width = pieces[0].shape[1]
    slots = codes.shape[0]
    whole = pl.BlockSpec(memory_space=pltpu.VMEM)
    outs = pl.pallas_call(
        functools.partial(fresh_kernel, n_pieces, experts, row_count, top_count, part_blocks),
        grid_spec=pltpu.PrefetchScalarGridSpec(
            num_scalar_prefetch=6,
            grid=(),
            in_specs=[whole] * (n_pieces + 1),
            out_specs=[whole] * (2 * len(part_blocks)),
            scratch_shapes=[
                pltpu.VMEM((experts * (width // BLK), rows, BLK), BF16),
                pltpu.VMEM((sum(part_blocks), rows, BLK), F32),
            ],
        ),
        out_shape=halves_of(rows, part_blocks),
        compiler_params=pltpu.CompilerParams(
            vmem_limit_bytes=2 * experts * width * rows + 4 * rows * cols + SPARE_VMEM
        ),
        cost_estimate=pl.CostEstimate(
            flops=2 * rows * BLK * BLK * slots, bytes_accessed=2 * slots * BLK * BLK + 2 * rows * cols, transcendentals=0
        ),
        name="fresh_product",
    )(pos, *plan, *[in_vmem(piece) for piece in pieces], in_vmem(codes))
    return [outs[2 * i : 2 * i + 2] for i in range(len(part_blocks))]


def fresh_plan(own_ids, own_scales, changed, col_blocks, row_blocks):
    slots_each = own_ids.shape[1]
    ids = own_ids.reshape(-1)
    count = ids.shape[0]
    column = ids % col_blocks
    index = jnp.repeat(changed, slots_each) * row_blocks + ids // col_blocks
    number = jnp.arange(count, dtype=jnp.int32)
    columns = jnp.arange(col_blocks, dtype=jnp.int32)
    most = -(-(count // 2 + (col_blocks + 1) // 2) // PAIRS) * PAIRS
    pairs = (jnp.sum((column[None, :] == columns[:, None]).astype(jnp.int32), axis=1) + 1) // 2
    before = jnp.sum(jnp.where(columns[None, :] < column[:, None], pairs[None, :], 0), axis=1)
    earlier = (column[None, :] == column[:, None]) & (number[None, :] < number[:, None])
    place = 2 * before + jnp.sum(earlier.astype(jnp.int32), axis=1)
    places = jnp.arange(2 * most, dtype=jnp.int32)
    slot = count - jnp.sum(jnp.where(place[None, :] == places[:, None], count - number[None, :], 0), axis=1)
    ends = jnp.sum(jnp.where(columns[None, :] <= columns[:, None], pairs[None, :], 0), axis=1)
    pair_column = jnp.sum((ends[None, :] <= places[:most, None]).astype(jnp.int32), axis=1)
    pair_column = jnp.minimum(pair_column, col_blocks - 1)
    steps = (ends[-1:] + PAIRS - 1) // PAIRS
    return steps, pair_column, slot, jnp.pad(index, (0, 1)), jnp.pad(own_scales.reshape(-1), (0, 1))


def add(*terms):
    total = terms[0].astype(F32)
    for term in terms[1:]:
        total = total + term.astype(F32)
    return total.astype(BF16)


class ChipGrid:
    SIZE = 16
    CYCLE = [(0, 0), (1, 0), (2, 0), (3, 0), (3, 1), (2, 1), (1, 1), (0, 1)]

    def __init__(self):
        cycle = self.CYCLE
        n = len(cycle)
        at = {chip: i for i, chip in enumerate(cycle)}
        number = lambda z, y, c: (z * 2 + y) * 2 + c
        self.forward, self.backward = [], []
        self.piece_rank = np.zeros((self.SIZE, self.SIZE), np.int32)
        self.rank_source = np.zeros((self.SIZE, self.SIZE), np.int32)
        for z in range(4):
            for y in range(2):
                for c in range(2):
                    me, i = number(z, y, c), at[(z, y)]
                    self.forward.append((me, number(*cycle[(i + 1) % n], c)))
                    self.backward.append((me, number(*cycle[(i - 1) % n], c)))
                    hops = [0, -1, 1, -2, 2, -3, 3, -4]
                    for dc in range(2):
                        for k, hop in enumerate(hops):
                            sz, sy = cycle[(i + hop) % n]
                            self.piece_rank[me, dc * 8 + k] = self.rank(sz ^ z, sy ^ y, dc)
                    for dz in range(4):
                        for dy in range(2):
                            for dc in range(2):
                                self.rank_source[me, self.rank(dz, dy, dc)] = number(z ^ dz, y ^ dy, c ^ dc)

    @staticmethod
    def rank(dz, dy, dc):
        return dc * 8 + dy * 4 + (dz % 2) * 2 + dz // 2

    def partner(self, x, dz, dy, dc):
        delta = (dz * 2 + dy) * 2 + dc
        return lax.ppermute(x, "expert", [(i, i ^ delta) for i in range(self.SIZE)])

    def ahead(self, x):
        return lax.ppermute(x, "expert", self.forward)

    def behind(self, x):
        return lax.ppermute(x, "expert", self.backward)

    def other_core(self, x):
        return self.partner(x, 0, 0, 1)

    def other_y(self, x):
        return self.partner(x, 0, 1, 0)

    def near_z(self, x):
        return self.partner(x, 1, 0, 0)

    def far_z(self, x):
        return self.partner(x, 2, 0, 0)


def add_rows(first, last, *terms):
    return add(*[term[first:last] for term in terms])


def body(
    hidden_act,
    routes,
    gates,
    down_codes,
    down_scales,
    changed,
    fresh_codes,
    fresh_scales,
    block_ids,
):
    experts = lax.axis_size("expert")
    learners = lax.axis_size("learner")
    own = lax.axis_index("expert")
    own_half = lax.axis_index("learner")
    step_count, row_count, top_count, width = hidden_act.shape
    cols = down_codes.shape[2]
    routed = row_count * top_count
    row_blocks, col_blocks = width // BLK, cols // BLK
    slots_each = fresh_codes.shape[2]
    some_unchanged = changed.shape[0] < experts

    gated = (hidden_act.astype(F32) * gates[..., None]).astype(BF16).reshape(step_count, routed, width)
    flat_routes = routes.reshape(step_count, routed)
    row = jnp.arange(experts * row_count, dtype=jnp.int32)
    entry = jnp.arange(routed, dtype=jnp.int32)

    def spread(step):
        pick = (row[:, None] // row_count == flat_routes[step][None, :]) & (
            row[:, None] % row_count == entry[None, :] // top_count
        )
        out = jnp.dot(pick.astype(BF16), gated[step], preferred_element_type=F32)
        return out.astype(BF16).reshape(experts, row_count, width)

    def with_routes(step):
        tail = jnp.zeros((PAD_ROWS, width), BF16).at[0, :routed].set(flat_routes[step].astype(BF16))
        return jnp.concatenate([gated[step], tail], axis=0)

    codes = fresh_codes.reshape((-1, BLK, BLK))
    scales = down_scales[0]

    part_blocks = (2 * (col_blocks // 4), col_blocks - 2 * (col_blocks // 4))

    def fresh_order(changed, block_ids):
        first = own * slots_each
        own_ids = lax.dynamic_slice_in_dim(block_ids[:, own_half], first, slots_each, axis=1)
        return fresh_plan(own_ids, fresh_scales[:, 0], changed, col_blocks, row_blocks)

    def old(act, order):
        return old_product(act, down_codes[0], scales, order)

    def fresh(pieces, pos, plan):
        return fresh_product(pieces, pos, codes, plan, part_blocks, experts, row_count, top_count)

    if experts == ChipGrid.SIZE and learners == 1 and not some_unchanged and step_count == 2:
        grid = ChipGrid()
        together = lax.optimization_barrier
        order = jnp.asarray(grid.rank_source)[own]
        pos = jnp.asarray(grid.piece_rank)[own]
        unit = row_count

        x = with_routes(1)
        f1, b1 = grid.ahead(x), grid.behind(x)
        act_old = lax.all_to_all(spread(0), "expert", split_axis=0, concat_axis=0, tiled=True)
        f1, b1, order, pos, changed, block_ids = together((f1, b1, order, pos, changed, block_ids))

        f2, b2 = grid.ahead(f1), grid.behind(b1)
        cores = [grid.other_core(piece) for piece in (x, f1, b1)]
        plan = fresh_order(changed, block_ids)
        f2, b2, cores, act_old, plan = together((f2, b2, cores, act_old, plan))

        f3, b3 = grid.ahead(f2), grid.behind(b2)
        keep_old, send_old = old(act_old, order)
        f3, b3, keep_old, send_old = together((f3, b3, keep_old, send_old))

        f4 = grid.ahead(f3)
        got_old = grid.other_core(send_old)
        cores += [grid.other_core(piece) for piece in (f2, b2, f3, b3)]
        far_old = add_rows(4 * unit, 8 * unit, keep_old, got_old)
        f4, cores, far_old = together((f4, cores, far_old))

        cut = 2 * (col_blocks // 3) * BLK
        first_old = grid.other_y(far_old[:, :cut])
        pieces = [x, f1, b1, f2, b2, f3, b3, f4] + cores + [grid.other_core(f4)]
        (keep_c, send_c), (keep_d, send_d) = fresh(pieces, pos, plan)
        first_old, send_c, send_d = together((first_old, send_c, send_d))

        rest_old = grid.other_y(far_old[:, cut:])
        got_c, got_d = grid.other_core(send_c), grid.other_core(send_d)
        far_c = add_rows(4 * unit, 8 * unit, keep_c, got_c)
        far_d = add_rows(4 * unit, 8 * unit, keep_d, got_d)
        rest_old, far_c, far_d = together((rest_old, far_c, far_d))

        old_terms = [keep_old, got_old, jnp.concatenate([first_old, rest_old], axis=1)]
        far_c = grid.other_y(far_c)
        near_old = grid.near_z(add_rows(2 * unit, 4 * unit, *old_terms))
        far_c, near_old, far_d = together((far_c, near_old, far_d))

        old_terms = [term[: 2 * unit] for term in old_terms] + [near_old]
        c_terms = [keep_c, got_c, far_c]
        far_d = grid.other_y(far_d)
        near_c = grid.near_z(add_rows(2 * unit, 4 * unit, *c_terms))
        end_old = grid.far_z(add_rows(unit, 2 * unit, *old_terms))
        far_d, near_c, end_old = together((far_d, near_c, end_old))

        c_terms = [term[: 2 * unit] for term in c_terms] + [near_c]
        d_terms = [keep_d, got_d, far_d]
        near_d = grid.near_z(add_rows(2 * unit, 4 * unit, *d_terms))
        end_c = grid.far_z(add_rows(unit, 2 * unit, *c_terms))
        near_d, end_c = together((near_d, end_c))

        d_terms = [term[: 2 * unit] for term in d_terms] + [near_d]
        end_d = grid.far_z(add_rows(unit, 2 * unit, *d_terms))
        out_old = add_rows(0, unit, *old_terms, end_old)
        out_c = add_rows(0, unit, *c_terms, end_c)
        out_d = add_rows(0, unit, *d_terms, end_d)
        return jnp.stack([out_old, jnp.concatenate([out_c, out_d], axis=1)])

    group = experts * learners
    straight = jnp.arange(group, dtype=jnp.int32)

    def joined(halves):
        return jnp.concatenate([jnp.concatenate(half, axis=0) for half in halves], axis=1)

    def combine(part):
        summed = lax.psum_scatter(part, "expert", scatter_dimension=0, tiled=True)
        return lax.all_to_all(summed, "learner", split_axis=0, concat_axis=1, tiled=True)

    def old_part(step):
        dense = lax.all_to_all(spread(step), "expert", split_axis=0, concat_axis=0, tiled=True)
        if step > 0:
            dense = jnp.where(jnp.any(changed == own), jnp.zeros_like(dense), dense)
        dense = lax.all_gather(dense, "learner", axis=1, tiled=False)
        dense = dense.reshape(group, row_count, width)
        chunks = []
        for first in range(0, group, at_once):
            act = dense[first : first + at_once]
            chunks.append(joined([old(act, straight[:at_once])]))
        return jnp.concatenate(chunks, axis=0)

    def fresh_part(step):
        everyone = lax.all_gather(with_routes(step), ("expert", "learner"), axis=0)
        chunks = []
        for first in range(0, group, at_once):
            pieces = [everyone[first + i] for i in range(at_once)]
            chunks.append(joined(fresh(pieces, straight[:at_once], plan)))
        return jnp.concatenate(chunks, axis=0)

    at_once = min(group, 16)
    plan = fresh_order(changed, block_ids)
    results = [combine(old_part(0))]
    for step in range(1, step_count):
        total = fresh_part(step)
        if some_unchanged:
            total = add(total, old_part(step))
        results.append(combine(total))
    return jnp.stack(results)


def solution(mesh):
    in_specs = (
        P(None, ("groups", "expert", "learner"), None, None),
        P(None, ("groups", "expert", "learner"), None),
        P(None, ("groups", "expert", "learner"), None),
        P("expert", None, "learner"),
        P("expert", None, "learner"),
        P("groups"),
        P("groups", "learner", "expert", None, None),
        P("groups", "learner", "expert"),
        P("groups", None, None),
    )
    out_specs = P(None, ("groups", "expert", "learner"), None)
    return jax.shard_map(body, mesh=mesh, in_specs=in_specs, out_specs=out_specs, check_vma=False)
```

time: 198 us -> 127 us (0.64)
  Pallas kernels: 73.1 us -> 23 us
  waiting for transfers between devices: 75.9 us -> 57 us
  local copies, waits for them, and re-layouts: 6.97 us -> 3.7 us
  starting transfers between devices: 31.5 us -> 34 us
    pallas_call x1, Pallas kernels: 57.6 us -> 15.1 us  [fresh_product(): pl.pallas_call(functools.partial(fresh_kernel, n_pieces, experts, row_cou...]
    ppermute x7, waiting for transfers between devices: 24.9 us -> 15.1 us  [the longest x4 12.7 us: ahead(): return lax.ppermute(x, 'expert', self.forward)]
    ppermute x18 -> x21, waiting for transfers between devices: 51 us -> 41.8 us  [partner(): return lax.ppermute(x, 'expert', [(i, i ^ delta) for i in range(self.SIZE)])]
    pallas_call x1, Pallas kernels: 15.6 us -> 7.86 us  [old_product(): pl.pallas_call(old_kernel, grid_spec=pltpu.PrefetchScalarGridSpec(num_sca...]
    ppermute x18 -> x21, starting transfers between devices: 14.1 us -> 17 us  [partner(): return lax.ppermute(x, 'expert', [(i, i ^ delta) for i in range(self.SIZE)])]
  transfers between devices with their start and end apart: 26 -> 29, of which waited for: 10 -> 18; matrix products, arithmetic and copies ran while one was open for 5% -> 5% of each run, Pallas kernels for 37% -> 18%
where the time goes in v2:
time: 127 us; the launch traced here: 126 us
  waiting for transfers between devices  57 us (45%)
  starting transfers between devices  34 us (27%)
  Pallas kernels  23 us (18%)
  other arithmetic  6.03 us (5%)
  local copies, waits for them, and re-layouts  3.7 us (3%)
    ppermute x21, waiting for transfers between devices, partner(): return lax.ppermute(x, 'expert', [(i, i ^ delta) for i in range(self.SIZE)])  41.8 us
    ppermute x21, starting transfers between devices, partner(): return lax.ppermute(x, 'expert', [(i, i ^ delta) for i in range(self.SIZE)])  17 us
    pallas_call x1, Pallas kernels, fresh_product(): pl.pallas_call(functools.partial(fresh_kernel, n_pieces, experts, row_cou...  15.1 us
    ppermute x4, waiting for transfers between devices, ahead(): return lax.ppermute(x, 'expert', self.forward)  12.7 us
    pallas_call x1, Pallas kernels, old_product(): pl.pallas_call(old_kernel, grid_spec=pltpu.PrefetchScalarGridSpec(num_sca...  7.86 us
    ppermute x4, starting transfers between devices, ahead(): return lax.ppermute(x, 'expert', self.forward)  7.83 us
    all_to_all x1, starting transfers between devices, body(): lax.all_to_all(spread(0), 'expert', split_axis=0, concat_axis=0, tiled=True)  6.3 us
    ppermute x3, starting transfers between devices, behind(): return lax.ppermute(x, 'expert', self.backward)  2.86 us
  transfers between devices with their start and end apart: 29, of which 18 were waited for; matrix products, arithmetic and copies ran while one was open for 5% of the time, Pallas kernels for 18%

profile of v2, /device:TPU:0, one launch (start us, length us, event | category | flops | bytes accessed | tf_op | source)
XLA Modules:
  0.0 125.9 jit_solution(9007345211661241948)
XLA Ops:
  3.5 2.6 %collective-permute-start.1 = (bf16[144,1024]{1,0:T(8,128)(2,1)S(1)}, bf16[144,1024]{1,0:T(8,128)(2,1)S(1)}, u32[]{:S(2)}, u32[]{:S(2)}) collective-permute-start(bf16[144,1024]{1,0:T(8,128)(2,1)S(1)} %fusion.2.refs_0_), channel_id=1, source_target_pairs={{0,2},{1,3},{2,6},{3,7},{4,0},{5,1},{6,10},{7,11},{8,4},{9,5},{10,... | collective-permute-start | bytes 884744 | tf_op jit(solution)/shard_map/ppermute | solution.py:249
  7.6 6.3 %all-to-all-start = ((bf16[16,16,1024]{2,1,0:T(8,128)(2,1)}), bf16[16,16,1024]{2,1,0:T(8,128)(2,1)S(1)}, u32[]{:S(2)}, u32[]{:S(2)}) async-start(bf16[16,16,1024]{2,1,0:T(8,128)(2,1)} %bitcast.4), calls=%async_computation | async-start | bytes 1048576 | tf_op jit(solution)/shard_map/all_to_all | solution.py:331
  17.6 1.7 %collective-permute-start.2 = (bf16[144,1024]{1,0:T(8,128)(2,1)S(1)}, bf16[144,1024]{1,0:T(8,128)(2,1)S(1)}, u32[]{:S(2)}, u32[]{:S(2)}) collective-permute-start(bf16[144,1024]{1,0:T(8,128)(2,1)S(1)} %collective-permute-done.refs_1_), channel_id=1, source_target_pairs={{0,4},{1,5},{2,0},{3,1},{4,8},{5,9},{6,2},{7,3},{8,12},{9,13},{10,... | collective-permute-start | bytes 884744 | tf_op jit(solution)/shard_map/ppermute | solution.py:246
  21.5 8.2 %collective-permute-done.2.refs_3_ = bf16[144,1024]{1,0:T(8,128)(2,1)S(1)} collective-permute-done((bf16[144,1024]{1,0:T(8,128)(2,1)S(1)}, bf16[144,1024]{1,0:T(8,128)(2,1)S(1)}, u32[]{:S(2)}, u32[]{:S(2)}) %collective-permute-start.2) | collective-permute-done | bytes 294944 | tf_op jit(solution)/shard_map/ppermute | solution.py:246
  29.7 2.0 %collective-permute-done.3.refs_4_ = bf16[144,1024]{1,0:T(8,128)(2,1)S(1)} collective-permute-done((bf16[144,1024]{1,0:T(8,128)(2,1)S(1)}, bf16[144,1024]{1,0:T(8,128)(2,1)S(1)}, u32[]{:S(2)}, u32[]{:S(2)}) %collective-permute-start.3) | collective-permute-done | bytes 294944 | tf_op jit(solution)/shard_map/ppermute | solution.py:249
  31.7 4.3 %collective-permute-start.7 = (bf16[144,1024]{1,0:T(8,128)(2,1)S(1)}, bf16[144,1024]{1,0:T(8,128)(2,1)S(1)}, u32[]{:S(2)}, u32[]{:S(2)}) collective-permute-start(bf16[144,1024]{1,0:T(8,128)(2,1)S(1)} %collective-permute-done.2.refs_3_), channel_id=1, source_target_pairs={{0,4},{1,5},{2,0},{3,1},{4,8},{5,9},{6,2},{7,3},{8,12},{9,13},{10,... | collective-permute-start | bytes 884744 | tf_op jit(solution)/shard_map/ppermute | solution.py:246
  36.0 7.9 %old_product.1 = (bf16[128,7168]{1,0:T(8,128)(2,1)S(1)}, bf16[128,7168]{1,0:T(8,128)(2,1)S(1)}) custom-call(s32[16]{0:T(128)S(1)} %get-tuple-element.73.order_ref, f32[448]{0:T(512)S(1)} %reshape_squeeze.7.scale_ref, bf16[16,16,1024]{2,1,0:T(8,128)(2,1)S(1)} %all-to-all-done.act_ref, bf16[1024,7168]{1,0:T(8,128)(2,1)} %bitcast.17), custom_call_target="tpu_custom_call" | custom-call | flops 3758096384 | bytes 18350080 | tf_op jit(solution)/shard_map/old_product/pallas_call | solution.py:69
  45.3 1.7 %collective-permute-start.10 = (bf16[144,1024]{1,0:T(8,128)(2,1)S(1)}, bf16[144,1024]{1,0:T(8,128)(2,1)S(1)}, u32[]{:S(2)}, u32[]{:S(2)}) collective-permute-start(bf16[144,1024]{1,0:T(8,128)(2,1)S(1)} %collective-permute-done.7.refs_5_), channel_id=1, source_target_pairs={{0,4},{1,5},{2,0},{3,1},{4,8},{5,9},{6,2},{7,3},{8,12},{9,13},{10,... | collective-permute-start | bytes 884744 | tf_op jit(solution)/shard_map/ppermute | solution.py:246
  49.8 4.5 %collective-permute-done.10.refs_7_ = bf16[144,1024]{1,0:T(8,128)(2,1)S(1)} collective-permute-done((bf16[144,1024]{1,0:T(8,128)(2,1)S(1)}, bf16[144,1024]{1,0:T(8,128)(2,1)S(1)}, u32[]{:S(2)}, u32[]{:S(2)}) %collective-permute-start.10) | collective-permute-done | bytes 294944 | tf_op jit(solution)/shard_map/ppermute | solution.py:246
  54.3 1.7 %collective-permute-start.15 = (bf16[64,4608]{1,0:T(8,128)(2,1)S(1)}, bf16[64,4608]{1,0:T(8,128)(2,1)S(1)}, u32[]{:S(2)}, u32[]{:S(2)}) collective-permute-start(bf16[64,4608]{1,0:T(8,128)(2,1)S(1)} %slice.199), channel_id=1, source_target_pairs={{0,2},{1,3},{2,0},{3,1},{4,6},{5,7},{6,4},{7,5},{8,10},{9,11},{10,... | collective-permute-start | bytes 1769480 | tf_op jit(solution)/shard_map/ppermute | solution.py:243
  56.0 15.1 %fresh_product.1 = (bf16[128,3584]{1,0:T(8,128)(2,1)S(1)}, bf16[128,3584]{1,0:T(8,128)(2,1)S(1)}, bf16[128,3584]{1,0:T(8,128)(2,1)S(1)}, bf16[128,3584]{1,0:T(8,128)(2,1)S(1)}) custom-call(s32[16]{0:T(128)S(1)} %get-tuple-element.85.pos_ref, s32[1]{0:T(128)S(6)} %select_n.93.steps_ref, s32[256]{0:T(256)S(1)} %broadcast_minimum_fusion.column_ref, ...), custom_call_target="tpu_custom_call" | custom-call | flops 3758096384 | bytes 18350080 | tf_op jit(solution)/shard_map/fresh_product/pallas_call | solution.py:156
  73.8 1.6 %collective-permute-done.19 = bf16[128,3584]{1,0:T(8,128)(2,1)S(1)} collective-permute-done((bf16[128,3584]{1,0:T(8,128)(2,1)S(1)}, bf16[128,3584]{1,0:T(8,128)(2,1)S(1)}, u32[]{:S(2)}, u32[]{:S(2)}) %collective-permute-start.19) | collective-permute-done | bytes 917536 | tf_op jit(solution)/shard_map/ppermute | solution.py:243
  75.5 5.9 %collective-permute-done.17 = bf16[64,2560]{1,0:T(8,128)(2,1)S(1)} collective-permute-done((bf16[64,2560]{1,0:T(8,128)(2,1)S(1)}, bf16[64,2560]{1,0:T(8,128)(2,1)S(1)}, u32[]{:S(2)}, u32[]{:S(2)}) %collective-permute-start.17) | collective-permute-done | bytes 327712 | tf_op jit(solution)/shard_map/ppermute | solution.py:243
  81.6 1.8 %collective-permute-start.21 = (bf16[32,7168]{1,0:T(8,128)(2,1)S(1)}, bf16[32,7168]{1,0:T(8,128)(2,1)S(1)}, u32[]{:S(2)}, u32[]{:S(2)}) collective-permute-start(bf16[32,7168]{1,0:T(8,128)(2,1)S(1)} %add_convert_fusion.1), channel_id=1, source_target_pairs={{0,4},{1,5},{2,6},{3,7},{4,0},{5,1},{6,2},{7,3},{8,12},{9,13},{10,... | collective-permute-start | bytes 1376264 | tf_op jit(solution)/shard_map/ppermute | solution.py:243
  84.9 8.7 %collective-permute-done.21 = bf16[32,7168]{1,0:T(8,128)(2,1)S(1)} collective-permute-done((bf16[32,7168]{1,0:T(8,128)(2,1)S(1)}, bf16[32,7168]{1,0:T(8,128)(2,1)S(1)}, u32[]{:S(2)}, u32[]{:S(2)}) %collective-permute-start.21) | collective-permute-done | bytes 458784 | tf_op jit(solution)/shard_map/ppermute | solution.py:243
  95.6 1.5 %collective-permute-start.22 = (bf16[64,3584]{1,0:T(8,128)(2,1)S(1)}, bf16[64,3584]{1,0:T(8,128)(2,1)S(1)}, u32[]{:S(2)}, u32[]{:S(2)}) collective-permute-start(bf16[64,3584]{1,0:T(8,128)(2,1)S(1)} %add_convert_fusion.2), channel_id=1, source_target_pairs={{0,2},{1,3},{2,0},{3,1},{4,6},{5,7},{6,4},{7,5},{8,10},{9,11},{10,... | collective-permute-start | bytes 1376264 | tf_op jit(solution)/shard_map/ppermute | solution.py:243
  97.2 1.7 %collective-permute-start.24 = (bf16[16,7168]{1,0:T(8,128)(2,1)S(1)}, bf16[16,7168]{1,0:T(8,128)(2,1)S(1)}, u32[]{:S(2)}, u32[]{:S(2)}) collective-permute-start(bf16[16,7168]{1,0:T(8,128)(2,1)S(1)} %add_convert_fusion.6), channel_id=1, source_target_pairs={{0,8},{1,9},{2,10},{3,11},{4,12},{5,13},{6,14},{7,15},{8,0},{9,1},... | collective-permute-start | bytes 688136 | tf_op jit(solution)/shard_map/ppermute | solution.py:243
  98.9 4.8 %collective-permute-done.23 = bf16[32,3584]{1,0:T(8,128)(2,1)S(1)} collective-permute-done((bf16[32,3584]{1,0:T(8,128)(2,1)S(1)}, bf16[32,3584]{1,0:T(8,128)(2,1)S(1)}, u32[]{:S(2)}, u32[]{:S(2)}) %collective-permute-start.23) | collective-permute-done | bytes 229408 | tf_op jit(solution)/shard_map/ppermute | solution.py:243
  103.7 6.2 %collective-permute-done.24 = bf16[16,7168]{1,0:T(8,128)(2,1)S(1)} collective-permute-done((bf16[16,7168]{1,0:T(8,128)(2,1)S(1)}, bf16[16,7168]{1,0:T(8,128)(2,1)S(1)}, u32[]{:S(2)}, u32[]{:S(2)}) %collective-permute-start.24) | collective-permute-done | bytes 229408 | tf_op jit(solution)/shard_map/ppermute | solution.py:243
  110.1 1.8 %collective-permute-start.25 = (bf16[32,3584]{1,0:T(8,128)(2,1)S(1)}, bf16[32,3584]{1,0:T(8,128)(2,1)S(1)}, u32[]{:S(2)}, u32[]{:S(2)}) collective-permute-start(bf16[32,3584]{1,0:T(8,128)(2,1)S(1)} %add_convert_fusion.4), channel_id=1, source_target_pairs={{0,4},{1,5},{2,6},{3,7},{4,0},{5,1},{6,2},{7,3},{8,12},{9,13},{10,... | collective-permute-start | bytes 688136 | tf_op jit(solution)/shard_map/ppermute | solution.py:243
  112.1 4.1 %collective-permute-done.26 = bf16[16,3584]{1,0:T(8,128)(2,1)S(1)} collective-permute-done((bf16[16,3584]{1,0:T(8,128)(2,1)S(1)}, bf16[16,3584]{1,0:T(8,128)(2,1)S(1)}, u32[]{:S(2)}, u32[]{:S(2)}) %collective-permute-start.26) | collective-permute-done | bytes 114720 | tf_op jit(solution)/shard_map/ppermute | solution.py:243
  116.2 1.7 %collective-permute-done.25 = bf16[32,3584]{1,0:T(8,128)(2,1)S(1)} collective-permute-done((bf16[32,3584]{1,0:T(8,128)(2,1)S(1)}, bf16[32,3584]{1,0:T(8,128)(2,1)S(1)}, u32[]{:S(2)}, u32[]{:S(2)}) %collective-permute-start.25) | collective-permute-done | bytes 229408 | tf_op jit(solution)/shard_map/ppermute | solution.py:243
  118.0 2.5 %collective-permute-start.27 = (bf16[16,3584]{1,0:T(8,128)(2,1)S(1)}, bf16[16,3584]{1,0:T(8,128)(2,1)S(1)}, u32[]{:S(2)}, u32[]{:S(2)}) collective-permute-start(bf16[16,3584]{1,0:T(8,128)(2,1)S(1)} %add_convert_fusion.9), channel_id=1, source_target_pairs={{0,8},{1,9},{2,10},{3,11},{4,12},{5,13},{6,14},{7,15},{8,0},{9,1},... | collective-permute-start | bytes 344072 | tf_op jit(solution)/shard_map/ppermute | solution.py:243
  120.6 4.4 %collective-permute-done.27 = bf16[16,3584]{1,0:T(8,128)(2,1)S(1)} collective-permute-done((bf16[16,3584]{1,0:T(8,128)(2,1)S(1)}, bf16[16,3584]{1,0:T(8,128)(2,1)S(1)}, u32[]{:S(2)}, u32[]{:S(2)}) %collective-permute-start.27) | collective-permute-done | bytes 114720 | tf_op jit(solution)/shard_map/ppermute | solution.py:243
  (106 shorter events, 22.2 us)
Async XLA Ops:
  3.0 18.5 %collective-permute-start.4 = (bf16[144,1024]{1,0:T(8,128)(2,1)S(1)}, bf16[144,1024]{1,0:T(8,128)(2,1)S(1)}, u32[]{:S(2)}, u32[]{:S(2)}) collective-permute-start(bf16[144,1024]{1,0:T(8,128)(2,1)S(1)} %fusion.2.refs_0_), channel_id=1, source_target_pairs={{0,1},{1,0},{2,3},{3,2},{4,5},{5,4},{6,7},{7,6},{8,9},{9,8},{10,11... | collective-permute-start | bytes 884744 | tf_op jit(solution)/shard_map/ppermute | solution.py:243
  3.5 12.5 %collective-permute-start.1 = (bf16[144,1024]{1,0:T(8,128)(2,1)S(1)}, bf16[144,1024]{1,0:T(8,128)(2,1)S(1)}, u32[]{:S(2)}, u32[]{:S(2)}) collective-permute-start(bf16[144,1024]{1,0:T(8,128)(2,1)S(1)} %fusion.2.refs_0_), channel_id=1, source_target_pairs={{0,2},{1,3},{2,6},{3,7},{4,0},{5,1},{6,10},{7,11},{8,4},{9,5},{10,... | collective-permute-start | bytes 884744 | tf_op jit(solution)/shard_map/ppermute | solution.py:249
  6.1 9.9 %collective-permute-start = (bf16[144,1024]{1,0:T(8,128)(2,1)S(1)}, bf16[144,1024]{1,0:T(8,128)(2,1)S(1)}, u32[]{:S(2)}, u32[]{:S(2)}) collective-permute-start(bf16[144,1024]{1,0:T(8,128)(2,1)S(1)} %fusion.2.refs_0_), channel_id=1, source_target_pairs={{0,4},{1,5},{2,0},{3,1},{4,8},{5,9},{6,2},{7,3},{8,12},{9,13},{10,... | collective-permute-start | bytes 884744 | tf_op jit(solution)/shard_map/ppermute | solution.py:246
  7.6 24.2 %all-to-all-start = ((bf16[16,16,1024]{2,1,0:T(8,128)(2,1)}), bf16[16,16,1024]{2,1,0:T(8,128)(2,1)S(1)}, u32[]{:S(2)}, u32[]{:S(2)}) async-start(bf16[16,16,1024]{2,1,0:T(8,128)(2,1)} %bitcast.4), calls=%async_computation | async-start | bytes 1048576 | tf_op jit(solution)/shard_map/all_to_all | solution.py:331
  17.1 4.4 %collective-permute-start.5 = (bf16[144,1024]{1,0:T(8,128)(2,1)S(1)}, bf16[144,1024]{1,0:T(8,128)(2,1)S(1)}, u32[]{:S(2)}, u32[]{:S(2)}) collective-permute-start(bf16[144,1024]{1,0:T(8,128)(2,1)S(1)} %collective-permute-done.refs_1_), channel_id=1, source_target_pairs={{0,1},{1,0},{2,3},{3,2},{4,5},{5,4},{6,7},{7,6},{8,9},{9,8},{10,11... | collective-permute-start | bytes 884744 | tf_op jit(solution)/shard_map/ppermute | solution.py:243
  17.6 12.1 %collective-permute-start.2 = (bf16[144,1024]{1,0:T(8,128)(2,1)S(1)}, bf16[144,1024]{1,0:T(8,128)(2,1)S(1)}, u32[]{:S(2)}, u32[]{:S(2)}) collective-permute-start(bf16[144,1024]{1,0:T(8,128)(2,1)S(1)} %collective-permute-done.refs_1_), channel_id=1, source_target_pairs={{0,4},{1,5},{2,0},{3,1},{4,8},{5,9},{6,2},{7,3},{8,12},{9,13},{10,... | collective-permute-start | bytes 884744 | tf_op jit(solution)/shard_map/ppermute | solution.py:246
  19.3 10.4 %collective-permute-start.6 = (bf16[144,1024]{1,0:T(8,128)(2,1)S(1)}, bf16[144,1024]{1,0:T(8,128)(2,1)S(1)}, u32[]{:S(2)}, u32[]{:S(2)}) collective-permute-start(bf16[144,1024]{1,0:T(8,128)(2,1)S(1)} %collective-permute-done.1.refs_2_), channel_id=1, source_target_pairs={{0,1},{1,0},{2,3},{3,2},{4,5},{5,4},{6,7},{7,6},{8,9},{9,8},{10,11... | collective-permute-start | bytes 884744 | tf_op jit(solution)/shard_map/ppermute | solution.py:243
  19.3 12.4 %collective-permute-start.3 = (bf16[144,1024]{1,0:T(8,128)(2,1)S(1)}, bf16[144,1024]{1,0:T(8,128)(2,1)S(1)}, u32[]{:S(2)}, u32[]{:S(2)}) collective-permute-start(bf16[144,1024]{1,0:T(8,128)(2,1)S(1)} %collective-permute-done.1.refs_2_), channel_id=1, source_target_pairs={{0,2},{1,3},{2,6},{3,7},{4,0},{5,1},{6,10},{7,11},{8,4},{9,5},{10,... | collective-permute-start | bytes 884744 | tf_op jit(solution)/shard_map/ppermute | solution.py:249
  31.7 12.2 %collective-permute-start.7 = (bf16[144,1024]{1,0:T(8,128)(2,1)S(1)}, bf16[144,1024]{1,0:T(8,128)(2,1)S(1)}, u32[]{:S(2)}, u32[]{:S(2)}) collective-permute-start(bf16[144,1024]{1,0:T(8,128)(2,1)S(1)} %collective-permute-done.2.refs_3_), channel_id=1, source_target_pairs={{0,4},{1,5},{2,0},{3,1},{4,8},{5,9},{6,2},{7,3},{8,12},{9,13},{10,... | collective-permute-start | bytes 884744 | tf_op jit(solution)/shard_map/ppermute | solution.py:246
  36.0 8.3 %collective-permute-start.8 = (bf16[144,1024]{1,0:T(8,128)(2,1)S(1)}, bf16[144,1024]{1,0:T(8,128)(2,1)S(1)}, u32[]{:S(2)}, u32[]{:S(2)}) collective-permute-start(bf16[144,1024]{1,0:T(8,128)(2,1)S(1)} %collective-permute-done.3.refs_4_), channel_id=1, source_target_pairs={{0,2},{1,3},{2,6},{3,7},{4,0},{5,1},{6,10},{7,11},{8,4},{9,5},{10,... | collective-permute-start | bytes 884744 | tf_op jit(solution)/shard_map/ppermute | solution.py:249
  44.3 4.2 %collective-permute-start.11 = (bf16[144,1024]{1,0:T(8,128)(2,1)S(1)}, bf16[144,1024]{1,0:T(8,128)(2,1)S(1)}, u32[]{:S(2)}, u32[]{:S(2)}) collective-permute-start(bf16[144,1024]{1,0:T(8,128)(2,1)S(1)} %collective-permute-done.2.refs_3_), channel_id=1, source_target_pairs={{0,1},{1,0},{2,3},{3,2},{4,5},{5,4},{6,7},{7,6},{8,9},{9,8},{10,11... | collective-permute-start | bytes 884744 | tf_op jit(solution)/shard_map/ppermute | solution.py:243
  44.8 4.1 %collective-permute-start.12 = (bf16[144,1024]{1,0:T(8,128)(2,1)S(1)}, bf16[144,1024]{1,0:T(8,128)(2,1)S(1)}, u32[]{:S(2)}, u32[]{:S(2)}) collective-permute-start(bf16[144,1024]{1,0:T(8,128)(2,1)S(1)} %collective-permute-done.3.refs_4_), channel_id=1, source_target_pairs={{0,1},{1,0},{2,3},{3,2},{4,5},{5,4},{6,7},{7,6},{8,9},{9,8},{10,11... | collective-permute-start | bytes 884744 | tf_op jit(solution)/shard_map/ppermute | solution.py:243
  44.8 5.0 %collective-permute-start.13 = (bf16[144,1024]{1,0:T(8,128)(2,1)S(1)}, bf16[144,1024]{1,0:T(8,128)(2,1)S(1)}, u32[]{:S(2)}, u32[]{:S(2)}) collective-permute-start(bf16[144,1024]{1,0:T(8,128)(2,1)S(1)} %collective-permute-done.7.refs_5_), channel_id=1, source_target_pairs={{0,1},{1,0},{2,3},{3,2},{4,5},{5,4},{6,7},{7,6},{8,9},{9,8},{10,11... | collective-permute-start | bytes 884744 | tf_op jit(solution)/shard_map/ppermute | solution.py:243
  45.3 8.9 %collective-permute-start.10 = (bf16[144,1024]{1,0:T(8,128)(2,1)S(1)}, bf16[144,1024]{1,0:T(8,128)(2,1)S(1)}, u32[]{:S(2)}, u32[]{:S(2)}) collective-permute-start(bf16[144,1024]{1,0:T(8,128)(2,1)S(1)} %collective-permute-done.7.refs_5_), channel_id=1, source_target_pairs={{0,4},{1,5},{2,0},{3,1},{4,8},{5,9},{6,2},{7,3},{8,12},{9,13},{10,... | collective-permute-start | bytes 884744 | tf_op jit(solution)/shard_map/ppermute | solution.py:246
  54.3 16.8 %collective-permute-start.15 = (bf16[64,4608]{1,0:T(8,128)(2,1)S(1)}, bf16[64,4608]{1,0:T(8,128)(2,1)S(1)}, u32[]{:S(2)}, u32[]{:S(2)}) collective-permute-start(bf16[64,4608]{1,0:T(8,128)(2,1)S(1)} %slice.199), channel_id=1, source_target_pairs={{0,2},{1,3},{2,0},{3,1},{4,6},{5,7},{6,4},{7,5},{8,10},{9,11},{10,... | collective-permute-start | bytes 1769480 | tf_op jit(solution)/shard_map/ppermute | solution.py:243
  71.4 10.0 %collective-permute-start.17 = (bf16[64,2560]{1,0:T(8,128)(2,1)S(1)}, bf16[64,2560]{1,0:T(8,128)(2,1)S(1)}, u32[]{:S(2)}, u32[]{:S(2)}) collective-permute-start(bf16[64,2560]{1,0:T(8,128)(2,1)S(1)} %slice.200), channel_id=1, source_target_pairs={{0,2},{1,3},{2,0},{3,1},{4,6},{5,7},{6,4},{7,5},{8,10},{9,11},{10,... | collective-permute-start | bytes 983048 | tf_op jit(solution)/shard_map/ppermute | solution.py:243
  81.6 12.0 %collective-permute-start.21 = (bf16[32,7168]{1,0:T(8,128)(2,1)S(1)}, bf16[32,7168]{1,0:T(8,128)(2,1)S(1)}, u32[]{:S(2)}, u32[]{:S(2)}) collective-permute-start(bf16[32,7168]{1,0:T(8,128)(2,1)S(1)} %add_convert_fusion.1), channel_id=1, source_target_pairs={{0,4},{1,5},{2,6},{3,7},{4,0},{5,1},{6,2},{7,3},{8,12},{9,13},{10,... | collective-permute-start | bytes 1376264 | tf_op jit(solution)/shard_map/ppermute | solution.py:243
  83.4 11.6 %collective-permute-start.20 = (bf16[64,3584]{1,0:T(8,128)(2,1)S(1)}, bf16[64,3584]{1,0:T(8,128)(2,1)S(1)}, u32[]{:S(2)}, u32[]{:S(2)}) collective-permute-start(bf16[64,3584]{1,0:T(8,128)(2,1)S(1)} %add_convert_fusion.3), channel_id=1, source_target_pairs={{0,2},{1,3},{2,0},{3,1},{4,6},{5,7},{6,4},{7,5},{8,10},{9,11},{10,... | collective-permute-start | bytes 1376264 | tf_op jit(solution)/shard_map/ppermute | solution.py:243
  95.1 8.5 %collective-permute-start.23 = (bf16[32,3584]{1,0:T(8,128)(2,1)S(1)}, bf16[32,3584]{1,0:T(8,128)(2,1)S(1)}, u32[]{:S(2)}, u32[]{:S(2)}) collective-permute-start(bf16[32,3584]{1,0:T(8,128)(2,1)S(1)} %add_convert_fusion.7), channel_id=1, source_target_pairs={{0,4},{1,5},{2,6},{3,7},{4,0},{5,1},{6,2},{7,3},{8,12},{9,13},{10,... | collective-permute-start | bytes 688136 | tf_op jit(solution)/shard_map/ppermute | solution.py:243
  95.6 14.3 %collective-permute-start.22 = (bf16[64,3584]{1,0:T(8,128)(2,1)S(1)}, bf16[64,3584]{1,0:T(8,128)(2,1)S(1)}, u32[]{:S(2)}, u32[]{:S(2)}) collective-permute-start(bf16[64,3584]{1,0:T(8,128)(2,1)S(1)} %add_convert_fusion.2), channel_id=1, source_target_pairs={{0,2},{1,3},{2,0},{3,1},{4,6},{5,7},{6,4},{7,5},{8,10},{9,11},{10,... | collective-permute-start | bytes 1376264 | tf_op jit(solution)/shard_map/ppermute | solution.py:243
  97.2 12.6 %collective-permute-start.24 = (bf16[16,7168]{1,0:T(8,128)(2,1)S(1)}, bf16[16,7168]{1,0:T(8,128)(2,1)S(1)}, u32[]{:S(2)}, u32[]{:S(2)}) collective-permute-start(bf16[16,7168]{1,0:T(8,128)(2,1)S(1)} %add_convert_fusion.6), channel_id=1, source_target_pairs={{0,8},{1,9},{2,10},{3,11},{4,12},{5,13},{6,14},{7,15},{8,0},{9,1},... | collective-permute-start | bytes 688136 | tf_op jit(solution)/shard_map/ppermute | solution.py:243
  109.9 6.2 %collective-permute-start.26 = (bf16[16,3584]{1,0:T(8,128)(2,1)S(1)}, bf16[16,3584]{1,0:T(8,128)(2,1)S(1)}, u32[]{:S(2)}, u32[]{:S(2)}) collective-permute-start(bf16[16,3584]{1,0:T(8,128)(2,1)S(1)} %add_convert_fusion.11), channel_id=1, source_target_pairs={{0,8},{1,9},{2,10},{3,11},{4,12},{5,13},{6,14},{7,15},{8,0},{9,1},... | collective-permute-start | bytes 344072 | tf_op jit(solution)/shard_map/ppermute | solution.py:243
  110.1 7.8 %collective-permute-start.25 = (bf16[32,3584]{1,0:T(8,128)(2,1)S(1)}, bf16[32,3584]{1,0:T(8,128)(2,1)S(1)}, u32[]{:S(2)}, u32[]{:S(2)}) collective-permute-start(bf16[32,3584]{1,0:T(8,128)(2,1)S(1)} %add_convert_fusion.4), channel_id=1, source_target_pairs={{0,4},{1,5},{2,6},{3,7},{4,0},{5,1},{6,2},{7,3},{8,12},{9,13},{10,... | collective-permute-start | bytes 688136 | tf_op jit(solution)/shard_map/ppermute | solution.py:243
  118.0 7.0 %collective-permute-start.27 = (bf16[16,3584]{1,0:T(8,128)(2,1)S(1)}, bf16[16,3584]{1,0:T(8,128)(2,1)S(1)}, u32[]{:S(2)}, u32[]{:S(2)}) collective-permute-start(bf16[16,3584]{1,0:T(8,128)(2,1)S(1)} %add_convert_fusion.9), channel_id=1, source_target_pairs={{0,8},{1,9},{2,10},{3,11},{4,12},{5,13},{6,14},{7,15},{8,0},{9,1},... | collective-permute-start | bytes 344072 | tf_op jit(solution)/shard_map/ppermute | solution.py:243
  (10 other events, 86.1 us)

commit v3 on v2

--- a/solution.py
+++ b/solution.py
@@ -81,9 +81,7 @@
         ),
         out_shape=halves_of(rows, (cols // BLK,)),
         compiler_params=pltpu.CompilerParams(vmem_limit_bytes=2 * (rows + cols) * width + SPARE_VMEM),
-        cost_estimate=pl.CostEstimate(
-            flops=2 * rows * width * cols, bytes_accessed=2 * width * cols + 2 * rows * cols, transcendentals=0
-        ),
+        cost_estimate=pl.CostEstimate(flops=0, bytes_accessed=0, transcendentals=0),
         name="old_product",
     )(order, scales.reshape(-1), in_vmem(act), pltpu.with_memory_space_constraint(codes, pltpu.HBM))
 
@@ -169,9 +167,7 @@
         compiler_params=pltpu.CompilerParams(
             vmem_limit_bytes=2 * experts * width * rows + 4 * rows * cols + SPARE_VMEM
         ),
-        cost_estimate=pl.CostEstimate(
-            flops=2 * rows * BLK * BLK * slots, bytes_accessed=2 * slots * BLK * BLK + 2 * rows * cols, transcendentals=0
-        ),
+        cost_estimate=pl.CostEstimate(flops=0, bytes_accessed=0, transcendentals=0),
         name="fresh_product",
     )(pos, *plan, *[in_vmem(piece) for piece in pieces], in_vmem(codes))
     return [outs[2 * i : 2 * i + 2] for i in range(len(part_blocks))]
@@ -215,20 +211,22 @@
         n = len(cycle)
         at = {chip: i for i, chip in enumerate(cycle)}
         number = lambda z, y, c: (z * 2 + y) * 2 + c
-        self.forward, self.backward = [], []
+        self.ring = []
         self.piece_rank = np.zeros((self.SIZE, self.SIZE), np.int32)
         self.rank_source = np.zeros((self.SIZE, self.SIZE), np.int32)
         for z in range(4):
             for y in range(2):
                 for c in range(2):
                     me, i = number(z, y, c), at[(z, y)]
-                    self.forward.append((me, number(*cycle[(i + 1) % n], c)))
-                    self.backward.append((me, number(*cycle[(i - 1) % n], c)))
-                    hops = [0, -1, 1, -2, 2, -3, 3, -4]
-                    for dc in range(2):
-                        for k, hop in enumerate(hops):
-                            sz, sy = cycle[(i + hop) % n]
-                            self.piece_rank[me, dc * 8 + k] = self.rank(sz ^ z, sy ^ y, dc)
+                    way = 1 if c == 0 else -1
+                    self.ring.append((me, number(*cycle[(i + way) % n], c)))
+                    found = [(0, 0), (0, 1)]
+                    for hop in (1, 2, 3):
+                        found += [(-way * hop, 0), (-way * hop, 1), (way * hop, 1), (way * hop, 0)]
+                    found += [(4, 0), (4, 1)]
+                    for k, (offset, dc) in enumerate(found):
+                        sz, sy = cycle[(i + offset) % n]
+                        self.piece_rank[me, k] = self.rank(sz ^ z, sy ^ y, dc)
                     for dz in range(4):
                         for dy in range(2):
                             for dc in range(2):
@@ -242,11 +240,8 @@
         delta = (dz * 2 + dy) * 2 + dc
         return lax.ppermute(x, "expert", [(i, i ^ delta) for i in range(self.SIZE)])
 
-    def ahead(self, x):
-        return lax.ppermute(x, "expert", self.forward)
-
-    def behind(self, x):
-        return lax.ppermute(x, "expert", self.backward)
+    def hop(self, x):
+        return lax.ppermute(x, "expert", self.ring)
 
     def other_core(self, x):
         return self.partner(x, 0, 0, 1)
@@ -263,6 +258,10 @@
 
 def add_rows(first, last, *terms):
     return add(*[term[first:last] for term in terms])
+
+
+def add_cols(first, last, first_col, last_col, *terms):
+    return add(*[term[first:last, first_col:last_col] for term in terms])
 
 
 def body(
@@ -306,9 +305,10 @@
     codes = fresh_codes.reshape((-1, BLK, BLK))
     scales = down_scales[0]
 
-    part_blocks = (2 * (col_blocks // 4), col_blocks - 2 * (col_blocks // 4))
-
-    def fresh_order(changed, block_ids):
+    third = 2 * (col_blocks // 6)
+    part_blocks = (col_blocks - 2 * third, third, third)
+
+    def fresh_order(changed, block_ids, fresh_scales):
         first = own * slots_each
         own_ids = lax.dynamic_slice_in_dim(block_ids[:, own_half], first, slots_each, axis=1)
         return fresh_plan(own_ids, fresh_scales[:, 0], changed, col_blocks, row_blocks)
@@ -326,62 +326,86 @@
         pos = jnp.asarray(grid.piece_rank)[own]
         unit = row_count
 
-        x = with_routes(1)
-        f1, b1 = grid.ahead(x), grid.behind(x)
-        act_old = lax.all_to_all(spread(0), "expert", split_axis=0, concat_axis=0, tiled=True)
-        f1, b1, order, pos, changed, block_ids = together((f1, b1, order, pos, changed, block_ids))
-
-        f2, b2 = grid.ahead(f1), grid.behind(b1)
-        cores = [grid.other_core(piece) for piece in (x, f1, b1)]
-        plan = fresh_order(changed, block_ids)
-        f2, b2, cores, act_old, plan = together((f2, b2, cores, act_old, plan))
-
-        f3, b3 = grid.ahead(f2), grid.behind(b2)
+        p = [with_routes(1)]
+        p.append(grid.hop(p[0]))
+        q = [grid.other_core(p[0])]
+        q[0], spread_old = together((q[0], spread(0)))
+        q.append(grid.hop(q[0]))
+        act_old = lax.all_to_all(spread_old, "expert", split_axis=0, concat_axis=0, tiled=True)
+        q[1], order, pos, changed, block_ids, fresh_scales = together(
+            (q[1], order, pos, changed, block_ids, fresh_scales)
+        )
+        plan = fresh_order(changed, block_ids, fresh_scales)
+
+        p.append(grid.hop(p[1]))
+        q.append(grid.hop(q[1]))
+        q[2], act_old, plan = together((q[2], act_old, plan))
+
+        p.append(grid.hop(p[2]))
+        q.append(grid.hop(q[2]))
         keep_old, send_old = old(act_old, order)
-        f3, b3, keep_old, send_old = together((f3, b3, keep_old, send_old))
-
-        f4 = grid.ahead(f3)
+        p[3], q[3], keep_old, send_old = together((p[3], q[3], keep_old, send_old))
+
+        p.append(grid.hop(p[3]))
         got_old = grid.other_core(send_old)
-        cores += [grid.other_core(piece) for piece in (f2, b2, f3, b3)]
-        far_old = add_rows(4 * unit, 8 * unit, keep_old, got_old)
-        f4, cores, far_old = together((f4, cores, far_old))
-
-        cut = 2 * (col_blocks // 3) * BLK
-        first_old = grid.other_y(far_old[:, :cut])
-        pieces = [x, f1, b1, f2, b2, f3, b3, f4] + cores + [grid.other_core(f4)]
-        (keep_c, send_c), (keep_d, send_d) = fresh(pieces, pos, plan)
-        first_old, send_c, send_d = together((first_old, send_c, send_d))
-
-        rest_old = grid.other_y(far_old[:, cut:])
-        got_c, got_d = grid.other_core(send_c), grid.other_core(send_d)
-        far_c = add_rows(4 * unit, 8 * unit, keep_c, got_c)
-        far_d = add_rows(4 * unit, 8 * unit, keep_d, got_d)
-        rest_old, far_c, far_d = together((rest_old, far_c, far_d))
-
-        old_terms = [keep_old, got_old, jnp.concatenate([first_old, rest_old], axis=1)]
-        far_c = grid.other_y(far_c)
-        near_old = grid.near_z(add_rows(2 * unit, 4 * unit, *old_terms))
-        far_c, near_old, far_d = together((far_c, near_old, far_d))
-
-        old_terms = [term[: 2 * unit] for term in old_terms] + [near_old]
-        c_terms = [keep_c, got_c, far_c]
-        far_d = grid.other_y(far_d)
-        near_c = grid.near_z(add_rows(2 * unit, 4 * unit, *c_terms))
-        end_old = grid.far_z(add_rows(unit, 2 * unit, *old_terms))
-        far_d, near_c, end_old = together((far_d, near_c, end_old))
-
-        c_terms = [term[: 2 * unit] for term in c_terms] + [near_c]
-        d_terms = [keep_d, got_d, far_d]
-        near_d = grid.near_z(add_rows(2 * unit, 4 * unit, *d_terms))
-        end_c = grid.far_z(add_rows(unit, 2 * unit, *c_terms))
-        near_d, end_c = together((near_d, end_c))
-
-        d_terms = [term[: 2 * unit] for term in d_terms] + [near_d]
-        end_d = grid.far_z(add_rows(unit, 2 * unit, *d_terms))
-        out_old = add_rows(0, unit, *old_terms, end_old)
-        out_c = add_rows(0, unit, *c_terms, end_c)
-        out_d = add_rows(0, unit, *d_terms, end_d)
-        return jnp.stack([out_old, jnp.concatenate([out_c, out_d], axis=1)])
+        pieces = [p[0], q[0]]
+        for k in (1, 2, 3):
+            pieces += [p[k], q[k], grid.other_core(p[k]), grid.other_core(q[k])]
+
+        cut = cols // 2 // BLK * BLK
+        rows_y = add_cols(4 * unit, 8 * unit, 0, cut, keep_old, got_old)
+        rows_z = jnp.concatenate(
+            [add_cols(first, first + 2 * unit, cut, cols, keep_old, got_old) for first in (2 * unit, 6 * unit)]
+        )
+        p[4], pieces, rows_y, rows_z = together((p[4], pieces, rows_y, rows_z))
+        pieces += [p[4], grid.other_core(p[4])]
+
+        old_y = grid.other_y(rows_y)
+        old_z = grid.near_z(rows_z)
+        halves = fresh(pieces, pos, plan)
+        old_y, old_z, halves = together((old_y, old_z, halves))
+
+        terms = [[keep, grid.other_core(send)] for keep, send in halves]
+        for term in terms:
+            term.append(grid.other_y(add_rows(4 * unit, 8 * unit, *term)))
+        y_terms = [keep_old[: 4 * unit, :cut], got_old[: 4 * unit, :cut], old_y]
+        z_terms = [
+            jnp.concatenate([term[: 2 * unit, cut:], term[4 * unit : 6 * unit, cut:]]) for term in (keep_old, got_old)
+        ] + [old_z]
+        near_y = grid.near_z(add_rows(2 * unit, 4 * unit, *y_terms))
+        far_z = jnp.concatenate([add_rows(first, first + unit, *z_terms) for first in (unit, 3 * unit)])
+        far_z = grid.far_z(far_z)
+        terms[0][2], near_y, far_z = together((terms[0][2], near_y, far_z))
+
+        y_terms = [term[: 2 * unit] for term in y_terms] + [near_y]
+        z_terms = [jnp.concatenate([term[:unit], term[2 * unit : 3 * unit]]) for term in z_terms] + [far_z]
+        end_y = grid.far_z(add_rows(unit, 2 * unit, *y_terms))
+        end_z = grid.other_y(add_rows(unit, 2 * unit, *z_terms))
+        ends = {}
+        parts = len(terms)
+        for phase in range(parts + 1):
+            moving = {}
+            if phase < parts:
+                moving["near"] = grid.near_z(add_rows(2 * unit, 4 * unit, *terms[phase]))
+            if phase >= 1:
+                last = [term[: 2 * unit] for term in terms[phase - 1]]
+                moving["end"] = grid.far_z(add_rows(unit, 2 * unit, *last))
+            if phase + 1 < parts:
+                moving["y"] = terms[phase + 1][2]
+            if phase == 0:
+                moving["old"] = (end_y, end_z)
+            moving = together(moving)
+            if phase < parts:
+                terms[phase].append(moving["near"])
+            if phase >= 1:
+                ends[phase - 1] = moving["end"]
+            if phase + 1 < parts:
+                terms[phase + 1][2] = moving["y"]
+            if phase == 0:
+                end_y, end_z = moving["old"]
+        old_out = [add_rows(0, unit, *y_terms, end_y), add_rows(0, unit, *z_terms, end_z)]
+        new_out = [add_rows(0, unit, *terms[i], ends[i]) for i in range(parts)]
+        return jnp.stack([jnp.concatenate(old_out, axis=1), jnp.concatenate(new_out, axis=1)])
 
     group = experts * learners
     straight = jnp.arange(group, dtype=jnp.int32)
@@ -414,7 +438,7 @@
         return jnp.concatenate(chunks, axis=0)
 
     at_once = min(group, 16)
-    plan = fresh_order(changed, block_ids)
+    plan = fresh_order(changed, block_ids, fresh_scales)
     results = [combine(old_part(0))]
     for step in range(1, step_count):
         total = fresh_part(step)

time: 127 us -> 120 us (0.945)
  waiting for transfers between devices: 57 us -> 42.4 us
  starting transfers between devices: 34 us -> 41.7 us
    ppermute x21 -> x27, waiting for transfers between devices: 41.8 us -> 34.3 us  [partner(): return lax.ppermute(x, 'expert', [(i, i ^ delta) for i in range(self.SIZE)])]
    ppermute x7, waiting for transfers between devices: 15.1 us -> 8.1 us  [hop(): return lax.ppermute(x, 'expert', self.ring)]
    ppermute x7, starting transfers between devices: 10.7 us -> 17.3 us  [hop(): return lax.ppermute(x, 'expert', self.ring)]
    ppermute x21 -> x27, starting transfers between devices: 17 us -> 20.4 us  [partner(): return lax.ppermute(x, 'expert', [(i, i ^ delta) for i in range(self.SIZE)])]
    all_to_all x1, starting transfers between devices: 6.3 us -> 3.91 us  [body(): lax.all_to_all(spread_old, 'expert', split_axis=0, concat_axis=0, tiled=T...]
  transfers between devices with their start and end apart: 29 -> 35, of which waited for: 18 -> 19; matrix products, arithmetic and copies ran while one was open for 5% -> 6% of each run, Pallas kernels for 18% -> 20%
where the time goes in v3:
time: 120 us
  waiting for transfers between devices  42.4 us (35%)
  starting transfers between devices  41.7 us (35%)
  Pallas kernels  23.7 us (20%)
  other arithmetic  6.04 us (5%)
  local copies, waits for them, and re-layouts  3.57 us (3%)
    ppermute x27, waiting for transfers between devices, partner(): return lax.ppermute(x, 'expert', [(i, i ^ delta) for i in range(self.SIZE)])  34.3 us
    ppermute x27, starting transfers between devices, partner(): return lax.ppermute(x, 'expert', [(i, i ^ delta) for i in range(self.SIZE)])  20.4 us
    ppermute x7, starting transfers between devices, hop(): return lax.ppermute(x, 'expert', self.ring)  17.3 us
    pallas_call x1, Pallas kernels, fresh_product(): pl.pallas_call(functools.partial(fresh_kernel, n_pieces, experts, row_cou...  15.9 us
    ppermute x7, waiting for transfers between devices, hop(): return lax.ppermute(x, 'expert', self.ring)  8.1 us
    pallas_call x1, Pallas kernels, old_product(): pl.pallas_call(old_kernel, grid_spec=pltpu.PrefetchScalarGridSpec(num_sca...  7.88 us
    all_to_all x1, starting transfers between devices, body(): lax.all_to_all(spread_old, 'expert', split_axis=0, concat_axis=0, tiled=T...  3.91 us
  transfers between devices with their start and end apart: 35, of which 19 were waited for; matrix products, arithmetic and copies ran while one was open for 6% of the time, Pallas kernels for 20%

profile of v3, /device:TPU:0, one launch (start us, length us, event | category | flops | bytes accessed | tf_op | source)
XLA Modules:
  0.0 119.6 jit_solution(12844697001013626918)
XLA Ops:
  3.5 2.6 %collective-permute-start = (bf16[144,1024]{1,0:T(8,128)(2,1)S(1)}, bf16[144,1024]{1,0:T(8,128)(2,1)S(1)}, u32[]{:S(2)}, u32[]{:S(2)}) collective-permute-start(bf16[144,1024]{1,0:T(8,128)(2,1)S(1)} %fusion.2.refs_0_), channel_id=1, source_target_pairs={{0,4},{1,3},{2,0},{3,7},{4,8},{5,1},{6,2},{7,11},{8,12},{9,5},{10,... | collective-permute-start | bytes 884744 | tf_op jit(solution)/shard_map/ppermute | solution.py:244
  7.5 1.6 %collective-permute-start.4 = (bf16[144,1024]{1,0:T(8,128)(2,1)S(1)}, bf16[144,1024]{1,0:T(8,128)(2,1)S(1)}, u32[]{:S(2)}, u32[]{:S(2)}) collective-permute-start(bf16[144,1024]{1,0:T(8,128)(2,1)S(1)} %collective-permute-done.3.refs_1_), channel_id=1, source_target_pairs={{0,4},{1,3},{2,0},{3,7},{4,8},{5,1},{6,2},{7,11},{8,12},{9,5},{10,... | collective-permute-start | bytes 884744 | tf_op jit(solution)/shard_map/ppermute | solution.py:244
  9.8 3.9 %all-to-all-start = ((bf16[16,16,1024]{2,1,0:T(8,128)(2,1)}), bf16[16,16,1024]{2,1,0:T(8,128)(2,1)S(1)}, u32[]{:S(2)}, u32[]{:S(2)}) async-start(bf16[16,16,1024]{2,1,0:T(8,128)(2,1)} %bitcast.2), calls=%async_computation | async-start | bytes 1048576 | tf_op jit(solution)/shard_map/all_to_all | solution.py:334
  13.7 2.0 %collective-permute-start.1 = (bf16[144,1024]{1,0:T(8,128)(2,1)S(1)}, bf16[144,1024]{1,0:T(8,128)(2,1)S(1)}, u32[]{:S(2)}, u32[]{:S(2)}) collective-permute-start(bf16[144,1024]{1,0:T(8,128)(2,1)S(1)} %collective-permute-done.refs_2_), channel_id=1, source_target_pairs={{0,4},{1,3},{2,0},{3,7},{4,8},{5,1},{6,2},{7,11},{8,12},{9,5},{10,... | collective-permute-start | bytes 884744 | tf_op jit(solution)/shard_map/ppermute | solution.py:244
  21.0 5.4 %collective-permute-done.1.refs_6_ = bf16[144,1024]{1,0:T(8,128)(2,1)S(1)} collective-permute-done((bf16[144,1024]{1,0:T(8,128)(2,1)S(1)}, bf16[144,1024]{1,0:T(8,128)(2,1)S(1)}, u32[]{:S(2)}, u32[]{:S(2)}) %collective-permute-start.1) | collective-permute-done | bytes 294944 | tf_op jit(solution)/shard_map/ppermute | solution.py:244
  26.4 4.5 %collective-permute-start.2 = (bf16[144,1024]{1,0:T(8,128)(2,1)S(1)}, bf16[144,1024]{1,0:T(8,128)(2,1)S(1)}, u32[]{:S(2)}, u32[]{:S(2)}) collective-permute-start(bf16[144,1024]{1,0:T(8,128)(2,1)S(1)} %collective-permute-done.1.refs_6_), channel_id=1, source_target_pairs={{0,4},{1,3},{2,0},{3,7},{4,8},{5,1},{6,2},{7,11},{8,12},{9,5},{10,... | collective-permute-start | bytes 884744 | tf_op jit(solution)/shard_map/ppermute | solution.py:244
  31.3 2.7 %collective-permute-start.6 = (bf16[144,1024]{1,0:T(8,128)(2,1)S(1)}, bf16[144,1024]{1,0:T(8,128)(2,1)S(1)}, u32[]{:S(2)}, u32[]{:S(2)}) collective-permute-start(bf16[144,1024]{1,0:T(8,128)(2,1)S(1)} %collective-permute-done.5.refs_7_), channel_id=1, source_target_pairs={{0,4},{1,3},{2,0},{3,7},{4,8},{5,1},{6,2},{7,11},{8,12},{9,5},{10,... | collective-permute-start | bytes 884744 | tf_op jit(solution)/shard_map/ppermute | solution.py:244
  34.1 7.9 %old_product.1 = (bf16[128,7168]{1,0:T(8,128)(2,1)S(1)}, bf16[128,7168]{1,0:T(8,128)(2,1)S(1)}) custom-call(s32[16]{0:T(128)S(1)} %get-tuple-element.88.order_ref, f32[448]{0:T(512)S(1)} %reshape_squeeze.7.scale_ref, bf16[16,16,1024]{2,1,0:T(8,128)(2,1)S(1)} %all-to-all-done.act_ref, bf16[1024,7168]{1,0:T(8,128)(2,1)} %bitcast.17), custom_call_target="tpu_custom_call" | custom-call | tf_op jit(solution)/shard_map/old_product/pallas_call | solution.py:69
  43.2 2.7 %collective-permute-done.7 = bf16[128,7168]{1,0:T(8,128)(2,1)S(1)} collective-permute-done((bf16[128,7168]{1,0:T(8,128)(2,1)S(1)}, bf16[128,7168]{1,0:T(8,128)(2,1)S(1)}, u32[]{:S(2)}, u32[]{:S(2)}) %collective-permute-start.7) | collective-permute-done | bytes 1835040 | tf_op jit(solution)/shard_map/ppermute | solution.py:241
  46.3 2.5 %collective-permute-start.8 = (bf16[144,1024]{1,0:T(8,128)(2,1)S(1)}, bf16[144,1024]{1,0:T(8,128)(2,1)S(1)}, u32[]{:S(2)}, u32[]{:S(2)}) collective-permute-start(bf16[144,1024]{1,0:T(8,128)(2,1)S(1)} %collective-permute-done.2.refs_10_), channel_id=1, source_target_pairs={{0,4},{1,3},{2,0},{3,7},{4,8},{5,1},{6,2},{7,11},{8,12},{9,5},{10,... | collective-permute-start | bytes 884744 | tf_op jit(solution)/shard_map/ppermute | solution.py:244
  48.8 1.5 %collective-permute-done.14.refs_13_ = bf16[144,1024]{1,0:T(8,128)(2,1)S(1)} collective-permute-done((bf16[144,1024]{1,0:T(8,128)(2,1)S(1)}, bf16[144,1024]{1,0:T(8,128)(2,1)S(1)}, u32[]{:S(2)}, u32[]{:S(2)}) %collective-permute-start.14) | collective-permute-done | bytes 294944 | tf_op jit(solution)/shard_map/ppermute | solution.py:241
  50.3 2.7 %collective-permute-done.8.refs_14_ = bf16[144,1024]{1,0:T(8,128)(2,1)S(1)} collective-permute-done((bf16[144,1024]{1,0:T(8,128)(2,1)S(1)}, bf16[144,1024]{1,0:T(8,128)(2,1)S(1)}, u32[]{:S(2)}, u32[]{:S(2)}) %collective-permute-start.8) | collective-permute-done | bytes 294944 | tf_op jit(solution)/shard_map/ppermute | solution.py:244
  53.0 1.5 %collective-permute-start.15 = (bf16[64,3584]{1,0:T(8,128)(2,1)S(1)}, bf16[64,3584]{1,0:T(8,128)(2,1)S(1)}, u32[]{:S(2)}, u32[]{:S(2)}) collective-permute-start(bf16[64,3584]{1,0:T(8,128)(2,1)S(1)} %add_convert_fusion), channel_id=1, source_target_pairs={{0,2},{1,3},{2,0},{3,1},{4,6},{5,7},{6,4},{7,5},{8,10},{9,11},{10,... | collective-permute-start | bytes 1376264 | tf_op jit(solution)/shard_map/ppermute | solution.py:241
  54.5 2.0 %collective-permute-start.16 = (bf16[64,3584]{1,0:T(8,128)(2,1)S(1)}, bf16[64,3584]{1,0:T(8,128)(2,1)S(1)}, u32[]{:S(2)}, u32[]{:S(2)}) collective-permute-start(bf16[64,3584]{1,0:T(8,128)(2,1)S(1)} %pad_maximum_fusion), channel_id=1, source_target_pairs={{0,4},{1,5},{2,6},{3,7},{4,0},{5,1},{6,2},{7,3},{8,12},{9,13},{10,... | collective-permute-start | bytes 1376264 | tf_op jit(solution)/shard_map/ppermute | solution.py:241
  56.6 1.6 %collective-permute-done.17.refs_15_ = bf16[144,1024]{1,0:T(8,128)(2,1)S(1)} collective-permute-done((bf16[144,1024]{1,0:T(8,128)(2,1)S(1)}, bf16[144,1024]{1,0:T(8,128)(2,1)S(1)}, u32[]{:S(2)}, u32[]{:S(2)}) %collective-permute-start.17) | collective-permute-done | bytes 294944 | tf_op jit(solution)/shard_map/ppermute | solution.py:241
  58.1 15.9 %fresh_product.1 = (bf16[128,2560]{1,0:T(8,128)(2,1)S(1)}, bf16[128,2560]{1,0:T(8,128)(2,1)S(1)}, bf16[128,2304]{1,0:T(8,128)(2,1)S(1)}, bf16[128,2304]{1,0:T(8,...) custom-call(s32[16]{0:T(128)S(1)} %get-tuple-element.98.pos_ref, s32[1]{0:T(128)S(6)} %select_n.93.steps_ref, ...), custom_call_target="tpu_custom_call" | custom-call | tf_op jit(solution)/shard_map/fresh_product/pallas_call | solution.py:154
  79.9 7.2 %collective-permute-done.21 = bf16[32,3584]{1,0:T(8,128)(2,1)S(1)} collective-permute-done((bf16[32,3584]{1,0:T(8,128)(2,1)S(1)}, bf16[32,3584]{1,0:T(8,128)(2,1)S(1)}, u32[]{:S(2)}, u32[]{:S(2)}) %collective-permute-start.21) | collective-permute-done | bytes 229408 | tf_op jit(solution)/shard_map/ppermute | solution.py:241
  90.1 1.5 %collective-permute-start.23 = (bf16[16,3584]{1,0:T(8,128)(2,1)S(1)}, bf16[16,3584]{1,0:T(8,128)(2,1)S(1)}, u32[]{:S(2)}, u32[]{:S(2)}) collective-permute-start(bf16[16,3584]{1,0:T(8,128)(2,1)S(1)} %get-tuple-element.152), channel_id=1, source_target_pairs={{0,8},{1,9},{2,10},{3,11},{4,12},{5,13},{6,14},{7,15},{8,0},{9,1},... | collective-permute-start | bytes 344072 | tf_op jit(solution)/shard_map/ppermute | solution.py:241
  93.0 1.6 %collective-permute-done.26 = bf16[64,2304]{1,0:T(8,128)(2,1)S(1)} collective-permute-done((bf16[64,2304]{1,0:T(8,128)(2,1)S(1)}, bf16[64,2304]{1,0:T(8,128)(2,1)S(1)}, u32[]{:S(2)}, u32[]{:S(2)}) %collective-permute-start.26) | collective-permute-done | bytes 294944 | tf_op jit(solution)/shard_map/ppermute | solution.py:241
  94.6 2.5 %collective-permute-done.24 = bf16[16,3584]{1,0:T(8,128)(2,1)S(1)} collective-permute-done((bf16[16,3584]{1,0:T(8,128)(2,1)S(1)}, bf16[16,3584]{1,0:T(8,128)(2,1)S(1)}, u32[]{:S(2)}, u32[]{:S(2)}) %collective-permute-start.24) | collective-permute-done | bytes 114720 | tf_op jit(solution)/shard_map/ppermute | solution.py:241
  100.4 2.2 %collective-permute-done.30 = bf16[64,2304]{1,0:T(8,128)(2,1)S(1)} collective-permute-done((bf16[64,2304]{1,0:T(8,128)(2,1)S(1)}, bf16[64,2304]{1,0:T(8,128)(2,1)S(1)}, u32[]{:S(2)}, u32[]{:S(2)}) %collective-permute-start.30) | collective-permute-done | bytes 294944 | tf_op jit(solution)/shard_map/ppermute | solution.py:241
  107.5 3.4 %collective-permute-done.31 = bf16[16,2304]{1,0:T(8,128)(2,1)S(1)} collective-permute-done((bf16[16,2304]{1,0:T(8,128)(2,1)S(1)}, bf16[16,2304]{1,0:T(8,128)(2,1)S(1)}, u32[]{:S(2)}, u32[]{:S(2)}) %collective-permute-start.31) | collective-permute-done | bytes 73760 | tf_op jit(solution)/shard_map/ppermute | solution.py:241
  110.9 1.6 %collective-permute-done.32 = bf16[32,2304]{1,0:T(8,128)(2,1)S(1)} collective-permute-done((bf16[32,2304]{1,0:T(8,128)(2,1)S(1)}, bf16[32,2304]{1,0:T(8,128)(2,1)S(1)}, u32[]{:S(2)}, u32[]{:S(2)}) %collective-permute-start.32) | collective-permute-done | bytes 147488 | tf_op jit(solution)/shard_map/ppermute | solution.py:241
  113.9 4.8 %collective-permute-done.33 = bf16[16,2304]{1,0:T(8,128)(2,1)S(1)} collective-permute-done((bf16[16,2304]{1,0:T(8,128)(2,1)S(1)}, bf16[16,2304]{1,0:T(8,128)(2,1)S(1)}, u32[]{:S(2)}, u32[]{:S(2)}) %collective-permute-start.33) | collective-permute-done | bytes 73760 | tf_op jit(solution)/shard_map/ppermute | solution.py:241
  (123 shorter events, 32.9 us)
Async XLA Ops:
  3.5 10.2 %collective-permute-start = (bf16[144,1024]{1,0:T(8,128)(2,1)S(1)}, bf16[144,1024]{1,0:T(8,128)(2,1)S(1)}, u32[]{:S(2)}, u32[]{:S(2)}) collective-permute-start(bf16[144,1024]{1,0:T(8,128)(2,1)S(1)} %fusion.2.refs_0_), channel_id=1, source_target_pairs={{0,4},{1,3},{2,0},{3,7},{4,8},{5,1},{6,2},{7,11},{8,12},{9,5},{10,... | collective-permute-start | bytes 884744 | tf_op jit(solution)/shard_map/ppermute | solution.py:244
  7.5 8.2 %collective-permute-start.4 = (bf16[144,1024]{1,0:T(8,128)(2,1)S(1)}, bf16[144,1024]{1,0:T(8,128)(2,1)S(1)}, u32[]{:S(2)}, u32[]{:S(2)}) collective-permute-start(bf16[144,1024]{1,0:T(8,128)(2,1)S(1)} %collective-permute-done.3.refs_1_), channel_id=1, source_target_pairs={{0,4},{1,3},{2,0},{3,7},{4,8},{5,1},{6,2},{7,11},{8,12},{9,5},{10,... | collective-permute-start | bytes 884744 | tf_op jit(solution)/shard_map/ppermute | solution.py:244
  9.8 21.6 %all-to-all-start = ((bf16[16,16,1024]{2,1,0:T(8,128)(2,1)}), bf16[16,16,1024]{2,1,0:T(8,128)(2,1)S(1)}, u32[]{:S(2)}, u32[]{:S(2)}) async-start(bf16[16,16,1024]{2,1,0:T(8,128)(2,1)} %bitcast.2), calls=%async_computation | async-start | bytes 1048576 | tf_op jit(solution)/shard_map/all_to_all | solution.py:334
  13.7 12.7 %collective-permute-start.1 = (bf16[144,1024]{1,0:T(8,128)(2,1)S(1)}, bf16[144,1024]{1,0:T(8,128)(2,1)S(1)}, u32[]{:S(2)}, u32[]{:S(2)}) collective-permute-start(bf16[144,1024]{1,0:T(8,128)(2,1)S(1)} %collective-permute-done.refs_2_), channel_id=1, source_target_pairs={{0,4},{1,3},{2,0},{3,7},{4,8},{5,1},{6,2},{7,11},{8,12},{9,5},{10,... | collective-permute-start | bytes 884744 | tf_op jit(solution)/shard_map/ppermute | solution.py:244
  19.4 11.9 %collective-permute-start.5 = (bf16[144,1024]{1,0:T(8,128)(2,1)S(1)}, bf16[144,1024]{1,0:T(8,128)(2,1)S(1)}, u32[]{:S(2)}, u32[]{:S(2)}) collective-permute-start(bf16[144,1024]{1,0:T(8,128)(2,1)S(1)} %collective-permute-done.4.refs_3_), channel_id=1, source_target_pairs={{0,4},{1,3},{2,0},{3,7},{4,8},{5,1},{6,2},{7,11},{8,12},{9,5},{10,... | collective-permute-start | bytes 884744 | tf_op jit(solution)/shard_map/ppermute | solution.py:244
  26.4 15.6 %collective-permute-start.2 = (bf16[144,1024]{1,0:T(8,128)(2,1)S(1)}, bf16[144,1024]{1,0:T(8,128)(2,1)S(1)}, u32[]{:S(2)}, u32[]{:S(2)}) collective-permute-start(bf16[144,1024]{1,0:T(8,128)(2,1)S(1)} %collective-permute-done.1.refs_6_), channel_id=1, source_target_pairs={{0,4},{1,3},{2,0},{3,7},{4,8},{5,1},{6,2},{7,11},{8,12},{9,5},{10,... | collective-permute-start | bytes 884744 | tf_op jit(solution)/shard_map/ppermute | solution.py:244
  31.3 10.7 %collective-permute-start.6 = (bf16[144,1024]{1,0:T(8,128)(2,1)S(1)}, bf16[144,1024]{1,0:T(8,128)(2,1)S(1)}, u32[]{:S(2)}, u32[]{:S(2)}) collective-permute-start(bf16[144,1024]{1,0:T(8,128)(2,1)S(1)} %collective-permute-done.5.refs_7_), channel_id=1, source_target_pairs={{0,4},{1,3},{2,0},{3,7},{4,8},{5,1},{6,2},{7,11},{8,12},{9,5},{10,... | collective-permute-start | bytes 884744 | tf_op jit(solution)/shard_map/ppermute | solution.py:244
  42.6 6.2 %collective-permute-start.10 = (bf16[144,1024]{1,0:T(8,128)(2,1)S(1)}, bf16[144,1024]{1,0:T(8,128)(2,1)S(1)}, u32[]{:S(2)}, u32[]{:S(2)}) collective-permute-start(bf16[144,1024]{1,0:T(8,128)(2,1)S(1)} %collective-permute-done.4.refs_3_), channel_id=1, source_target_pairs={{0,1},{1,0},{2,3},{3,2},{4,5},{5,4},{6,7},{7,6},{8,9},{9,8},{10,11... | collective-permute-start | bytes 884744 | tf_op jit(solution)/shard_map/ppermute | solution.py:241
  42.7 6.1 %collective-permute-start.11 = (bf16[144,1024]{1,0:T(8,128)(2,1)S(1)}, bf16[144,1024]{1,0:T(8,128)(2,1)S(1)}, u32[]{:S(2)}, u32[]{:S(2)}) collective-permute-start(bf16[144,1024]{1,0:T(8,128)(2,1)S(1)} %collective-permute-done.1.refs_6_), channel_id=1, source_target_pairs={{0,1},{1,0},{2,3},{3,2},{4,5},{5,4},{6,7},{7,6},{8,9},{9,8},{10,11... | collective-permute-start | bytes 884744 | tf_op jit(solution)/shard_map/ppermute | solution.py:241
  46.3 6.7 %collective-permute-start.8 = (bf16[144,1024]{1,0:T(8,128)(2,1)S(1)}, bf16[144,1024]{1,0:T(8,128)(2,1)S(1)}, u32[]{:S(2)}, u32[]{:S(2)}) collective-permute-start(bf16[144,1024]{1,0:T(8,128)(2,1)S(1)} %collective-permute-done.2.refs_10_), channel_id=1, source_target_pairs={{0,4},{1,3},{2,0},{3,7},{4,8},{5,1},{6,2},{7,11},{8,12},{9,5},{10,... | collective-permute-start | bytes 884744 | tf_op jit(solution)/shard_map/ppermute | solution.py:244
  53.0 21.0 %collective-permute-start.15 = (bf16[64,3584]{1,0:T(8,128)(2,1)S(1)}, bf16[64,3584]{1,0:T(8,128)(2,1)S(1)}, u32[]{:S(2)}, u32[]{:S(2)}) collective-permute-start(bf16[64,3584]{1,0:T(8,128)(2,1)S(1)} %add_convert_fusion), channel_id=1, source_target_pairs={{0,2},{1,3},{2,0},{3,1},{4,6},{5,7},{6,4},{7,5},{8,10},{9,11},{10,... | collective-permute-start | bytes 1376264 | tf_op jit(solution)/shard_map/ppermute | solution.py:241
  54.5 19.5 %collective-permute-start.16 = (bf16[64,3584]{1,0:T(8,128)(2,1)S(1)}, bf16[64,3584]{1,0:T(8,128)(2,1)S(1)}, u32[]{:S(2)}, u32[]{:S(2)}) collective-permute-start(bf16[64,3584]{1,0:T(8,128)(2,1)S(1)} %pad_maximum_fusion), channel_id=1, source_target_pairs={{0,4},{1,5},{2,6},{3,7},{4,0},{5,1},{6,2},{7,3},{8,12},{9,13},{10,... | collective-permute-start | bytes 1376264 | tf_op jit(solution)/shard_map/ppermute | solution.py:241
  74.1 12.9 %collective-permute-start.21 = (bf16[32,3584]{1,0:T(8,128)(2,1)S(1)}, bf16[32,3584]{1,0:T(8,128)(2,1)S(1)}, u32[]{:S(2)}, u32[]{:S(2)}) collective-permute-start(bf16[32,3584]{1,0:T(8,128)(2,1)S(1)} %pad_maximum_fusion.2), channel_id=1, source_target_pairs={{0,8},{1,9},{2,10},{3,11},{4,12},{5,13},{6,14},{7,15},{8,0},{9,1},... | collective-permute-start | bytes 688136 | tf_op jit(solution)/shard_map/ppermute | solution.py:241
  75.5 12.8 %collective-permute-start.20 = (bf16[32,3584]{1,0:T(8,128)(2,1)S(1)}, bf16[32,3584]{1,0:T(8,128)(2,1)S(1)}, u32[]{:S(2)}, u32[]{:S(2)}) collective-permute-start(bf16[32,3584]{1,0:T(8,128)(2,1)S(1)} %add_convert_fusion.4), channel_id=1, source_target_pairs={{0,4},{1,5},{2,6},{3,7},{4,0},{5,1},{6,2},{7,3},{8,12},{9,13},{10,... | collective-permute-start | bytes 688136 | tf_op jit(solution)/shard_map/ppermute | solution.py:241
  77.1 14.5 %collective-permute-start.29 = (bf16[128,2304]{1,0:T(8,128)(2,1)S(1)}, bf16[128,2304]{1,0:T(8,128)(2,1)S(1)}, u32[]{:S(2)}, u32[]{:S(2)}) collective-permute-start(bf16[128,2304]{1,0:T(8,128)(2,1)S(1)} %get-tuple-element.139), channel_id=1, source_target_pairs={{0,1},{1,0},{2,3},{3,2},{4,5},{5,4},{6,7},{7,6},{8,9},{9,8},{10,11... | collective-permute-start | bytes 1769480 | tf_op jit(solution)/shard_map/ppermute | solution.py:241
  77.6 10.7 %collective-permute-start.19 = (bf16[64,2560]{1,0:T(8,128)(2,1)S(1)}, bf16[64,2560]{1,0:T(8,128)(2,1)S(1)}, u32[]{:S(2)}, u32[]{:S(2)}) collective-permute-start(bf16[64,2560]{1,0:T(8,128)(2,1)S(1)} %add_convert_fusion.1), channel_id=1, source_target_pairs={{0,2},{1,3},{2,0},{3,1},{4,6},{5,7},{6,4},{7,5},{8,10},{9,11},{10,... | collective-permute-start | bytes 983048 | tf_op jit(solution)/shard_map/ppermute | solution.py:241
  79.0 15.6 %collective-permute-start.26 = (bf16[64,2304]{1,0:T(8,128)(2,1)S(1)}, bf16[64,2304]{1,0:T(8,128)(2,1)S(1)}, u32[]{:S(2)}, u32[]{:S(2)}) collective-permute-start(bf16[64,2304]{1,0:T(8,128)(2,1)S(1)} %add_convert_fusion.3), channel_id=1, source_target_pairs={{0,2},{1,3},{2,0},{3,1},{4,6},{5,7},{6,4},{7,5},{8,10},{9,11},{10,... | collective-permute-start | bytes 884744 | tf_op jit(solution)/shard_map/ppermute | solution.py:241
  88.4 9.1 %collective-permute-start.22 = (bf16[32,2560]{1,0:T(8,128)(2,1)S(1)}, bf16[32,2560]{1,0:T(8,128)(2,1)S(1)}, u32[]{:S(2)}, u32[]{:S(2)}) collective-permute-start(bf16[32,2560]{1,0:T(8,128)(2,1)S(1)} %add_convert_fusion.7), channel_id=1, source_target_pairs={{0,4},{1,5},{2,6},{3,7},{4,0},{5,1},{6,2},{7,3},{8,12},{9,13},{10,... | collective-permute-start | bytes 491528 | tf_op jit(solution)/shard_map/ppermute | solution.py:241
  89.8 7.2 %collective-permute-start.24 = (bf16[16,3584]{1,0:T(8,128)(2,1)S(1)}, bf16[16,3584]{1,0:T(8,128)(2,1)S(1)}, u32[]{:S(2)}, u32[]{:S(2)}) collective-permute-start(bf16[16,3584]{1,0:T(8,128)(2,1)S(1)} %get-tuple-element.151), channel_id=1, source_target_pairs={{0,2},{1,3},{2,0},{3,1},{4,6},{5,7},{6,4},{7,5},{8,10},{9,11},{10,... | collective-permute-start | bytes 344072 | tf_op jit(solution)/shard_map/ppermute | solution.py:241
  90.1 7.4 %collective-permute-start.23 = (bf16[16,3584]{1,0:T(8,128)(2,1)S(1)}, bf16[16,3584]{1,0:T(8,128)(2,1)S(1)}, u32[]{:S(2)}, u32[]{:S(2)}) collective-permute-start(bf16[16,3584]{1,0:T(8,128)(2,1)S(1)} %get-tuple-element.152), channel_id=1, source_target_pairs={{0,8},{1,9},{2,10},{3,11},{4,12},{5,13},{6,14},{7,15},{8,0},{9,1},... | collective-permute-start | bytes 344072 | tf_op jit(solution)/shard_map/ppermute | solution.py:241
  91.7 10.8 %collective-permute-start.30 = (bf16[64,2304]{1,0:T(8,128)(2,1)S(1)}, bf16[64,2304]{1,0:T(8,128)(2,1)S(1)}, u32[]{:S(2)}, u32[]{:S(2)}) collective-permute-start(bf16[64,2304]{1,0:T(8,128)(2,1)S(1)} %add_convert_fusion.2), channel_id=1, source_target_pairs={{0,2},{1,3},{2,0},{3,1},{4,6},{5,7},{6,4},{7,5},{8,10},{9,11},{10,... | collective-permute-start | bytes 884744 | tf_op jit(solution)/shard_map/ppermute | solution.py:241
  97.6 6.4 %collective-permute-start.27 = (bf16[16,2560]{1,0:T(8,128)(2,1)S(1)}, bf16[16,2560]{1,0:T(8,128)(2,1)S(1)}, u32[]{:S(2)}, u32[]{:S(2)}) collective-permute-start(bf16[16,2560]{1,0:T(8,128)(2,1)S(1)} %add_convert_fusion.17), channel_id=1, source_target_pairs={{0,8},{1,9},{2,10},{3,11},{4,12},{5,13},{6,14},{7,15},{8,0},{9,1},... | collective-permute-start | bytes 245768 | tf_op jit(solution)/shard_map/ppermute | solution.py:241
  104.7 6.2 %collective-permute-start.31 = (bf16[16,2304]{1,0:T(8,128)(2,1)S(1)}, bf16[16,2304]{1,0:T(8,128)(2,1)S(1)}, u32[]{:S(2)}, u32[]{:S(2)}) collective-permute-start(bf16[16,2304]{1,0:T(8,128)(2,1)S(1)} %add_convert_fusion.21), channel_id=1, source_target_pairs={{0,8},{1,9},{2,10},{3,11},{4,12},{5,13},{6,14},{7,15},{8,0},{9,1},... | collective-permute-start | bytes 221192 | tf_op jit(solution)/shard_map/ppermute | solution.py:241
  106.0 6.5 %collective-permute-start.32 = (bf16[32,2304]{1,0:T(8,128)(2,1)S(1)}, bf16[32,2304]{1,0:T(8,128)(2,1)S(1)}, u32[]{:S(2)}, u32[]{:S(2)}) collective-permute-start(bf16[32,2304]{1,0:T(8,128)(2,1)S(1)} %add_convert_fusion.8), channel_id=1, source_target_pairs={{0,4},{1,5},{2,6},{3,7},{4,0},{5,1},{6,2},{7,3},{8,12},{9,13},{10,... | collective-permute-start | bytes 442376 | tf_op jit(solution)/shard_map/ppermute | solution.py:241
  (16 other events, 142.3 us)

commit v4 on v3

--- a/solution.py
+++ b/solution.py
@@ -19,6 +19,73 @@
 
 def in_vmem(x):
     return pltpu.with_memory_space_constraint(x, pltpu.VMEM)
+
+
+def in_hbm(x):
+    return pltpu.with_memory_space_constraint(x, pltpu.HBM)
+
+
+def prepare_kernel(experts, act_hbm, route_hbm, gate_hbm, spread_ref, piece_ref, act_ref, route_ref, gate_ref, sems):
+    _, row_count, top_count, width = act_ref.shape
+    routed = row_count * top_count
+    arrivals = [
+        pltpu.make_async_copy(source, here, sems.at[i])
+        for i, (source, here) in enumerate(((act_hbm, act_ref), (route_hbm, route_ref), (gate_hbm, gate_ref)))
+    ]
+    for arrival in arrivals:
+        arrival.start()
+    for arrival in arrivals:
+        arrival.wait()
+    choice = lax.broadcasted_iota(jnp.int32, (top_count, routed), 0)
+    entry = lax.broadcasted_iota(jnp.int32, (top_count, routed), 1)
+
+    def gated(step):
+        rows = [act_ref[step, r].astype(F32) * gate_ref[step][:, r : r + 1] for r in range(row_count)]
+        return jnp.concatenate(rows, axis=0).astype(BF16)
+
+    def route_row(step):
+        routes = route_ref[step].astype(F32)
+        wide = jnp.zeros((top_count, routed), F32)
+        for r in range(row_count):
+            wide = jnp.where(entry // top_count == r, routes[:, r : r + 1], wide)
+        return jnp.sum(jnp.where(entry % top_count == choice, wide, 0.0), axis=0, keepdims=True)
+
+    piece_ref[0:routed, :] = gated(1)
+    piece_ref[routed:, :] = jnp.zeros((PAD_ROWS, width), BF16)
+    top = lax.broadcasted_iota(jnp.int32, (PAD_ROWS, routed), 0) == 0
+    piece_ref[routed:, 0:routed] = jnp.where(top, route_row(1), 0.0).astype(BF16)
+    long_row = lax.broadcasted_iota(jnp.int32, (experts * row_count, routed), 0)
+    long_entry = lax.broadcasted_iota(jnp.int32, (experts * row_count, routed), 1)
+    match = (long_row % row_count == long_entry // top_count) & (
+        (long_row // row_count).astype(F32) == route_row(0)
+    )
+    pick = jnp.where(match, 1.0, 0.0).astype(BF16)
+    spread = jnp.dot(pick, gated(0), preferred_element_type=F32).astype(BF16)
+    for e in range(experts):
+        spread_ref[e] = spread[e * row_count : (e + 1) * row_count]
+
+
+def prepare(hidden_act, routes, gates, experts):
+    _, row_count, top_count, width = hidden_act.shape
+    whole = pl.BlockSpec(memory_space=pltpu.VMEM)
+    return pl.pallas_call(
+        functools.partial(prepare_kernel, experts),
+        in_specs=[pl.BlockSpec(memory_space=pl.ANY)] * 3,
+        out_specs=[whole] * 2,
+        scratch_shapes=[
+            pltpu.VMEM(hidden_act.shape, BF16),
+            pltpu.VMEM((2, top_count, row_count), jnp.int32),
+            pltpu.VMEM((2, top_count, row_count), F32),
+            pltpu.SemaphoreType.DMA((3,)),
+        ],
+        out_shape=[
+            pltpu.VMEM((experts, row_count, width), BF16),
+            pltpu.VMEM((row_count * top_count + PAD_ROWS, width), BF16),
+        ],
+        compiler_params=pltpu.CompilerParams(vmem_limit_bytes=6 * SPARE_VMEM),
+        cost_estimate=pl.CostEstimate(flops=0, bytes_accessed=0, transcendentals=0),
+        name="prepare",
+    )(*[in_hbm(x) for x in (hidden_act, routes.transpose(0, 2, 1), gates.transpose(0, 2, 1))])
 
 
 def old_kernel(order_ref, scale_ref, act_ref, code_hbm, keep_ref, send_ref, act_scratch, code_buf, code_sem):
@@ -83,7 +150,7 @@
         compiler_params=pltpu.CompilerParams(vmem_limit_bytes=2 * (rows + cols) * width + SPARE_VMEM),
         cost_estimate=pl.CostEstimate(flops=0, bytes_accessed=0, transcendentals=0),
         name="old_product",
-    )(order, scales.reshape(-1), in_vmem(act), pltpu.with_memory_space_constraint(codes, pltpu.HBM))
+    )(order, scales.reshape(-1), in_vmem(act), in_hbm(codes))
 
 
 def fresh_kernel(
@@ -326,10 +393,11 @@
         pos = jnp.asarray(grid.piece_rank)[own]
         unit = row_count
 
-        p = [with_routes(1)]
+        spread_old, first_piece = prepare(hidden_act, routes, gates, experts)
+        p = [first_piece]
         p.append(grid.hop(p[0]))
         q = [grid.other_core(p[0])]
-        q[0], spread_old = together((q[0], spread(0)))
+        q[0], spread_old = together((q[0], spread_old))
         q.append(grid.hop(q[0]))
         act_old = lax.all_to_all(spread_old, "expert", split_axis=0, concat_axis=0, tiled=True)
         q[1], order, pos, changed, block_ids, fresh_scales = together(
@@ -357,7 +425,7 @@
         rows_z = jnp.concatenate(
             [add_cols(first, first + 2 * unit, cut, cols, keep_old, got_old) for first in (2 * unit, 6 * unit)]
         )
-        p[4], pieces, rows_y, rows_z = together((p[4], pieces, rows_y, rows_z))
+        pieces, rows_y, rows_z = together((pieces, rows_y, rows_z))
         pieces += [p[4], grid.other_core(p[4])]
 
         old_y = grid.other_y(rows_y)

time: 120 us -> 117 us (0.975)
  waiting for transfers between devices: 42.4 us -> 37.1 us
  Pallas kernels: 23.7 us -> 26 us
    ppermute x7, waiting for transfers between devices: 8.1 us -> 2.67 us  [hop(): return lax.ppermute(x, 'expert', self.ring)]
    pallas_call x0 -> x1, Pallas kernels: none -> 2.31 us  [prepare(): pl.pallas_call(functools.partial(prepare_kernel, experts), in_specs=[pl.B...]
    convert_element_type x1 -> x0, other arithmetic: 1.23 us -> none  [body(): (hidden_act.astype(F32) * gates[..., None]).astype(BF16)]
  transfers between devices with their start and end apart: 35 -> 35, of which waited for: 19 -> 17; matrix products, arithmetic and copies ran while one was open for 6% -> 7% of each run, Pallas kernels for 20% -> 20%
where the time goes in v4:
time: 117 us; the launch traced here: 116 us
  starting transfers between devices  42.9 us (37%)
  waiting for transfers between devices  37.1 us (32%)
  Pallas kernels  26 us (22%)
  other arithmetic  6.86 us (6%)
  local copies, waits for them, and re-layouts  2.42 us (2%)
    ppermute x27, waiting for transfers between devices, partner(): return lax.ppermute(x, 'expert', [(i, i ^ delta) for i in range(self.SIZE)])  34.4 us
    ppermute x27, starting transfers between devices, partner(): return lax.ppermute(x, 'expert', [(i, i ^ delta) for i in range(self.SIZE)])  20.8 us
    ppermute x7, starting transfers between devices, hop(): return lax.ppermute(x, 'expert', self.ring)  17.3 us
    pallas_call x1, Pallas kernels, fresh_product(): pl.pallas_call(functools.partial(fresh_kernel, n_pieces, experts, row_cou...  15.9 us
    pallas_call x1, Pallas kernels, old_product(): pl.pallas_call(old_kernel, grid_spec=pltpu.PrefetchScalarGridSpec(num_sca...  7.87 us
    all_to_all x1, starting transfers between devices, body(): lax.all_to_all(spread_old, 'expert', split_axis=0, concat_axis=0, tiled=T...  4.86 us
    ppermute x7, waiting for transfers between devices, hop(): return lax.ppermute(x, 'expert', self.ring)  2.67 us
  transfers between devices with their start and end apart: 35, of which 17 were waited for; matrix products, arithmetic and copies ran while one was open for 7% of the time, Pallas kernels for 20%

profile of v4, /device:TPU:0, one launch (start us, length us, event | category | flops | bytes accessed | tf_op | source)
XLA Modules:
  0.0 116.4 jit_solution(14127310314940938854)
XLA Ops:
  0.0 2.3 %prepare.1 = (bf16[16,16,1024]{2,1,0:T(8,128)(2,1)}, bf16[144,1024]{1,0:T(8,128)(2,1)S(1)}) custom-call(bf16[2,16,8,1024]{3,2,1,0:T(8,128)(2,1)} %act_hbm.1, s32[2,8,16]{2,1,0:T(8,128)} %bitcast.14, f32[2,8,16]{2,1,0:T(8,128)} %bitcast.15), custom_call_target="tpu_custom_call" | custom-call | tf_op jit(solution)/shard_map/prepare/pallas_call | solution.py:71
  2.8 2.6 %collective-permute-start = (bf16[144,1024]{1,0:T(8,128)(2,1)S(1)}, bf16[144,1024]{1,0:T(8,128)(2,1)S(1)}, u32[]{:S(2)}, u32[]{:S(2)}) collective-permute-start(bf16[144,1024]{1,0:T(8,128)(2,1)S(1)} %get-tuple-element.95.refs_0_), channel_id=1, source_target_pairs={{0,4},{1,3},{2,0},{3,7},{4,8},{5,1},{6,2},{7,11},{8,12},{9,5},{10,... | collective-permute-start | bytes 884744 | tf_op jit(solution)/shard_map/ppermute | solution.py:311
  7.8 4.9 %all-to-all-start = ((bf16[16,16,1024]{2,1,0:T(8,128)(2,1)}), bf16[16,16,1024]{2,1,0:T(8,128)(2,1)S(1)}, u32[]{:S(2)}, u32[]{:S(2)}) async-start(bf16[16,16,1024]{2,1,0:T(8,128)(2,1)} %get-tuple-element.74), calls=%async_computation | async-start | bytes 1048576 | tf_op jit(solution)/shard_map/all_to_all | solution.py:402
  12.7 2.0 %collective-permute-start.1 = (bf16[144,1024]{1,0:T(8,128)(2,1)S(1)}, bf16[144,1024]{1,0:T(8,128)(2,1)S(1)}, u32[]{:S(2)}, u32[]{:S(2)}) collective-permute-start(bf16[144,1024]{1,0:T(8,128)(2,1)S(1)} %collective-permute-done.refs_2_), channel_id=1, source_target_pairs={{0,4},{1,3},{2,0},{3,7},{4,8},{5,1},{6,2},{7,11},{8,12},{9,5},{10,... | collective-permute-start | bytes 884744 | tf_op jit(solution)/shard_map/ppermute | solution.py:311
  22.7 2.7 %collective-permute-done.1.refs_6_ = bf16[144,1024]{1,0:T(8,128)(2,1)S(1)} collective-permute-done((bf16[144,1024]{1,0:T(8,128)(2,1)S(1)}, bf16[144,1024]{1,0:T(8,128)(2,1)S(1)}, u32[]{:S(2)}, u32[]{:S(2)}) %collective-permute-start.1) | collective-permute-done | bytes 294944 | tf_op jit(solution)/shard_map/ppermute | solution.py:311
  25.3 4.5 %collective-permute-start.2 = (bf16[144,1024]{1,0:T(8,128)(2,1)S(1)}, bf16[144,1024]{1,0:T(8,128)(2,1)S(1)}, u32[]{:S(2)}, u32[]{:S(2)}) collective-permute-start(bf16[144,1024]{1,0:T(8,128)(2,1)S(1)} %collective-permute-done.1.refs_6_), channel_id=1, source_target_pairs={{0,4},{1,3},{2,0},{3,7},{4,8},{5,1},{6,2},{7,11},{8,12},{9,5},{10,... | collective-permute-start | bytes 884744 | tf_op jit(solution)/shard_map/ppermute | solution.py:311
  30.3 2.7 %collective-permute-start.6 = (bf16[144,1024]{1,0:T(8,128)(2,1)S(1)}, bf16[144,1024]{1,0:T(8,128)(2,1)S(1)}, u32[]{:S(2)}, u32[]{:S(2)}) collective-permute-start(bf16[144,1024]{1,0:T(8,128)(2,1)S(1)} %collective-permute-done.5.refs_7_), channel_id=1, source_target_pairs={{0,4},{1,3},{2,0},{3,7},{4,8},{5,1},{6,2},{7,11},{8,12},{9,5},{10,... | collective-permute-start | bytes 884744 | tf_op jit(solution)/shard_map/ppermute | solution.py:311
  33.0 7.9 %old_product.1 = (bf16[128,7168]{1,0:T(8,128)(2,1)S(1)}, bf16[128,7168]{1,0:T(8,128)(2,1)S(1)}) custom-call(s32[16]{0:T(128)S(1)} %get-tuple-element.79.order_ref, f32[448]{0:T(512)S(1)} %reshape_squeeze.7.scale_ref, bf16[16,16,1024]{2,1,0:T(8,128)(2,1)S(1)} %all-to-all-done.act_ref, bf16[1024,7168]{1,0:T(8,128)(2,1)} %bitcast.13), custom_call_target="tpu_custom_call" | custom-call | tf_op jit(solution)/shard_map/old_product/pallas_call | solution.py:136
  42.1 2.7 %collective-permute-done.7 = bf16[128,7168]{1,0:T(8,128)(2,1)S(1)} collective-permute-done((bf16[128,7168]{1,0:T(8,128)(2,1)S(1)}, bf16[128,7168]{1,0:T(8,128)(2,1)S(1)}, u32[]{:S(2)}, u32[]{:S(2)}) %collective-permute-start.7) | collective-permute-done | bytes 1835040 | tf_op jit(solution)/shard_map/ppermute | solution.py:308
  44.8 2.5 %collective-permute-start.16 = (bf16[144,1024]{1,0:T(8,128)(2,1)S(1)}, bf16[144,1024]{1,0:T(8,128)(2,1)S(1)}, u32[]{:S(2)}, u32[]{:S(2)}) collective-permute-start(bf16[144,1024]{1,0:T(8,128)(2,1)S(1)} %collective-permute-done.2.refs_10_), channel_id=1, source_target_pairs={{0,4},{1,3},{2,0},{3,7},{4,8},{5,1},{6,2},{7,11},{8,12},{9,5},{10,... | collective-permute-start | bytes 884744 | tf_op jit(solution)/shard_map/ppermute | solution.py:311
  50.2 1.8 %collective-permute-start.15 = (bf16[64,3584]{1,0:T(8,128)(2,1)S(1)}, bf16[64,3584]{1,0:T(8,128)(2,1)S(1)}, u32[]{:S(2)}, u32[]{:S(2)}) collective-permute-start(bf16[64,3584]{1,0:T(8,128)(2,1)S(1)} %pad_maximum_fusion), channel_id=1, source_target_pairs={{0,4},{1,5},{2,6},{3,7},{4,0},{5,1},{6,2},{7,3},{8,12},{9,13},{10,... | collective-permute-start | bytes 1376264 | tf_op jit(solution)/shard_map/ppermute | solution.py:308
  53.6 15.9 %fresh_product.1 = (bf16[128,2560]{1,0:T(8,128)(2,1)S(1)}, bf16[128,2560]{1,0:T(8,128)(2,1)S(1)}, bf16[128,2304]{1,0:T(8,128)(2,1)S(1)}, bf16[128,2304]{1,0:T(8,...) custom-call(s32[16]{0:T(128)S(1)} %get-tuple-element.89.pos_ref, s32[1]{0:T(128)S(6)} %select_n.59.steps_ref, ...), custom_call_target="tpu_custom_call" | custom-call | tf_op jit(solution)/shard_map/fresh_product/pallas_call | solution.py:221
  73.4 3.1 %collective-permute-start.19 = (bf16[64,2560]{1,0:T(8,128)(2,1)S(1)}, bf16[64,2560]{1,0:T(8,128)(2,1)S(1)}, u32[]{:S(2)}, u32[]{:S(2)}) collective-permute-start(bf16[64,2560]{1,0:T(8,128)(2,1)S(1)} %add_convert_fusion.1), channel_id=1, source_target_pairs={{0,2},{1,3},{2,0},{3,1},{4,6},{5,7},{6,4},{7,5},{8,10},{9,11},{10,... | collective-permute-start | bytes 983048 | tf_op jit(solution)/shard_map/ppermute | solution.py:308
  77.3 5.1 %collective-permute-done.21 = bf16[32,3584]{1,0:T(8,128)(2,1)S(1)} collective-permute-done((bf16[32,3584]{1,0:T(8,128)(2,1)S(1)}, bf16[32,3584]{1,0:T(8,128)(2,1)S(1)}, u32[]{:S(2)}, u32[]{:S(2)}) %collective-permute-start.21) | collective-permute-done | bytes 229408 | tf_op jit(solution)/shard_map/ppermute | solution.py:308
  82.7 2.2 %collective-permute-done.19 = bf16[64,2560]{1,0:T(8,128)(2,1)S(1)} collective-permute-done((bf16[64,2560]{1,0:T(8,128)(2,1)S(1)}, bf16[64,2560]{1,0:T(8,128)(2,1)S(1)}, u32[]{:S(2)}, u32[]{:S(2)}) %collective-permute-start.19) | collective-permute-done | bytes 327712 | tf_op jit(solution)/shard_map/ppermute | solution.py:308
  85.8 2.1 %collective-permute-start.24 = (bf16[16,3584]{1,0:T(8,128)(2,1)S(1)}, bf16[16,3584]{1,0:T(8,128)(2,1)S(1)}, u32[]{:S(2)}, u32[]{:S(2)}) collective-permute-start(bf16[16,3584]{1,0:T(8,128)(2,1)S(1)} %get-tuple-element.141), channel_id=1, source_target_pairs={{0,2},{1,3},{2,0},{3,1},{4,6},{5,7},{6,4},{7,5},{8,10},{9,11},{10,... | collective-permute-start | bytes 344072 | tf_op jit(solution)/shard_map/ppermute | solution.py:308
  89.1 2.2 %collective-permute-done.26 = bf16[64,2304]{1,0:T(8,128)(2,1)S(1)} collective-permute-done((bf16[64,2304]{1,0:T(8,128)(2,1)S(1)}, bf16[64,2304]{1,0:T(8,128)(2,1)S(1)}, u32[]{:S(2)}, u32[]{:S(2)}) %collective-permute-start.26) | collective-permute-done | bytes 294944 | tf_op jit(solution)/shard_map/ppermute | solution.py:308
  91.3 2.5 %collective-permute-done.24 = bf16[16,3584]{1,0:T(8,128)(2,1)S(1)} collective-permute-done((bf16[16,3584]{1,0:T(8,128)(2,1)S(1)}, bf16[16,3584]{1,0:T(8,128)(2,1)S(1)}, u32[]{:S(2)}, u32[]{:S(2)}) %collective-permute-start.24) | collective-permute-done | bytes 114720 | tf_op jit(solution)/shard_map/ppermute | solution.py:308
  95.6 2.1 %collective-permute-start.28 = (bf16[32,2304]{1,0:T(8,128)(2,1)S(1)}, bf16[32,2304]{1,0:T(8,128)(2,1)S(1)}, u32[]{:S(2)}, u32[]{:S(2)}) collective-permute-start(bf16[32,2304]{1,0:T(8,128)(2,1)S(1)} %add_convert_fusion.9), channel_id=1, source_target_pairs={{0,4},{1,5},{2,6},{3,7},{4,0},{5,1},{6,2},{7,3},{8,12},{9,13},{10,... | collective-permute-start | bytes 442376 | tf_op jit(solution)/shard_map/ppermute | solution.py:308
  97.8 1.7 %collective-permute-done.30 = bf16[64,2304]{1,0:T(8,128)(2,1)S(1)} collective-permute-done((bf16[64,2304]{1,0:T(8,128)(2,1)S(1)}, bf16[64,2304]{1,0:T(8,128)(2,1)S(1)}, u32[]{:S(2)}, u32[]{:S(2)}) %collective-permute-start.30) | collective-permute-done | bytes 294944 | tf_op jit(solution)/shard_map/ppermute | solution.py:308
  101.8 2.1 %collective-permute-start.31 = (bf16[16,2304]{1,0:T(8,128)(2,1)S(1)}, bf16[16,2304]{1,0:T(8,128)(2,1)S(1)}, u32[]{:S(2)}, u32[]{:S(2)}) collective-permute-start(bf16[16,2304]{1,0:T(8,128)(2,1)S(1)} %add_convert_fusion.21), channel_id=1, source_target_pairs={{0,8},{1,9},{2,10},{3,11},{4,12},{5,13},{6,14},{7,15},{8,0},{9,1},... | collective-permute-start | bytes 221192 | tf_op jit(solution)/shard_map/ppermute | solution.py:308
  104.8 2.3 %collective-permute-done.31 = bf16[16,2304]{1,0:T(8,128)(2,1)S(1)} collective-permute-done((bf16[16,2304]{1,0:T(8,128)(2,1)S(1)}, bf16[16,2304]{1,0:T(8,128)(2,1)S(1)}, u32[]{:S(2)}, u32[]{:S(2)}) %collective-permute-start.31) | collective-permute-done | bytes 73760 | tf_op jit(solution)/shard_map/ppermute | solution.py:308
  107.1 2.7 %collective-permute-done.32 = bf16[32,2304]{1,0:T(8,128)(2,1)S(1)} collective-permute-done((bf16[32,2304]{1,0:T(8,128)(2,1)S(1)}, bf16[32,2304]{1,0:T(8,128)(2,1)S(1)}, u32[]{:S(2)}, u32[]{:S(2)}) %collective-permute-start.32) | collective-permute-done | bytes 147488 | tf_op jit(solution)/shard_map/ppermute | solution.py:308
  110.9 4.6 %collective-permute-done.33 = bf16[16,2304]{1,0:T(8,128)(2,1)S(1)} collective-permute-done((bf16[16,2304]{1,0:T(8,128)(2,1)S(1)}, bf16[16,2304]{1,0:T(8,128)(2,1)S(1)}, u32[]{:S(2)}, u32[]{:S(2)}) %collective-permute-start.33) | collective-permute-done | bytes 73760 | tf_op jit(solution)/shard_map/ppermute | solution.py:308
  (106 shorter events, 30.4 us)
Async XLA Ops:
  2.8 9.8 %collective-permute-start = (bf16[144,1024]{1,0:T(8,128)(2,1)S(1)}, bf16[144,1024]{1,0:T(8,128)(2,1)S(1)}, u32[]{:S(2)}, u32[]{:S(2)}) collective-permute-start(bf16[144,1024]{1,0:T(8,128)(2,1)S(1)} %get-tuple-element.95.refs_0_), channel_id=1, source_target_pairs={{0,4},{1,3},{2,0},{3,7},{4,8},{5,1},{6,2},{7,11},{8,12},{9,5},{10,... | collective-permute-start | bytes 884744 | tf_op jit(solution)/shard_map/ppermute | solution.py:311
  5.5 9.2 %collective-permute-start.4 = (bf16[144,1024]{1,0:T(8,128)(2,1)S(1)}, bf16[144,1024]{1,0:T(8,128)(2,1)S(1)}, u32[]{:S(2)}, u32[]{:S(2)}) collective-permute-start(bf16[144,1024]{1,0:T(8,128)(2,1)S(1)} %collective-permute-done.3.refs_1_), channel_id=1, source_target_pairs={{0,4},{1,3},{2,0},{3,7},{4,8},{5,1},{6,2},{7,11},{8,12},{9,5},{10,... | collective-permute-start | bytes 884744 | tf_op jit(solution)/shard_map/ppermute | solution.py:311
  7.8 22.5 %all-to-all-start = ((bf16[16,16,1024]{2,1,0:T(8,128)(2,1)}), bf16[16,16,1024]{2,1,0:T(8,128)(2,1)S(1)}, u32[]{:S(2)}, u32[]{:S(2)}) async-start(bf16[16,16,1024]{2,1,0:T(8,128)(2,1)} %get-tuple-element.74), calls=%async_computation | async-start | bytes 1048576 | tf_op jit(solution)/shard_map/all_to_all | solution.py:402
  12.7 12.7 %collective-permute-start.1 = (bf16[144,1024]{1,0:T(8,128)(2,1)S(1)}, bf16[144,1024]{1,0:T(8,128)(2,1)S(1)}, u32[]{:S(2)}, u32[]{:S(2)}) collective-permute-start(bf16[144,1024]{1,0:T(8,128)(2,1)S(1)} %collective-permute-done.refs_2_), channel_id=1, source_target_pairs={{0,4},{1,3},{2,0},{3,7},{4,8},{5,1},{6,2},{7,11},{8,12},{9,5},{10,... | collective-permute-start | bytes 884744 | tf_op jit(solution)/shard_map/ppermute | solution.py:311
  21.1 9.1 %collective-permute-start.5 = (bf16[144,1024]{1,0:T(8,128)(2,1)S(1)}, bf16[144,1024]{1,0:T(8,128)(2,1)S(1)}, u32[]{:S(2)}, u32[]{:S(2)}) collective-permute-start(bf16[144,1024]{1,0:T(8,128)(2,1)S(1)} %collective-permute-done.4.refs_3_), channel_id=1, source_target_pairs={{0,4},{1,3},{2,0},{3,7},{4,8},{5,1},{6,2},{7,11},{8,12},{9,5},{10,... | collective-permute-start | bytes 884744 | tf_op jit(solution)/shard_map/ppermute | solution.py:311
  25.3 15.6 %collective-permute-start.2 = (bf16[144,1024]{1,0:T(8,128)(2,1)S(1)}, bf16[144,1024]{1,0:T(8,128)(2,1)S(1)}, u32[]{:S(2)}, u32[]{:S(2)}) collective-permute-start(bf16[144,1024]{1,0:T(8,128)(2,1)S(1)} %collective-permute-done.1.refs_6_), channel_id=1, source_target_pairs={{0,4},{1,3},{2,0},{3,7},{4,8},{5,1},{6,2},{7,11},{8,12},{9,5},{10,... | collective-permute-start | bytes 884744 | tf_op jit(solution)/shard_map/ppermute | solution.py:311
  30.3 10.7 %collective-permute-start.6 = (bf16[144,1024]{1,0:T(8,128)(2,1)S(1)}, bf16[144,1024]{1,0:T(8,128)(2,1)S(1)}, u32[]{:S(2)}, u32[]{:S(2)}) collective-permute-start(bf16[144,1024]{1,0:T(8,128)(2,1)S(1)} %collective-permute-done.5.refs_7_), channel_id=1, source_target_pairs={{0,4},{1,3},{2,0},{3,7},{4,8},{5,1},{6,2},{7,11},{8,12},{9,5},{10,... | collective-permute-start | bytes 884744 | tf_op jit(solution)/shard_map/ppermute | solution.py:311
  41.0 6.5 %collective-permute-start.8 = (bf16[144,1024]{1,0:T(8,128)(2,1)S(1)}, bf16[144,1024]{1,0:T(8,128)(2,1)S(1)}, u32[]{:S(2)}, u32[]{:S(2)}) collective-permute-start(bf16[144,1024]{1,0:T(8,128)(2,1)S(1)} %collective-permute-done.refs_2_), channel_id=1, source_target_pairs={{0,1},{1,0},{2,3},{3,2},{4,5},{5,4},{6,7},{7,6},{8,9},{9,8},{10,11... | collective-permute-start | bytes 884744 | tf_op jit(solution)/shard_map/ppermute | solution.py:308
  41.5 6.1 %collective-permute-start.9 = (bf16[144,1024]{1,0:T(8,128)(2,1)S(1)}, bf16[144,1024]{1,0:T(8,128)(2,1)S(1)}, u32[]{:S(2)}, u32[]{:S(2)}) collective-permute-start(bf16[144,1024]{1,0:T(8,128)(2,1)S(1)} %collective-permute-done.4.refs_3_), channel_id=1, source_target_pairs={{0,1},{1,0},{2,3},{3,2},{4,5},{5,4},{6,7},{7,6},{8,9},{9,8},{10,11... | collective-permute-start | bytes 884744 | tf_op jit(solution)/shard_map/ppermute | solution.py:308
  41.6 6.5 %collective-permute-start.10 = (bf16[144,1024]{1,0:T(8,128)(2,1)S(1)}, bf16[144,1024]{1,0:T(8,128)(2,1)S(1)}, u32[]{:S(2)}, u32[]{:S(2)}) collective-permute-start(bf16[144,1024]{1,0:T(8,128)(2,1)S(1)} %collective-permute-done.1.refs_6_), channel_id=1, source_target_pairs={{0,1},{1,0},{2,3},{3,2},{4,5},{5,4},{6,7},{7,6},{8,9},{9,8},{10,11... | collective-permute-start | bytes 884744 | tf_op jit(solution)/shard_map/ppermute | solution.py:308
  42.0 6.1 %collective-permute-start.11 = (bf16[144,1024]{1,0:T(8,128)(2,1)S(1)}, bf16[144,1024]{1,0:T(8,128)(2,1)S(1)}, u32[]{:S(2)}, u32[]{:S(2)}) collective-permute-start(bf16[144,1024]{1,0:T(8,128)(2,1)S(1)} %collective-permute-done.5.refs_7_), channel_id=1, source_target_pairs={{0,1},{1,0},{2,3},{3,2},{4,5},{5,4},{6,7},{7,6},{8,9},{9,8},{10,11... | collective-permute-start | bytes 884744 | tf_op jit(solution)/shard_map/ppermute | solution.py:308
  44.8 7.2 %collective-permute-start.16 = (bf16[144,1024]{1,0:T(8,128)(2,1)S(1)}, bf16[144,1024]{1,0:T(8,128)(2,1)S(1)}, u32[]{:S(2)}, u32[]{:S(2)}) collective-permute-start(bf16[144,1024]{1,0:T(8,128)(2,1)S(1)} %collective-permute-done.2.refs_10_), channel_id=1, source_target_pairs={{0,4},{1,3},{2,0},{3,7},{4,8},{5,1},{6,2},{7,11},{8,12},{9,5},{10,... | collective-permute-start | bytes 884744 | tf_op jit(solution)/shard_map/ppermute | solution.py:311
  49.6 19.8 %collective-permute-start.14 = (bf16[64,3584]{1,0:T(8,128)(2,1)S(1)}, bf16[64,3584]{1,0:T(8,128)(2,1)S(1)}, u32[]{:S(2)}, u32[]{:S(2)}) collective-permute-start(bf16[64,3584]{1,0:T(8,128)(2,1)S(1)} %add_convert_fusion), channel_id=1, source_target_pairs={{0,2},{1,3},{2,0},{3,1},{4,6},{5,7},{6,4},{7,5},{8,10},{9,11},{10,... | collective-permute-start | bytes 1376264 | tf_op jit(solution)/shard_map/ppermute | solution.py:308
  50.2 19.3 %collective-permute-start.15 = (bf16[64,3584]{1,0:T(8,128)(2,1)S(1)}, bf16[64,3584]{1,0:T(8,128)(2,1)S(1)}, u32[]{:S(2)}, u32[]{:S(2)}) collective-permute-start(bf16[64,3584]{1,0:T(8,128)(2,1)S(1)} %pad_maximum_fusion), channel_id=1, source_target_pairs={{0,4},{1,5},{2,6},{3,7},{4,0},{5,1},{6,2},{7,3},{8,12},{9,13},{10,... | collective-permute-start | bytes 1376264 | tf_op jit(solution)/shard_map/ppermute | solution.py:308
  69.6 12.9 %collective-permute-start.21 = (bf16[32,3584]{1,0:T(8,128)(2,1)S(1)}, bf16[32,3584]{1,0:T(8,128)(2,1)S(1)}, u32[]{:S(2)}, u32[]{:S(2)}) collective-permute-start(bf16[32,3584]{1,0:T(8,128)(2,1)S(1)} %pad_maximum_fusion.2), channel_id=1, source_target_pairs={{0,8},{1,9},{2,10},{3,11},{4,12},{5,13},{6,14},{7,15},{8,0},{9,1},... | collective-permute-start | bytes 688136 | tf_op jit(solution)/shard_map/ppermute | solution.py:308
  71.3 11.4 %collective-permute-start.20 = (bf16[32,3584]{1,0:T(8,128)(2,1)S(1)}, bf16[32,3584]{1,0:T(8,128)(2,1)S(1)}, u32[]{:S(2)}, u32[]{:S(2)}) collective-permute-start(bf16[32,3584]{1,0:T(8,128)(2,1)S(1)} %add_convert_fusion.4), channel_id=1, source_target_pairs={{0,4},{1,5},{2,6},{3,7},{4,0},{5,1},{6,2},{7,3},{8,12},{9,13},{10,... | collective-permute-start | bytes 688136 | tf_op jit(solution)/shard_map/ppermute | solution.py:308
  72.0 16.4 %collective-permute-start.29 = (bf16[128,2304]{1,0:T(8,128)(2,1)S(1)}, bf16[128,2304]{1,0:T(8,128)(2,1)S(1)}, u32[]{:S(2)}, u32[]{:S(2)}) collective-permute-start(bf16[128,2304]{1,0:T(8,128)(2,1)S(1)} %get-tuple-element.129), channel_id=1, source_target_pairs={{0,1},{1,0},{2,3},{3,2},{4,5},{5,4},{6,7},{7,6},{8,9},{9,8},{10,11... | collective-permute-start | bytes 1769480 | tf_op jit(solution)/shard_map/ppermute | solution.py:308
  73.4 11.6 %collective-permute-start.19 = (bf16[64,2560]{1,0:T(8,128)(2,1)S(1)}, bf16[64,2560]{1,0:T(8,128)(2,1)S(1)}, u32[]{:S(2)}, u32[]{:S(2)}) collective-permute-start(bf16[64,2560]{1,0:T(8,128)(2,1)S(1)} %add_convert_fusion.1), channel_id=1, source_target_pairs={{0,2},{1,3},{2,0},{3,1},{4,6},{5,7},{6,4},{7,5},{8,10},{9,11},{10,... | collective-permute-start | bytes 983048 | tf_op jit(solution)/shard_map/ppermute | solution.py:308
  76.6 14.7 %collective-permute-start.26 = (bf16[64,2304]{1,0:T(8,128)(2,1)S(1)}, bf16[64,2304]{1,0:T(8,128)(2,1)S(1)}, u32[]{:S(2)}, u32[]{:S(2)}) collective-permute-start(bf16[64,2304]{1,0:T(8,128)(2,1)S(1)} %add_convert_fusion.3), channel_id=1, source_target_pairs={{0,2},{1,3},{2,0},{3,1},{4,6},{5,7},{6,4},{7,5},{8,10},{9,11},{10,... | collective-permute-start | bytes 884744 | tf_op jit(solution)/shard_map/ppermute | solution.py:308
  85.0 10.4 %collective-permute-start.22 = (bf16[32,2560]{1,0:T(8,128)(2,1)S(1)}, bf16[32,2560]{1,0:T(8,128)(2,1)S(1)}, u32[]{:S(2)}, u32[]{:S(2)}) collective-permute-start(bf16[32,2560]{1,0:T(8,128)(2,1)S(1)} %add_convert_fusion.7), channel_id=1, source_target_pairs={{0,4},{1,5},{2,6},{3,7},{4,0},{5,1},{6,2},{7,3},{8,12},{9,13},{10,... | collective-permute-start | bytes 491528 | tf_op jit(solution)/shard_map/ppermute | solution.py:308
  85.8 7.9 %collective-permute-start.24 = (bf16[16,3584]{1,0:T(8,128)(2,1)S(1)}, bf16[16,3584]{1,0:T(8,128)(2,1)S(1)}, u32[]{:S(2)}, u32[]{:S(2)}) collective-permute-start(bf16[16,3584]{1,0:T(8,128)(2,1)S(1)} %get-tuple-element.141), channel_id=1, source_target_pairs={{0,2},{1,3},{2,0},{3,1},{4,6},{5,7},{6,4},{7,5},{8,10},{9,11},{10,... | collective-permute-start | bytes 344072 | tf_op jit(solution)/shard_map/ppermute | solution.py:308
  87.9 7.5 %collective-permute-start.23 = (bf16[16,3584]{1,0:T(8,128)(2,1)S(1)}, bf16[16,3584]{1,0:T(8,128)(2,1)S(1)}, u32[]{:S(2)}, u32[]{:S(2)}) collective-permute-start(bf16[16,3584]{1,0:T(8,128)(2,1)S(1)} %get-tuple-element.142), channel_id=1, source_target_pairs={{0,8},{1,9},{2,10},{3,11},{4,12},{5,13},{6,14},{7,15},{8,0},{9,1},... | collective-permute-start | bytes 344072 | tf_op jit(solution)/shard_map/ppermute | solution.py:308
  88.4 11.2 %collective-permute-start.30 = (bf16[64,2304]{1,0:T(8,128)(2,1)S(1)}, bf16[64,2304]{1,0:T(8,128)(2,1)S(1)}, u32[]{:S(2)}, u32[]{:S(2)}) collective-permute-start(bf16[64,2304]{1,0:T(8,128)(2,1)S(1)} %add_convert_fusion.2), channel_id=1, source_target_pairs={{0,2},{1,3},{2,0},{3,1},{4,6},{5,7},{6,4},{7,5},{8,10},{9,11},{10,... | collective-permute-start | bytes 884744 | tf_op jit(solution)/shard_map/ppermute | solution.py:308
  95.6 6.1 %collective-permute-start.28 = (bf16[32,2304]{1,0:T(8,128)(2,1)S(1)}, bf16[32,2304]{1,0:T(8,128)(2,1)S(1)}, u32[]{:S(2)}, u32[]{:S(2)}) collective-permute-start(bf16[32,2304]{1,0:T(8,128)(2,1)S(1)} %add_convert_fusion.9), channel_id=1, source_target_pairs={{0,4},{1,5},{2,6},{3,7},{4,0},{5,1},{6,2},{7,3},{8,12},{9,13},{10,... | collective-permute-start | bytes 442376 | tf_op jit(solution)/shard_map/ppermute | solution.py:308
  (13 other events, 96.0 us)

commit v5 on v4

--- a/solution.py
+++ b/solution.py
@@ -11,8 +11,8 @@
 BLK = 128
 LANES = 128
 PAD_ROWS = 16
-PAIRS = 16
-SPARE_VMEM = 3 * 1024 * 1024
+PAIRS = 24
+SPARE_VMEM = 8 * 1024 * 1024
 F32 = jnp.float32
 BF16 = jnp.bfloat16
 
@@ -82,7 +82,7 @@
             pltpu.VMEM((experts, row_count, width), BF16),
             pltpu.VMEM((row_count * top_count + PAD_ROWS, width), BF16),
         ],
-        compiler_params=pltpu.CompilerParams(vmem_limit_bytes=6 * SPARE_VMEM),
+        compiler_params=pltpu.CompilerParams(vmem_limit_bytes=2 * SPARE_VMEM),
         cost_estimate=pl.CostEstimate(flops=0, bytes_accessed=0, transcendentals=0),
         name="prepare",
     )(*[in_hbm(x) for x in (hidden_act, routes.transpose(0, 2, 1), gates.transpose(0, 2, 1))])

time: 117 us -> 116 us (level)
  Pallas kernels: 26 us -> 24.5 us
    pallas_call x1, Pallas kernels: 15.9 us -> 14.3 us  [fresh_product(): pl.pallas_call(functools.partial(fresh_kernel, n_pieces, experts, row_cou...]
  transfers between devices with their start and end apart: 35 -> 35, of which waited for: 17 -> 17; matrix products, arithmetic and copies ran while one was open for 7% -> 7% of each run, Pallas kernels for 20% -> 19%
where the time goes in v5:
time: 116 us
  starting transfers between devices  44 us (38%)
  waiting for transfers between devices  36.9 us (32%)
  Pallas kernels  24.5 us (21%)
  other arithmetic  6.88 us (6%)
  local copies, waits for them, and re-layouts  2.42 us (2%)
    ppermute x27, waiting for transfers between devices, partner(): return lax.ppermute(x, 'expert', [(i, i ^ delta) for i in range(self.SIZE)])  34.2 us
    ppermute x27, starting transfers between devices, partner(): return lax.ppermute(x, 'expert', [(i, i ^ delta) for i in range(self.SIZE)])  21.8 us
    ppermute x7, starting transfers between devices, hop(): return lax.ppermute(x, 'expert', self.ring)  17.3 us
    pallas_call x1, Pallas kernels, fresh_product(): pl.pallas_call(functools.partial(fresh_kernel, n_pieces, experts, row_cou...  14.3 us
    pallas_call x1, Pallas kernels, old_product(): pl.pallas_call(old_kernel, grid_spec=pltpu.PrefetchScalarGridSpec(num_sca...  7.87 us
    all_to_all x1, starting transfers between devices, body(): lax.all_to_all(spread_old, 'expert', split_axis=0, concat_axis=0, tiled=T...  4.86 us
    ppermute x7, waiting for transfers between devices, hop(): return lax.ppermute(x, 'expert', self.ring)  2.68 us
  transfers between devices with their start and end apart: 35, of which 17 were waited for; matrix products, arithmetic and copies ran while one was open for 7% of the time, Pallas kernels for 19%

profile of v5, /device:TPU:0, one launch (start us, length us, event | category | flops | bytes accessed | tf_op | source)
XLA Modules:
  0.0 115.7 jit_solution(14960727295979850383)
XLA Ops:
  0.0 2.3 %prepare.1 = (bf16[16,16,1024]{2,1,0:T(8,128)(2,1)}, bf16[144,1024]{1,0:T(8,128)(2,1)S(1)}) custom-call(bf16[2,16,8,1024]{3,2,1,0:T(8,128)(2,1)} %act_hbm.1, s32[2,8,16]{2,1,0:T(8,128)} %bitcast.14, f32[2,8,16]{2,1,0:T(8,128)} %bitcast.15), custom_call_target="tpu_custom_call" | custom-call | tf_op jit(solution)/shard_map/prepare/pallas_call | solution.py:71
  2.8 2.6 %collective-permute-start = (bf16[144,1024]{1,0:T(8,128)(2,1)S(1)}, bf16[144,1024]{1,0:T(8,128)(2,1)S(1)}, u32[]{:S(2)}, u32[]{:S(2)}) collective-permute-start(bf16[144,1024]{1,0:T(8,128)(2,1)S(1)} %get-tuple-element.95.refs_0_), channel_id=1, source_target_pairs={{0,4},{1,3},{2,0},{3,7},{4,8},{5,1},{6,2},{7,11},{8,12},{9,5},{10,... | collective-permute-start | bytes 884744 | tf_op jit(solution)/shard_map/ppermute | solution.py:311
  7.8 4.9 %all-to-all-start = ((bf16[16,16,1024]{2,1,0:T(8,128)(2,1)}), bf16[16,16,1024]{2,1,0:T(8,128)(2,1)S(1)}, u32[]{:S(2)}, u32[]{:S(2)}) async-start(bf16[16,16,1024]{2,1,0:T(8,128)(2,1)} %get-tuple-element.74), calls=%async_computation | async-start | bytes 1048576 | tf_op jit(solution)/shard_map/all_to_all | solution.py:402
  12.7 2.0 %collective-permute-start.1 = (bf16[144,1024]{1,0:T(8,128)(2,1)S(1)}, bf16[144,1024]{1,0:T(8,128)(2,1)S(1)}, u32[]{:S(2)}, u32[]{:S(2)}) collective-permute-start(bf16[144,1024]{1,0:T(8,128)(2,1)S(1)} %collective-permute-done.refs_2_), channel_id=1, source_target_pairs={{0,4},{1,3},{2,0},{3,7},{4,8},{5,1},{6,2},{7,11},{8,12},{9,5},{10,... | collective-permute-start | bytes 884744 | tf_op jit(solution)/shard_map/ppermute | solution.py:311
  22.7 2.7 %collective-permute-done.1.refs_6_ = bf16[144,1024]{1,0:T(8,128)(2,1)S(1)} collective-permute-done((bf16[144,1024]{1,0:T(8,128)(2,1)S(1)}, bf16[144,1024]{1,0:T(8,128)(2,1)S(1)}, u32[]{:S(2)}, u32[]{:S(2)}) %collective-permute-start.1) | collective-permute-done | bytes 294944 | tf_op jit(solution)/shard_map/ppermute | solution.py:311
  25.3 4.5 %collective-permute-start.2 = (bf16[144,1024]{1,0:T(8,128)(2,1)S(1)}, bf16[144,1024]{1,0:T(8,128)(2,1)S(1)}, u32[]{:S(2)}, u32[]{:S(2)}) collective-permute-start(bf16[144,1024]{1,0:T(8,128)(2,1)S(1)} %collective-permute-done.1.refs_6_), channel_id=1, source_target_pairs={{0,4},{1,3},{2,0},{3,7},{4,8},{5,1},{6,2},{7,11},{8,12},{9,5},{10,... | collective-permute-start | bytes 884744 | tf_op jit(solution)/shard_map/ppermute | solution.py:311
  30.3 2.7 %collective-permute-start.6 = (bf16[144,1024]{1,0:T(8,128)(2,1)S(1)}, bf16[144,1024]{1,0:T(8,128)(2,1)S(1)}, u32[]{:S(2)}, u32[]{:S(2)}) collective-permute-start(bf16[144,1024]{1,0:T(8,128)(2,1)S(1)} %collective-permute-done.5.refs_7_), channel_id=1, source_target_pairs={{0,4},{1,3},{2,0},{3,7},{4,8},{5,1},{6,2},{7,11},{8,12},{9,5},{10,... | collective-permute-start | bytes 884744 | tf_op jit(solution)/shard_map/ppermute | solution.py:311
  33.0 7.9 %old_product.1 = (bf16[128,7168]{1,0:T(8,128)(2,1)S(1)}, bf16[128,7168]{1,0:T(8,128)(2,1)S(1)}) custom-call(s32[16]{0:T(128)S(1)} %get-tuple-element.79.order_ref, f32[448]{0:T(512)S(1)} %reshape_squeeze.7.scale_ref, bf16[16,16,1024]{2,1,0:T(8,128)(2,1)S(1)} %all-to-all-done.act_ref, bf16[1024,7168]{1,0:T(8,128)(2,1)} %bitcast.13), custom_call_target="tpu_custom_call" | custom-call | tf_op jit(solution)/shard_map/old_product/pallas_call | solution.py:136
  42.1 2.7 %collective-permute-done.7 = bf16[128,7168]{1,0:T(8,128)(2,1)S(1)} collective-permute-done((bf16[128,7168]{1,0:T(8,128)(2,1)S(1)}, bf16[128,7168]{1,0:T(8,128)(2,1)S(1)}, u32[]{:S(2)}, u32[]{:S(2)}) %collective-permute-start.7) | collective-permute-done | bytes 1835040 | tf_op jit(solution)/shard_map/ppermute | solution.py:308
  44.8 2.5 %collective-permute-start.16 = (bf16[144,1024]{1,0:T(8,128)(2,1)S(1)}, bf16[144,1024]{1,0:T(8,128)(2,1)S(1)}, u32[]{:S(2)}, u32[]{:S(2)}) collective-permute-start(bf16[144,1024]{1,0:T(8,128)(2,1)S(1)} %collective-permute-done.2.refs_10_), channel_id=1, source_target_pairs={{0,4},{1,3},{2,0},{3,7},{4,8},{5,1},{6,2},{7,11},{8,12},{9,5},{10,... | collective-permute-start | bytes 884744 | tf_op jit(solution)/shard_map/ppermute | solution.py:311
  50.2 1.8 %collective-permute-start.15 = (bf16[64,3584]{1,0:T(8,128)(2,1)S(1)}, bf16[64,3584]{1,0:T(8,128)(2,1)S(1)}, u32[]{:S(2)}, u32[]{:S(2)}) collective-permute-start(bf16[64,3584]{1,0:T(8,128)(2,1)S(1)} %pad_maximum_fusion), channel_id=1, source_target_pairs={{0,4},{1,5},{2,6},{3,7},{4,0},{5,1},{6,2},{7,3},{8,12},{9,13},{10,... | collective-permute-start | bytes 1376264 | tf_op jit(solution)/shard_map/ppermute | solution.py:308
  53.6 14.3 %fresh_product.1 = (bf16[128,2560]{1,0:T(8,128)(2,1)S(1)}, bf16[128,2560]{1,0:T(8,128)(2,1)S(1)}, bf16[128,2304]{1,0:T(8,128)(2,1)S(1)}, bf16[128,2304]{1,0:T(8,...) custom-call(s32[16]{0:T(128)S(1)} %get-tuple-element.89.pos_ref, s32[1]{0:T(128)S(6)} %select_n.59.steps_ref, ...), custom_call_target="tpu_custom_call" | custom-call | tf_op jit(solution)/shard_map/fresh_product/pallas_call | solution.py:221
  68.0 2.4 %collective-permute-start.21 = (bf16[32,3584]{1,0:T(8,128)(2,1)S(1)}, bf16[32,3584]{1,0:T(8,128)(2,1)S(1)}, u32[]{:S(2)}, u32[]{:S(2)}) collective-permute-start(bf16[32,3584]{1,0:T(8,128)(2,1)S(1)} %pad_maximum_fusion.2), channel_id=1, source_target_pairs={{0,8},{1,9},{2,10},{3,11},{4,12},{5,13},{6,14},{7,15},{8,0},{9,1},... | collective-permute-start | bytes 688136 | tf_op jit(solution)/shard_map/ppermute | solution.py:308
  72.6 3.6 %collective-permute-start.19 = (bf16[64,2560]{1,0:T(8,128)(2,1)S(1)}, bf16[64,2560]{1,0:T(8,128)(2,1)S(1)}, u32[]{:S(2)}, u32[]{:S(2)}) collective-permute-start(bf16[64,2560]{1,0:T(8,128)(2,1)S(1)} %add_convert_fusion.1), channel_id=1, source_target_pairs={{0,2},{1,3},{2,0},{3,1},{4,6},{5,7},{6,4},{7,5},{8,10},{9,11},{10,... | collective-permute-start | bytes 983048 | tf_op jit(solution)/shard_map/ppermute | solution.py:308
  77.0 4.6 %collective-permute-done.21 = bf16[32,3584]{1,0:T(8,128)(2,1)S(1)} collective-permute-done((bf16[32,3584]{1,0:T(8,128)(2,1)S(1)}, bf16[32,3584]{1,0:T(8,128)(2,1)S(1)}, u32[]{:S(2)}, u32[]{:S(2)}) %collective-permute-start.21) | collective-permute-done | bytes 229408 | tf_op jit(solution)/shard_map/ppermute | solution.py:308
  81.9 2.8 %collective-permute-done.19 = bf16[64,2560]{1,0:T(8,128)(2,1)S(1)} collective-permute-done((bf16[64,2560]{1,0:T(8,128)(2,1)S(1)}, bf16[64,2560]{1,0:T(8,128)(2,1)S(1)}, u32[]{:S(2)}, u32[]{:S(2)}) %collective-permute-start.19) | collective-permute-done | bytes 327712 | tf_op jit(solution)/shard_map/ppermute | solution.py:308
  85.9 2.1 %collective-permute-start.24 = (bf16[16,3584]{1,0:T(8,128)(2,1)S(1)}, bf16[16,3584]{1,0:T(8,128)(2,1)S(1)}, u32[]{:S(2)}, u32[]{:S(2)}) collective-permute-start(bf16[16,3584]{1,0:T(8,128)(2,1)S(1)} %get-tuple-element.141), channel_id=1, source_target_pairs={{0,2},{1,3},{2,0},{3,1},{4,6},{5,7},{6,4},{7,5},{8,10},{9,11},{10,... | collective-permute-start | bytes 344072 | tf_op jit(solution)/shard_map/ppermute | solution.py:308
  88.6 2.4 %collective-permute-done.26 = bf16[64,2304]{1,0:T(8,128)(2,1)S(1)} collective-permute-done((bf16[64,2304]{1,0:T(8,128)(2,1)S(1)}, bf16[64,2304]{1,0:T(8,128)(2,1)S(1)}, u32[]{:S(2)}, u32[]{:S(2)}) %collective-permute-start.26) | collective-permute-done | bytes 294944 | tf_op jit(solution)/shard_map/ppermute | solution.py:308
  91.0 2.5 %collective-permute-done.24 = bf16[16,3584]{1,0:T(8,128)(2,1)S(1)} collective-permute-done((bf16[16,3584]{1,0:T(8,128)(2,1)S(1)}, bf16[16,3584]{1,0:T(8,128)(2,1)S(1)}, u32[]{:S(2)}, u32[]{:S(2)}) %collective-permute-start.24) | collective-permute-done | bytes 114720 | tf_op jit(solution)/shard_map/ppermute | solution.py:308
  97.0 2.5 %collective-permute-done.30 = bf16[64,2304]{1,0:T(8,128)(2,1)S(1)} collective-permute-done((bf16[64,2304]{1,0:T(8,128)(2,1)S(1)}, bf16[64,2304]{1,0:T(8,128)(2,1)S(1)}, u32[]{:S(2)}, u32[]{:S(2)}) %collective-permute-start.30) | collective-permute-done | bytes 294944 | tf_op jit(solution)/shard_map/ppermute | solution.py:308
  101.4 2.3 %collective-permute-start.31 = (bf16[16,2304]{1,0:T(8,128)(2,1)S(1)}, bf16[16,2304]{1,0:T(8,128)(2,1)S(1)}, u32[]{:S(2)}, u32[]{:S(2)}) collective-permute-start(bf16[16,2304]{1,0:T(8,128)(2,1)S(1)} %add_convert_fusion.21), channel_id=1, source_target_pairs={{0,8},{1,9},{2,10},{3,11},{4,12},{5,13},{6,14},{7,15},{8,0},{9,1},... | collective-permute-start | bytes 221192 | tf_op jit(solution)/shard_map/ppermute | solution.py:308
  105.3 2.3 %collective-permute-done.31 = bf16[16,2304]{1,0:T(8,128)(2,1)S(1)} collective-permute-done((bf16[16,2304]{1,0:T(8,128)(2,1)S(1)}, bf16[16,2304]{1,0:T(8,128)(2,1)S(1)}, u32[]{:S(2)}, u32[]{:S(2)}) %collective-permute-start.31) | collective-permute-done | bytes 73760 | tf_op jit(solution)/shard_map/ppermute | solution.py:308
  107.6 1.9 %collective-permute-done.32 = bf16[32,2304]{1,0:T(8,128)(2,1)S(1)} collective-permute-done((bf16[32,2304]{1,0:T(8,128)(2,1)S(1)}, bf16[32,2304]{1,0:T(8,128)(2,1)S(1)}, u32[]{:S(2)}, u32[]{:S(2)}) %collective-permute-start.32) | collective-permute-done | bytes 147488 | tf_op jit(solution)/shard_map/ppermute | solution.py:308
  110.4 4.4 %collective-permute-done.33 = bf16[16,2304]{1,0:T(8,128)(2,1)S(1)} collective-permute-done((bf16[16,2304]{1,0:T(8,128)(2,1)S(1)}, bf16[16,2304]{1,0:T(8,128)(2,1)S(1)}, u32[]{:S(2)}, u32[]{:S(2)}) %collective-permute-start.33) | collective-permute-done | bytes 73760 | tf_op jit(solution)/shard_map/ppermute | solution.py:308
  (106 shorter events, 30.2 us)
Async XLA Ops:
  2.8 9.8 %collective-permute-start = (bf16[144,1024]{1,0:T(8,128)(2,1)S(1)}, bf16[144,1024]{1,0:T(8,128)(2,1)S(1)}, u32[]{:S(2)}, u32[]{:S(2)}) collective-permute-start(bf16[144,1024]{1,0:T(8,128)(2,1)S(1)} %get-tuple-element.95.refs_0_), channel_id=1, source_target_pairs={{0,4},{1,3},{2,0},{3,7},{4,8},{5,1},{6,2},{7,11},{8,12},{9,5},{10,... | collective-permute-start | bytes 884744 | tf_op jit(solution)/shard_map/ppermute | solution.py:311
  5.5 9.2 %collective-permute-start.4 = (bf16[144,1024]{1,0:T(8,128)(2,1)S(1)}, bf16[144,1024]{1,0:T(8,128)(2,1)S(1)}, u32[]{:S(2)}, u32[]{:S(2)}) collective-permute-start(bf16[144,1024]{1,0:T(8,128)(2,1)S(1)} %collective-permute-done.3.refs_1_), channel_id=1, source_target_pairs={{0,4},{1,3},{2,0},{3,7},{4,8},{5,1},{6,2},{7,11},{8,12},{9,5},{10,... | collective-permute-start | bytes 884744 | tf_op jit(solution)/shard_map/ppermute | solution.py:311
  7.8 22.5 %all-to-all-start = ((bf16[16,16,1024]{2,1,0:T(8,128)(2,1)}), bf16[16,16,1024]{2,1,0:T(8,128)(2,1)S(1)}, u32[]{:S(2)}, u32[]{:S(2)}) async-start(bf16[16,16,1024]{2,1,0:T(8,128)(2,1)} %get-tuple-element.74), calls=%async_computation | async-start | bytes 1048576 | tf_op jit(solution)/shard_map/all_to_all | solution.py:402
  12.7 12.7 %collective-permute-start.1 = (bf16[144,1024]{1,0:T(8,128)(2,1)S(1)}, bf16[144,1024]{1,0:T(8,128)(2,1)S(1)}, u32[]{:S(2)}, u32[]{:S(2)}) collective-permute-start(bf16[144,1024]{1,0:T(8,128)(2,1)S(1)} %collective-permute-done.refs_2_), channel_id=1, source_target_pairs={{0,4},{1,3},{2,0},{3,7},{4,8},{5,1},{6,2},{7,11},{8,12},{9,5},{10,... | collective-permute-start | bytes 884744 | tf_op jit(solution)/shard_map/ppermute | solution.py:311
  21.1 9.1 %collective-permute-start.5 = (bf16[144,1024]{1,0:T(8,128)(2,1)S(1)}, bf16[144,1024]{1,0:T(8,128)(2,1)S(1)}, u32[]{:S(2)}, u32[]{:S(2)}) collective-permute-start(bf16[144,1024]{1,0:T(8,128)(2,1)S(1)} %collective-permute-done.4.refs_3_), channel_id=1, source_target_pairs={{0,4},{1,3},{2,0},{3,7},{4,8},{5,1},{6,2},{7,11},{8,12},{9,5},{10,... | collective-permute-start | bytes 884744 | tf_op jit(solution)/shard_map/ppermute | solution.py:311
  25.3 15.6 %collective-permute-start.2 = (bf16[144,1024]{1,0:T(8,128)(2,1)S(1)}, bf16[144,1024]{1,0:T(8,128)(2,1)S(1)}, u32[]{:S(2)}, u32[]{:S(2)}) collective-permute-start(bf16[144,1024]{1,0:T(8,128)(2,1)S(1)} %collective-permute-done.1.refs_6_), channel_id=1, source_target_pairs={{0,4},{1,3},{2,0},{3,7},{4,8},{5,1},{6,2},{7,11},{8,12},{9,5},{10,... | collective-permute-start | bytes 884744 | tf_op jit(solution)/shard_map/ppermute | solution.py:311
  30.3 10.6 %collective-permute-start.6 = (bf16[144,1024]{1,0:T(8,128)(2,1)S(1)}, bf16[144,1024]{1,0:T(8,128)(2,1)S(1)}, u32[]{:S(2)}, u32[]{:S(2)}) collective-permute-start(bf16[144,1024]{1,0:T(8,128)(2,1)S(1)} %collective-permute-done.5.refs_7_), channel_id=1, source_target_pairs={{0,4},{1,3},{2,0},{3,7},{4,8},{5,1},{6,2},{7,11},{8,12},{9,5},{10,... | collective-permute-start | bytes 884744 | tf_op jit(solution)/shard_map/ppermute | solution.py:311
  41.0 6.5 %collective-permute-start.8 = (bf16[144,1024]{1,0:T(8,128)(2,1)S(1)}, bf16[144,1024]{1,0:T(8,128)(2,1)S(1)}, u32[]{:S(2)}, u32[]{:S(2)}) collective-permute-start(bf16[144,1024]{1,0:T(8,128)(2,1)S(1)} %collective-permute-done.refs_2_), channel_id=1, source_target_pairs={{0,1},{1,0},{2,3},{3,2},{4,5},{5,4},{6,7},{7,6},{8,9},{9,8},{10,11... | collective-permute-start | bytes 884744 | tf_op jit(solution)/shard_map/ppermute | solution.py:308
  41.6 6.5 %collective-permute-start.10 = (bf16[144,1024]{1,0:T(8,128)(2,1)S(1)}, bf16[144,1024]{1,0:T(8,128)(2,1)S(1)}, u32[]{:S(2)}, u32[]{:S(2)}) collective-permute-start(bf16[144,1024]{1,0:T(8,128)(2,1)S(1)} %collective-permute-done.1.refs_6_), channel_id=1, source_target_pairs={{0,1},{1,0},{2,3},{3,2},{4,5},{5,4},{6,7},{7,6},{8,9},{9,8},{10,11... | collective-permute-start | bytes 884744 | tf_op jit(solution)/shard_map/ppermute | solution.py:308
  42.0 6.1 %collective-permute-start.11 = (bf16[144,1024]{1,0:T(8,128)(2,1)S(1)}, bf16[144,1024]{1,0:T(8,128)(2,1)S(1)}, u32[]{:S(2)}, u32[]{:S(2)}) collective-permute-start(bf16[144,1024]{1,0:T(8,128)(2,1)S(1)} %collective-permute-done.5.refs_7_), channel_id=1, source_target_pairs={{0,1},{1,0},{2,3},{3,2},{4,5},{5,4},{6,7},{7,6},{8,9},{9,8},{10,11... | collective-permute-start | bytes 884744 | tf_op jit(solution)/shard_map/ppermute | solution.py:308
  44.8 7.2 %collective-permute-start.16 = (bf16[144,1024]{1,0:T(8,128)(2,1)S(1)}, bf16[144,1024]{1,0:T(8,128)(2,1)S(1)}, u32[]{:S(2)}, u32[]{:S(2)}) collective-permute-start(bf16[144,1024]{1,0:T(8,128)(2,1)S(1)} %collective-permute-done.2.refs_10_), channel_id=1, source_target_pairs={{0,4},{1,3},{2,0},{3,7},{4,8},{5,1},{6,2},{7,11},{8,12},{9,5},{10,... | collective-permute-start | bytes 884744 | tf_op jit(solution)/shard_map/ppermute | solution.py:311
  49.6 18.3 %collective-permute-start.14 = (bf16[64,3584]{1,0:T(8,128)(2,1)S(1)}, bf16[64,3584]{1,0:T(8,128)(2,1)S(1)}, u32[]{:S(2)}, u32[]{:S(2)}) collective-permute-start(bf16[64,3584]{1,0:T(8,128)(2,1)S(1)} %add_convert_fusion), channel_id=1, source_target_pairs={{0,2},{1,3},{2,0},{3,1},{4,6},{5,7},{6,4},{7,5},{8,10},{9,11},{10,... | collective-permute-start | bytes 1376264 | tf_op jit(solution)/shard_map/ppermute | solution.py:308
  50.2 17.7 %collective-permute-start.15 = (bf16[64,3584]{1,0:T(8,128)(2,1)S(1)}, bf16[64,3584]{1,0:T(8,128)(2,1)S(1)}, u32[]{:S(2)}, u32[]{:S(2)}) collective-permute-start(bf16[64,3584]{1,0:T(8,128)(2,1)S(1)} %pad_maximum_fusion), channel_id=1, source_target_pairs={{0,4},{1,5},{2,6},{3,7},{4,0},{5,1},{6,2},{7,3},{8,12},{9,13},{10,... | collective-permute-start | bytes 1376264 | tf_op jit(solution)/shard_map/ppermute | solution.py:308
  68.0 13.6 %collective-permute-start.21 = (bf16[32,3584]{1,0:T(8,128)(2,1)S(1)}, bf16[32,3584]{1,0:T(8,128)(2,1)S(1)}, u32[]{:S(2)}, u32[]{:S(2)}) collective-permute-start(bf16[32,3584]{1,0:T(8,128)(2,1)S(1)} %pad_maximum_fusion.2), channel_id=1, source_target_pairs={{0,8},{1,9},{2,10},{3,11},{4,12},{5,13},{6,14},{7,15},{8,0},{9,1},... | collective-permute-start | bytes 688136 | tf_op jit(solution)/shard_map/ppermute | solution.py:308
  70.5 11.4 %collective-permute-start.20 = (bf16[32,3584]{1,0:T(8,128)(2,1)S(1)}, bf16[32,3584]{1,0:T(8,128)(2,1)S(1)}, u32[]{:S(2)}, u32[]{:S(2)}) collective-permute-start(bf16[32,3584]{1,0:T(8,128)(2,1)S(1)} %add_convert_fusion.4), channel_id=1, source_target_pairs={{0,4},{1,5},{2,6},{3,7},{4,0},{5,1},{6,2},{7,3},{8,12},{9,13},{10,... | collective-permute-start | bytes 688136 | tf_op jit(solution)/shard_map/ppermute | solution.py:308
  71.1 17.2 %collective-permute-start.29 = (bf16[128,2304]{1,0:T(8,128)(2,1)S(1)}, bf16[128,2304]{1,0:T(8,128)(2,1)S(1)}, u32[]{:S(2)}, u32[]{:S(2)}) collective-permute-start(bf16[128,2304]{1,0:T(8,128)(2,1)S(1)} %get-tuple-element.129), channel_id=1, source_target_pairs={{0,1},{1,0},{2,3},{3,2},{4,5},{5,4},{6,7},{7,6},{8,9},{9,8},{10,11... | collective-permute-start | bytes 1769480 | tf_op jit(solution)/shard_map/ppermute | solution.py:308
  72.6 12.1 %collective-permute-start.19 = (bf16[64,2560]{1,0:T(8,128)(2,1)S(1)}, bf16[64,2560]{1,0:T(8,128)(2,1)S(1)}, u32[]{:S(2)}, u32[]{:S(2)}) collective-permute-start(bf16[64,2560]{1,0:T(8,128)(2,1)S(1)} %add_convert_fusion.1), channel_id=1, source_target_pairs={{0,2},{1,3},{2,0},{3,1},{4,6},{5,7},{6,4},{7,5},{8,10},{9,11},{10,... | collective-permute-start | bytes 983048 | tf_op jit(solution)/shard_map/ppermute | solution.py:308
  76.2 14.8 %collective-permute-start.26 = (bf16[64,2304]{1,0:T(8,128)(2,1)S(1)}, bf16[64,2304]{1,0:T(8,128)(2,1)S(1)}, u32[]{:S(2)}, u32[]{:S(2)}) collective-permute-start(bf16[64,2304]{1,0:T(8,128)(2,1)S(1)} %add_convert_fusion.3), channel_id=1, source_target_pairs={{0,2},{1,3},{2,0},{3,1},{4,6},{5,7},{6,4},{7,5},{8,10},{9,11},{10,... | collective-permute-start | bytes 884744 | tf_op jit(solution)/shard_map/ppermute | solution.py:308
  84.8 10.4 %collective-permute-start.22 = (bf16[32,2560]{1,0:T(8,128)(2,1)S(1)}, bf16[32,2560]{1,0:T(8,128)(2,1)S(1)}, u32[]{:S(2)}, u32[]{:S(2)}) collective-permute-start(bf16[32,2560]{1,0:T(8,128)(2,1)S(1)} %add_convert_fusion.7), channel_id=1, source_target_pairs={{0,4},{1,5},{2,6},{3,7},{4,0},{5,1},{6,2},{7,3},{8,12},{9,13},{10,... | collective-permute-start | bytes 491528 | tf_op jit(solution)/shard_map/ppermute | solution.py:308
  85.9 7.6 %collective-permute-start.24 = (bf16[16,3584]{1,0:T(8,128)(2,1)S(1)}, bf16[16,3584]{1,0:T(8,128)(2,1)S(1)}, u32[]{:S(2)}, u32[]{:S(2)}) collective-permute-start(bf16[16,3584]{1,0:T(8,128)(2,1)S(1)} %get-tuple-element.141), channel_id=1, source_target_pairs={{0,2},{1,3},{2,0},{3,1},{4,6},{5,7},{6,4},{7,5},{8,10},{9,11},{10,... | collective-permute-start | bytes 344072 | tf_op jit(solution)/shard_map/ppermute | solution.py:308
  88.0 7.1 %collective-permute-start.23 = (bf16[16,3584]{1,0:T(8,128)(2,1)S(1)}, bf16[16,3584]{1,0:T(8,128)(2,1)S(1)}, u32[]{:S(2)}, u32[]{:S(2)}) collective-permute-start(bf16[16,3584]{1,0:T(8,128)(2,1)S(1)} %get-tuple-element.142), channel_id=1, source_target_pairs={{0,8},{1,9},{2,10},{3,11},{4,12},{5,13},{6,14},{7,15},{8,0},{9,1},... | collective-permute-start | bytes 344072 | tf_op jit(solution)/shard_map/ppermute | solution.py:308
  88.4 11.0 %collective-permute-start.30 = (bf16[64,2304]{1,0:T(8,128)(2,1)S(1)}, bf16[64,2304]{1,0:T(8,128)(2,1)S(1)}, u32[]{:S(2)}, u32[]{:S(2)}) collective-permute-start(bf16[64,2304]{1,0:T(8,128)(2,1)S(1)} %add_convert_fusion.2), channel_id=1, source_target_pairs={{0,2},{1,3},{2,0},{3,1},{4,6},{5,7},{6,4},{7,5},{8,10},{9,11},{10,... | collective-permute-start | bytes 884744 | tf_op jit(solution)/shard_map/ppermute | solution.py:308
  95.3 6.1 %collective-permute-start.28 = (bf16[32,2304]{1,0:T(8,128)(2,1)S(1)}, bf16[32,2304]{1,0:T(8,128)(2,1)S(1)}, u32[]{:S(2)}, u32[]{:S(2)}) collective-permute-start(bf16[32,2304]{1,0:T(8,128)(2,1)S(1)} %add_convert_fusion.9), channel_id=1, source_target_pairs={{0,4},{1,5},{2,6},{3,7},{4,0},{5,1},{6,2},{7,3},{8,12},{9,13},{10,... | collective-permute-start | bytes 442376 | tf_op jit(solution)/shard_map/ppermute | solution.py:308
  101.4 6.1 %collective-permute-start.31 = (bf16[16,2304]{1,0:T(8,128)(2,1)S(1)}, bf16[16,2304]{1,0:T(8,128)(2,1)S(1)}, u32[]{:S(2)}, u32[]{:S(2)}) collective-permute-start(bf16[16,2304]{1,0:T(8,128)(2,1)S(1)} %add_convert_fusion.21), channel_id=1, source_target_pairs={{0,8},{1,9},{2,10},{3,11},{4,12},{5,13},{6,14},{7,15},{8,0},{9,1},... | collective-permute-start | bytes 221192 | tf_op jit(solution)/shard_map/ppermute | solution.py:308
  (13 other events, 96.8 us)

commit v6 on v5

--- a/solution.py
+++ b/solution.py
@@ -26,7 +26,8 @@
 
 
 def prepare_kernel(experts, act_hbm, route_hbm, gate_hbm, spread_ref, piece_ref, act_ref, route_ref, gate_ref, sems):
-    _, row_count, top_count, width = act_ref.shape
+    _, top_count, row_count = gate_ref.shape
+    width = act_ref.shape[1]
     routed = row_count * top_count
     arrivals = [
         pltpu.make_async_copy(source, here, sems.at[i])
@@ -40,8 +41,8 @@
     entry = lax.broadcasted_iota(jnp.int32, (top_count, routed), 1)
 
     def gated(step):
-        rows = [act_ref[step, r].astype(F32) * gate_ref[step][:, r : r + 1] for r in range(row_count)]
-        return jnp.concatenate(rows, axis=0).astype(BF16)
+        gate = jnp.concatenate([gate_ref[step][:, r : r + 1] for r in range(row_count)], axis=0)
+        return (act_ref[step * routed : (step + 1) * routed, :].astype(F32) * gate).astype(BF16)
 
     def route_row(step):
         routes = route_ref[step].astype(F32)
@@ -73,7 +74,7 @@
         in_specs=[pl.BlockSpec(memory_space=pl.ANY)] * 3,
         out_specs=[whole] * 2,
         scratch_shapes=[
-            pltpu.VMEM(hidden_act.shape, BF16),
+            pltpu.VMEM((2 * row_count * top_count, width), BF16),
             pltpu.VMEM((2, top_count, row_count), jnp.int32),
             pltpu.VMEM((2, top_count, row_count), F32),
             pltpu.SemaphoreType.DMA((3,)),
@@ -85,7 +86,7 @@
         compiler_params=pltpu.CompilerParams(vmem_limit_bytes=2 * SPARE_VMEM),
         cost_estimate=pl.CostEstimate(flops=0, bytes_accessed=0, transcendentals=0),
         name="prepare",
-    )(*[in_hbm(x) for x in (hidden_act, routes.transpose(0, 2, 1), gates.transpose(0, 2, 1))])
+    )(*[in_hbm(x) for x in (hidden_act.reshape(-1, width), routes.transpose(0, 2, 1), gates.transpose(0, 2, 1))])
 
 
 def old_kernel(order_ref, scale_ref, act_ref, code_hbm, keep_ref, send_ref, act_scratch, code_buf, code_sem):

time: 116 us -> 116 us (level)
  no operation moved by 1% of the time
where the time goes in v6:
time: 116 us
  starting transfers between devices  43.1 us (37%)
  waiting for transfers between devices  37.6 us (32%)
  Pallas kernels  24.5 us (21%)
  other arithmetic  6.88 us (6%)
  local copies, waits for them, and re-layouts  2.42 us (2%)
    ppermute x27, waiting for transfers between devices, partner(): return lax.ppermute(x, 'expert', [(i, i ^ delta) for i in range(self.SIZE)])  34.9 us
    ppermute x27, starting transfers between devices, partner(): return lax.ppermute(x, 'expert', [(i, i ^ delta) for i in range(self.SIZE)])  21 us
    ppermute x7, starting transfers between devices, hop(): return lax.ppermute(x, 'expert', self.ring)  17.3 us
    pallas_call x1, Pallas kernels, fresh_product(): pl.pallas_call(functools.partial(fresh_kernel, n_pieces, experts, row_cou...  14.3 us
    pallas_call x1, Pallas kernels, old_product(): pl.pallas_call(old_kernel, grid_spec=pltpu.PrefetchScalarGridSpec(num_sca...  7.88 us
    all_to_all x1, starting transfers between devices, body(): lax.all_to_all(spread_old, 'expert', split_axis=0, concat_axis=0, tiled=T...  4.86 us
    ppermute x7, waiting for transfers between devices, hop(): return lax.ppermute(x, 'expert', self.ring)  2.68 us
    pallas_call x1, Pallas kernels, prepare(): pl.pallas_call(functools.partial(prepare_kernel, experts), in_specs=[pl.B...  2.34 us
  transfers between devices with their start and end apart: 35, of which 17 were waited for; matrix products, arithmetic and copies ran while one was open for 7% of the time, Pallas kernels for 19%

profile of v6, /device:TPU:0, one launch (start us, length us, event | category | flops | bytes accessed | tf_op | source)
XLA Modules:
  0.0 115.5 jit_solution(6935158549391627297)
XLA Ops:
  0.0 2.3 %prepare.1 = (bf16[16,16,1024]{2,1,0:T(8,128)(2,1)}, bf16[144,1024]{1,0:T(8,128)(2,1)S(1)}) custom-call(bf16[256,1024]{1,0:T(8,128)(2,1)} %bitcast.15, s32[2,8,16]{2,1,0:T(8,128)} %bitcast.16, f32[2,8,16]{2,1,0:T(8,128)} %bitcast.17), custom_call_target="tpu_custom_call" | custom-call | tf_op jit(solution)/shard_map/prepare/pallas_call | solution.py:72
  2.9 2.6 %collective-permute-start = (bf16[144,1024]{1,0:T(8,128)(2,1)S(1)}, bf16[144,1024]{1,0:T(8,128)(2,1)S(1)}, u32[]{:S(2)}, u32[]{:S(2)}) collective-permute-start(bf16[144,1024]{1,0:T(8,128)(2,1)S(1)} %get-tuple-element.95.refs_0_), channel_id=1, source_target_pairs={{0,4},{1,3},{2,0},{3,7},{4,8},{5,1},{6,2},{7,11},{8,12},{9,5},{10,... | collective-permute-start | bytes 884744 | tf_op jit(solution)/shard_map/ppermute | solution.py:312
  7.8 4.9 %all-to-all-start = ((bf16[16,16,1024]{2,1,0:T(8,128)(2,1)}), bf16[16,16,1024]{2,1,0:T(8,128)(2,1)S(1)}, u32[]{:S(2)}, u32[]{:S(2)}) async-start(bf16[16,16,1024]{2,1,0:T(8,128)(2,1)} %get-tuple-element.74), calls=%async_computation | async-start | bytes 1048576 | tf_op jit(solution)/shard_map/all_to_all | solution.py:403
  12.7 2.0 %collective-permute-start.1 = (bf16[144,1024]{1,0:T(8,128)(2,1)S(1)}, bf16[144,1024]{1,0:T(8,128)(2,1)S(1)}, u32[]{:S(2)}, u32[]{:S(2)}) collective-permute-start(bf16[144,1024]{1,0:T(8,128)(2,1)S(1)} %collective-permute-done.refs_2_), channel_id=1, source_target_pairs={{0,4},{1,3},{2,0},{3,7},{4,8},{5,1},{6,2},{7,11},{8,12},{9,5},{10,... | collective-permute-start | bytes 884744 | tf_op jit(solution)/shard_map/ppermute | solution.py:312
  22.7 2.7 %collective-permute-done.1.refs_6_ = bf16[144,1024]{1,0:T(8,128)(2,1)S(1)} collective-permute-done((bf16[144,1024]{1,0:T(8,128)(2,1)S(1)}, bf16[144,1024]{1,0:T(8,128)(2,1)S(1)}, u32[]{:S(2)}, u32[]{:S(2)}) %collective-permute-start.1) | collective-permute-done | bytes 294944 | tf_op jit(solution)/shard_map/ppermute | solution.py:312
  25.4 4.5 %collective-permute-start.2 = (bf16[144,1024]{1,0:T(8,128)(2,1)S(1)}, bf16[144,1024]{1,0:T(8,128)(2,1)S(1)}, u32[]{:S(2)}, u32[]{:S(2)}) collective-permute-start(bf16[144,1024]{1,0:T(8,128)(2,1)S(1)} %collective-permute-done.1.refs_6_), channel_id=1, source_target_pairs={{0,4},{1,3},{2,0},{3,7},{4,8},{5,1},{6,2},{7,11},{8,12},{9,5},{10,... | collective-permute-start | bytes 884744 | tf_op jit(solution)/shard_map/ppermute | solution.py:312
  30.3 2.7 %collective-permute-start.6 = (bf16[144,1024]{1,0:T(8,128)(2,1)S(1)}, bf16[144,1024]{1,0:T(8,128)(2,1)S(1)}, u32[]{:S(2)}, u32[]{:S(2)}) collective-permute-start(bf16[144,1024]{1,0:T(8,128)(2,1)S(1)} %collective-permute-done.5.refs_7_), channel_id=1, source_target_pairs={{0,4},{1,3},{2,0},{3,7},{4,8},{5,1},{6,2},{7,11},{8,12},{9,5},{10,... | collective-permute-start | bytes 884744 | tf_op jit(solution)/shard_map/ppermute | solution.py:312
  33.1 7.9 %old_product.1 = (bf16[128,7168]{1,0:T(8,128)(2,1)S(1)}, bf16[128,7168]{1,0:T(8,128)(2,1)S(1)}) custom-call(s32[16]{0:T(128)S(1)} %get-tuple-element.79.order_ref, f32[448]{0:T(512)S(1)} %reshape_squeeze.7.scale_ref, bf16[16,16,1024]{2,1,0:T(8,128)(2,1)S(1)} %all-to-all-done.act_ref, bf16[1024,7168]{1,0:T(8,128)(2,1)} %bitcast.14), custom_call_target="tpu_custom_call" | custom-call | tf_op jit(solution)/shard_map/old_product/pallas_call | solution.py:137
  42.1 2.7 %collective-permute-done.7 = bf16[128,7168]{1,0:T(8,128)(2,1)S(1)} collective-permute-done((bf16[128,7168]{1,0:T(8,128)(2,1)S(1)}, bf16[128,7168]{1,0:T(8,128)(2,1)S(1)}, u32[]{:S(2)}, u32[]{:S(2)}) %collective-permute-start.7) | collective-permute-done | bytes 1835040 | tf_op jit(solution)/shard_map/ppermute | solution.py:309
  44.8 2.5 %collective-permute-start.16 = (bf16[144,1024]{1,0:T(8,128)(2,1)S(1)}, bf16[144,1024]{1,0:T(8,128)(2,1)S(1)}, u32[]{:S(2)}, u32[]{:S(2)}) collective-permute-start(bf16[144,1024]{1,0:T(8,128)(2,1)S(1)} %collective-permute-done.2.refs_10_), channel_id=1, source_target_pairs={{0,4},{1,3},{2,0},{3,7},{4,8},{5,1},{6,2},{7,11},{8,12},{9,5},{10,... | collective-permute-start | bytes 884744 | tf_op jit(solution)/shard_map/ppermute | solution.py:312
  50.2 1.8 %collective-permute-start.15 = (bf16[64,3584]{1,0:T(8,128)(2,1)S(1)}, bf16[64,3584]{1,0:T(8,128)(2,1)S(1)}, u32[]{:S(2)}, u32[]{:S(2)}) collective-permute-start(bf16[64,3584]{1,0:T(8,128)(2,1)S(1)} %pad_maximum_fusion), channel_id=1, source_target_pairs={{0,4},{1,5},{2,6},{3,7},{4,0},{5,1},{6,2},{7,3},{8,12},{9,13},{10,... | collective-permute-start | bytes 1376264 | tf_op jit(solution)/shard_map/ppermute | solution.py:309
  53.6 14.3 %fresh_product.1 = (bf16[128,2560]{1,0:T(8,128)(2,1)S(1)}, bf16[128,2560]{1,0:T(8,128)(2,1)S(1)}, bf16[128,2304]{1,0:T(8,128)(2,1)S(1)}, bf16[128,2304]{1,0:T(8,...) custom-call(s32[16]{0:T(128)S(1)} %get-tuple-element.89.pos_ref, s32[1]{0:T(128)S(6)} %select_n.59.steps_ref, ...), custom_call_target="tpu_custom_call" | custom-call | tf_op jit(solution)/shard_map/fresh_product/pallas_call | solution.py:222
  68.0 3.4 %collective-permute-start.21 = (bf16[32,3584]{1,0:T(8,128)(2,1)S(1)}, bf16[32,3584]{1,0:T(8,128)(2,1)S(1)}, u32[]{:S(2)}, u32[]{:S(2)}) collective-permute-start(bf16[32,3584]{1,0:T(8,128)(2,1)S(1)} %pad_maximum_fusion.2), channel_id=1, source_target_pairs={{0,8},{1,9},{2,10},{3,11},{4,12},{5,13},{6,14},{7,15},{8,0},{9,1},... | collective-permute-start | bytes 688136 | tf_op jit(solution)/shard_map/ppermute | solution.py:309
  73.6 2.1 %collective-permute-start.19 = (bf16[64,2560]{1,0:T(8,128)(2,1)S(1)}, bf16[64,2560]{1,0:T(8,128)(2,1)S(1)}, u32[]{:S(2)}, u32[]{:S(2)}) collective-permute-start(bf16[64,2560]{1,0:T(8,128)(2,1)S(1)} %add_convert_fusion.1), channel_id=1, source_target_pairs={{0,2},{1,3},{2,0},{3,1},{4,6},{5,7},{6,4},{7,5},{8,10},{9,11},{10,... | collective-permute-start | bytes 983048 | tf_op jit(solution)/shard_map/ppermute | solution.py:309
  76.5 5.1 %collective-permute-done.21 = bf16[32,3584]{1,0:T(8,128)(2,1)S(1)} collective-permute-done((bf16[32,3584]{1,0:T(8,128)(2,1)S(1)}, bf16[32,3584]{1,0:T(8,128)(2,1)S(1)}, u32[]{:S(2)}, u32[]{:S(2)}) %collective-permute-start.21) | collective-permute-done | bytes 229408 | tf_op jit(solution)/shard_map/ppermute | solution.py:309
  85.0 2.1 %collective-permute-start.24 = (bf16[16,3584]{1,0:T(8,128)(2,1)S(1)}, bf16[16,3584]{1,0:T(8,128)(2,1)S(1)}, u32[]{:S(2)}, u32[]{:S(2)}) collective-permute-start(bf16[16,3584]{1,0:T(8,128)(2,1)S(1)} %get-tuple-element.141), channel_id=1, source_target_pairs={{0,2},{1,3},{2,0},{3,1},{4,6},{5,7},{6,4},{7,5},{8,10},{9,11},{10,... | collective-permute-start | bytes 344072 | tf_op jit(solution)/shard_map/ppermute | solution.py:309
  88.3 2.2 %collective-permute-done.26 = bf16[64,2304]{1,0:T(8,128)(2,1)S(1)} collective-permute-done((bf16[64,2304]{1,0:T(8,128)(2,1)S(1)}, bf16[64,2304]{1,0:T(8,128)(2,1)S(1)}, u32[]{:S(2)}, u32[]{:S(2)}) %collective-permute-start.26) | collective-permute-done | bytes 294944 | tf_op jit(solution)/shard_map/ppermute | solution.py:309
  90.5 2.5 %collective-permute-done.24 = bf16[16,3584]{1,0:T(8,128)(2,1)S(1)} collective-permute-done((bf16[16,3584]{1,0:T(8,128)(2,1)S(1)}, bf16[16,3584]{1,0:T(8,128)(2,1)S(1)}, u32[]{:S(2)}, u32[]{:S(2)}) %collective-permute-start.24) | collective-permute-done | bytes 114720 | tf_op jit(solution)/shard_map/ppermute | solution.py:309
  94.8 1.9 %collective-permute-start.28 = (bf16[32,2304]{1,0:T(8,128)(2,1)S(1)}, bf16[32,2304]{1,0:T(8,128)(2,1)S(1)}, u32[]{:S(2)}, u32[]{:S(2)}) collective-permute-start(bf16[32,2304]{1,0:T(8,128)(2,1)S(1)} %add_convert_fusion.9), channel_id=1, source_target_pairs={{0,4},{1,5},{2,6},{3,7},{4,0},{5,1},{6,2},{7,3},{8,12},{9,13},{10,... | collective-permute-start | bytes 442376 | tf_op jit(solution)/shard_map/ppermute | solution.py:309
  96.9 1.9 %collective-permute-done.30 = bf16[64,2304]{1,0:T(8,128)(2,1)S(1)} collective-permute-done((bf16[64,2304]{1,0:T(8,128)(2,1)S(1)}, bf16[64,2304]{1,0:T(8,128)(2,1)S(1)}, u32[]{:S(2)}, u32[]{:S(2)}) %collective-permute-start.30) | collective-permute-done | bytes 294944 | tf_op jit(solution)/shard_map/ppermute | solution.py:309
  100.9 2.1 %collective-permute-start.31 = (bf16[16,2304]{1,0:T(8,128)(2,1)S(1)}, bf16[16,2304]{1,0:T(8,128)(2,1)S(1)}, u32[]{:S(2)}, u32[]{:S(2)}) collective-permute-start(bf16[16,2304]{1,0:T(8,128)(2,1)S(1)} %add_convert_fusion.21), channel_id=1, source_target_pairs={{0,8},{1,9},{2,10},{3,11},{4,12},{5,13},{6,14},{7,15},{8,0},{9,1},... | collective-permute-start | bytes 221192 | tf_op jit(solution)/shard_map/ppermute | solution.py:309
  103.9 2.3 %collective-permute-done.31 = bf16[16,2304]{1,0:T(8,128)(2,1)S(1)} collective-permute-done((bf16[16,2304]{1,0:T(8,128)(2,1)S(1)}, bf16[16,2304]{1,0:T(8,128)(2,1)S(1)}, u32[]{:S(2)}, u32[]{:S(2)}) %collective-permute-start.31) | collective-permute-done | bytes 73760 | tf_op jit(solution)/shard_map/ppermute | solution.py:309
  106.3 2.8 %collective-permute-done.32 = bf16[32,2304]{1,0:T(8,128)(2,1)S(1)} collective-permute-done((bf16[32,2304]{1,0:T(8,128)(2,1)S(1)}, bf16[32,2304]{1,0:T(8,128)(2,1)S(1)}, u32[]{:S(2)}, u32[]{:S(2)}) %collective-permute-start.32) | collective-permute-done | bytes 147488 | tf_op jit(solution)/shard_map/ppermute | solution.py:309
  109.9 4.7 %collective-permute-done.33 = bf16[16,2304]{1,0:T(8,128)(2,1)S(1)} collective-permute-done((bf16[16,2304]{1,0:T(8,128)(2,1)S(1)}, bf16[16,2304]{1,0:T(8,128)(2,1)S(1)}, u32[]{:S(2)}, u32[]{:S(2)}) %collective-permute-start.33) | collective-permute-done | bytes 73760 | tf_op jit(solution)/shard_map/ppermute | solution.py:309
  (106 shorter events, 30.7 us)
Async XLA Ops:
  2.9 9.8 %collective-permute-start = (bf16[144,1024]{1,0:T(8,128)(2,1)S(1)}, bf16[144,1024]{1,0:T(8,128)(2,1)S(1)}, u32[]{:S(2)}, u32[]{:S(2)}) collective-permute-start(bf16[144,1024]{1,0:T(8,128)(2,1)S(1)} %get-tuple-element.95.refs_0_), channel_id=1, source_target_pairs={{0,4},{1,3},{2,0},{3,7},{4,8},{5,1},{6,2},{7,11},{8,12},{9,5},{10,... | collective-permute-start | bytes 884744 | tf_op jit(solution)/shard_map/ppermute | solution.py:312
  5.5 9.2 %collective-permute-start.4 = (bf16[144,1024]{1,0:T(8,128)(2,1)S(1)}, bf16[144,1024]{1,0:T(8,128)(2,1)S(1)}, u32[]{:S(2)}, u32[]{:S(2)}) collective-permute-start(bf16[144,1024]{1,0:T(8,128)(2,1)S(1)} %collective-permute-done.3.refs_1_), channel_id=1, source_target_pairs={{0,4},{1,3},{2,0},{3,7},{4,8},{5,1},{6,2},{7,11},{8,12},{9,5},{10,... | collective-permute-start | bytes 884744 | tf_op jit(solution)/shard_map/ppermute | solution.py:312
  7.8 22.5 %all-to-all-start = ((bf16[16,16,1024]{2,1,0:T(8,128)(2,1)}), bf16[16,16,1024]{2,1,0:T(8,128)(2,1)S(1)}, u32[]{:S(2)}, u32[]{:S(2)}) async-start(bf16[16,16,1024]{2,1,0:T(8,128)(2,1)} %get-tuple-element.74), calls=%async_computation | async-start | bytes 1048576 | tf_op jit(solution)/shard_map/all_to_all | solution.py:403
  12.7 12.7 %collective-permute-start.1 = (bf16[144,1024]{1,0:T(8,128)(2,1)S(1)}, bf16[144,1024]{1,0:T(8,128)(2,1)S(1)}, u32[]{:S(2)}, u32[]{:S(2)}) collective-permute-start(bf16[144,1024]{1,0:T(8,128)(2,1)S(1)} %collective-permute-done.refs_2_), channel_id=1, source_target_pairs={{0,4},{1,3},{2,0},{3,7},{4,8},{5,1},{6,2},{7,11},{8,12},{9,5},{10,... | collective-permute-start | bytes 884744 | tf_op jit(solution)/shard_map/ppermute | solution.py:312
  21.2 9.1 %collective-permute-start.5 = (bf16[144,1024]{1,0:T(8,128)(2,1)S(1)}, bf16[144,1024]{1,0:T(8,128)(2,1)S(1)}, u32[]{:S(2)}, u32[]{:S(2)}) collective-permute-start(bf16[144,1024]{1,0:T(8,128)(2,1)S(1)} %collective-permute-done.4.refs_3_), channel_id=1, source_target_pairs={{0,4},{1,3},{2,0},{3,7},{4,8},{5,1},{6,2},{7,11},{8,12},{9,5},{10,... | collective-permute-start | bytes 884744 | tf_op jit(solution)/shard_map/ppermute | solution.py:312
  25.4 15.6 %collective-permute-start.2 = (bf16[144,1024]{1,0:T(8,128)(2,1)S(1)}, bf16[144,1024]{1,0:T(8,128)(2,1)S(1)}, u32[]{:S(2)}, u32[]{:S(2)}) collective-permute-start(bf16[144,1024]{1,0:T(8,128)(2,1)S(1)} %collective-permute-done.1.refs_6_), channel_id=1, source_target_pairs={{0,4},{1,3},{2,0},{3,7},{4,8},{5,1},{6,2},{7,11},{8,12},{9,5},{10,... | collective-permute-start | bytes 884744 | tf_op jit(solution)/shard_map/ppermute | solution.py:312
  30.3 10.6 %collective-permute-start.6 = (bf16[144,1024]{1,0:T(8,128)(2,1)S(1)}, bf16[144,1024]{1,0:T(8,128)(2,1)S(1)}, u32[]{:S(2)}, u32[]{:S(2)}) collective-permute-start(bf16[144,1024]{1,0:T(8,128)(2,1)S(1)} %collective-permute-done.5.refs_7_), channel_id=1, source_target_pairs={{0,4},{1,3},{2,0},{3,7},{4,8},{5,1},{6,2},{7,11},{8,12},{9,5},{10,... | collective-permute-start | bytes 884744 | tf_op jit(solution)/shard_map/ppermute | solution.py:312
  41.1 6.5 %collective-permute-start.8 = (bf16[144,1024]{1,0:T(8,128)(2,1)S(1)}, bf16[144,1024]{1,0:T(8,128)(2,1)S(1)}, u32[]{:S(2)}, u32[]{:S(2)}) collective-permute-start(bf16[144,1024]{1,0:T(8,128)(2,1)S(1)} %collective-permute-done.refs_2_), channel_id=1, source_target_pairs={{0,1},{1,0},{2,3},{3,2},{4,5},{5,4},{6,7},{7,6},{8,9},{9,8},{10,11... | collective-permute-start | bytes 884744 | tf_op jit(solution)/shard_map/ppermute | solution.py:309
  41.6 6.1 %collective-permute-start.9 = (bf16[144,1024]{1,0:T(8,128)(2,1)S(1)}, bf16[144,1024]{1,0:T(8,128)(2,1)S(1)}, u32[]{:S(2)}, u32[]{:S(2)}) collective-permute-start(bf16[144,1024]{1,0:T(8,128)(2,1)S(1)} %collective-permute-done.4.refs_3_), channel_id=1, source_target_pairs={{0,1},{1,0},{2,3},{3,2},{4,5},{5,4},{6,7},{7,6},{8,9},{9,8},{10,11... | collective-permute-start | bytes 884744 | tf_op jit(solution)/shard_map/ppermute | solution.py:309
  41.6 6.5 %collective-permute-start.10 = (bf16[144,1024]{1,0:T(8,128)(2,1)S(1)}, bf16[144,1024]{1,0:T(8,128)(2,1)S(1)}, u32[]{:S(2)}, u32[]{:S(2)}) collective-permute-start(bf16[144,1024]{1,0:T(8,128)(2,1)S(1)} %collective-permute-done.1.refs_6_), channel_id=1, source_target_pairs={{0,1},{1,0},{2,3},{3,2},{4,5},{5,4},{6,7},{7,6},{8,9},{9,8},{10,11... | collective-permute-start | bytes 884744 | tf_op jit(solution)/shard_map/ppermute | solution.py:309
  42.1 6.1 %collective-permute-start.11 = (bf16[144,1024]{1,0:T(8,128)(2,1)S(1)}, bf16[144,1024]{1,0:T(8,128)(2,1)S(1)}, u32[]{:S(2)}, u32[]{:S(2)}) collective-permute-start(bf16[144,1024]{1,0:T(8,128)(2,1)S(1)} %collective-permute-done.5.refs_7_), channel_id=1, source_target_pairs={{0,1},{1,0},{2,3},{3,2},{4,5},{5,4},{6,7},{7,6},{8,9},{9,8},{10,11... | collective-permute-start | bytes 884744 | tf_op jit(solution)/shard_map/ppermute | solution.py:309
  44.8 7.2 %collective-permute-start.16 = (bf16[144,1024]{1,0:T(8,128)(2,1)S(1)}, bf16[144,1024]{1,0:T(8,128)(2,1)S(1)}, u32[]{:S(2)}, u32[]{:S(2)}) collective-permute-start(bf16[144,1024]{1,0:T(8,128)(2,1)S(1)} %collective-permute-done.2.refs_10_), channel_id=1, source_target_pairs={{0,4},{1,3},{2,0},{3,7},{4,8},{5,1},{6,2},{7,11},{8,12},{9,5},{10,... | collective-permute-start | bytes 884744 | tf_op jit(solution)/shard_map/ppermute | solution.py:312
  49.6 18.3 %collective-permute-start.14 = (bf16[64,3584]{1,0:T(8,128)(2,1)S(1)}, bf16[64,3584]{1,0:T(8,128)(2,1)S(1)}, u32[]{:S(2)}, u32[]{:S(2)}) collective-permute-start(bf16[64,3584]{1,0:T(8,128)(2,1)S(1)} %add_convert_fusion), channel_id=1, source_target_pairs={{0,2},{1,3},{2,0},{3,1},{4,6},{5,7},{6,4},{7,5},{8,10},{9,11},{10,... | collective-permute-start | bytes 1376264 | tf_op jit(solution)/shard_map/ppermute | solution.py:309
  50.2 17.7 %collective-permute-start.15 = (bf16[64,3584]{1,0:T(8,128)(2,1)S(1)}, bf16[64,3584]{1,0:T(8,128)(2,1)S(1)}, u32[]{:S(2)}, u32[]{:S(2)}) collective-permute-start(bf16[64,3584]{1,0:T(8,128)(2,1)S(1)} %pad_maximum_fusion), channel_id=1, source_target_pairs={{0,4},{1,5},{2,6},{3,7},{4,0},{5,1},{6,2},{7,3},{8,12},{9,13},{10,... | collective-permute-start | bytes 1376264 | tf_op jit(solution)/shard_map/ppermute | solution.py:309
  68.0 13.6 %collective-permute-start.21 = (bf16[32,3584]{1,0:T(8,128)(2,1)S(1)}, bf16[32,3584]{1,0:T(8,128)(2,1)S(1)}, u32[]{:S(2)}, u32[]{:S(2)}) collective-permute-start(bf16[32,3584]{1,0:T(8,128)(2,1)S(1)} %pad_maximum_fusion.2), channel_id=1, source_target_pairs={{0,8},{1,9},{2,10},{3,11},{4,12},{5,13},{6,14},{7,15},{8,0},{9,1},... | collective-permute-start | bytes 688136 | tf_op jit(solution)/shard_map/ppermute | solution.py:309
  71.5 11.4 %collective-permute-start.20 = (bf16[32,3584]{1,0:T(8,128)(2,1)S(1)}, bf16[32,3584]{1,0:T(8,128)(2,1)S(1)}, u32[]{:S(2)}, u32[]{:S(2)}) collective-permute-start(bf16[32,3584]{1,0:T(8,128)(2,1)S(1)} %add_convert_fusion.4), channel_id=1, source_target_pairs={{0,4},{1,5},{2,6},{3,7},{4,0},{5,1},{6,2},{7,3},{8,12},{9,13},{10,... | collective-permute-start | bytes 688136 | tf_op jit(solution)/shard_map/ppermute | solution.py:309
  72.2 15.2 %collective-permute-start.29 = (bf16[128,2304]{1,0:T(8,128)(2,1)S(1)}, bf16[128,2304]{1,0:T(8,128)(2,1)S(1)}, u32[]{:S(2)}, u32[]{:S(2)}) collective-permute-start(bf16[128,2304]{1,0:T(8,128)(2,1)S(1)} %get-tuple-element.129), channel_id=1, source_target_pairs={{0,1},{1,0},{2,3},{3,2},{4,5},{5,4},{6,7},{7,6},{8,9},{9,8},{10,11... | collective-permute-start | bytes 1769480 | tf_op jit(solution)/shard_map/ppermute | solution.py:309
  73.6 10.6 %collective-permute-start.19 = (bf16[64,2560]{1,0:T(8,128)(2,1)S(1)}, bf16[64,2560]{1,0:T(8,128)(2,1)S(1)}, u32[]{:S(2)}, u32[]{:S(2)}) collective-permute-start(bf16[64,2560]{1,0:T(8,128)(2,1)S(1)} %add_convert_fusion.1), channel_id=1, source_target_pairs={{0,2},{1,3},{2,0},{3,1},{4,6},{5,7},{6,4},{7,5},{8,10},{9,11},{10,... | collective-permute-start | bytes 983048 | tf_op jit(solution)/shard_map/ppermute | solution.py:309
  75.8 14.8 %collective-permute-start.26 = (bf16[64,2304]{1,0:T(8,128)(2,1)S(1)}, bf16[64,2304]{1,0:T(8,128)(2,1)S(1)}, u32[]{:S(2)}, u32[]{:S(2)}) collective-permute-start(bf16[64,2304]{1,0:T(8,128)(2,1)S(1)} %add_convert_fusion.3), channel_id=1, source_target_pairs={{0,2},{1,3},{2,0},{3,1},{4,6},{5,7},{6,4},{7,5},{8,10},{9,11},{10,... | collective-permute-start | bytes 884744 | tf_op jit(solution)/shard_map/ppermute | solution.py:309
  84.3 10.3 %collective-permute-start.22 = (bf16[32,2560]{1,0:T(8,128)(2,1)S(1)}, bf16[32,2560]{1,0:T(8,128)(2,1)S(1)}, u32[]{:S(2)}, u32[]{:S(2)}) collective-permute-start(bf16[32,2560]{1,0:T(8,128)(2,1)S(1)} %add_convert_fusion.7), channel_id=1, source_target_pairs={{0,4},{1,5},{2,6},{3,7},{4,0},{5,1},{6,2},{7,3},{8,12},{9,13},{10,... | collective-permute-start | bytes 491528 | tf_op jit(solution)/shard_map/ppermute | solution.py:309
  85.0 7.9 %collective-permute-start.24 = (bf16[16,3584]{1,0:T(8,128)(2,1)S(1)}, bf16[16,3584]{1,0:T(8,128)(2,1)S(1)}, u32[]{:S(2)}, u32[]{:S(2)}) collective-permute-start(bf16[16,3584]{1,0:T(8,128)(2,1)S(1)} %get-tuple-element.141), channel_id=1, source_target_pairs={{0,2},{1,3},{2,0},{3,1},{4,6},{5,7},{6,4},{7,5},{8,10},{9,11},{10,... | collective-permute-start | bytes 344072 | tf_op jit(solution)/shard_map/ppermute | solution.py:309
  87.1 7.5 %collective-permute-start.23 = (bf16[16,3584]{1,0:T(8,128)(2,1)S(1)}, bf16[16,3584]{1,0:T(8,128)(2,1)S(1)}, u32[]{:S(2)}, u32[]{:S(2)}) collective-permute-start(bf16[16,3584]{1,0:T(8,128)(2,1)S(1)} %get-tuple-element.142), channel_id=1, source_target_pairs={{0,8},{1,9},{2,10},{3,11},{4,12},{5,13},{6,14},{7,15},{8,0},{9,1},... | collective-permute-start | bytes 344072 | tf_op jit(solution)/shard_map/ppermute | solution.py:309
  87.5 11.3 %collective-permute-start.30 = (bf16[64,2304]{1,0:T(8,128)(2,1)S(1)}, bf16[64,2304]{1,0:T(8,128)(2,1)S(1)}, u32[]{:S(2)}, u32[]{:S(2)}) collective-permute-start(bf16[64,2304]{1,0:T(8,128)(2,1)S(1)} %add_convert_fusion.2), channel_id=1, source_target_pairs={{0,2},{1,3},{2,0},{3,1},{4,6},{5,7},{6,4},{7,5},{8,10},{9,11},{10,... | collective-permute-start | bytes 884744 | tf_op jit(solution)/shard_map/ppermute | solution.py:309
  94.8 6.1 %collective-permute-start.28 = (bf16[32,2304]{1,0:T(8,128)(2,1)S(1)}, bf16[32,2304]{1,0:T(8,128)(2,1)S(1)}, u32[]{:S(2)}, u32[]{:S(2)}) collective-permute-start(bf16[32,2304]{1,0:T(8,128)(2,1)S(1)} %add_convert_fusion.9), channel_id=1, source_target_pairs={{0,4},{1,5},{2,6},{3,7},{4,0},{5,1},{6,2},{7,3},{8,12},{9,13},{10,... | collective-permute-start | bytes 442376 | tf_op jit(solution)/shard_map/ppermute | solution.py:309
  (13 other events, 94.9 us)
